TPU v7x, 768 devices: a whole 4x8x12 slice. The times are simulated.
768 devices in a mesh: dp: 32 (over z_hi, y, core), tensor: 24 (over z_lo, x).
Axes of the slice: x: 4, y: 8, z: 12 (z_hi: 2, z_lo: 6; z = z_hi * 6 + z_lo), core: 2. Of those that a mesh axis runs over, the one named last changes fastest.
Arguments:
- attention: bfloat16 [6144, 6144], P('dp', 'tensor'), may hold values from -6 to 6
- out_proj: bfloat16 [6144, 8192], P('tensor'), may hold values from -0.078125 to 0.078125
- residual: bfloat16 [6144, 8192], P(('dp', 'tensor')), may hold values from -6 to 6
- gain: float32 [8192], replicated, may hold values from 0.1 to 1.9
- grad_normed: bfloat16 [6144, 8192], P(('dp', 'tensor')), may hold values from -6 to 6
- grad_residual: bfloat16 [6144, 8192], P(('dp', 'tensor')), may hold values from -6 to 6
Outputs:
- normed: bfloat16 [6144, 8192], P(('dp', 'tensor'))
- grad_mixed: bfloat16 [6144, 8192], P(('dp', 'tensor'))
- grad_attention: bfloat16 [6144, 6144], P('dp', 'tensor')
- grad_out_proj: float32 [6144, 8192], P('tensor', 'dp')
All inputs are finite; a program needn't handle non-finite values.
Results may differ from a plain program's by a relative error of at most 0.02.
Values may be sent and summed in bfloat16 or wider, within the bound.
No kernel may reach another device: no remote copies, remote signals or barrier semaphores. Data moves between devices by JAX's collectives and lax.ppermute only.
A program may use at most 32 MiB of HBM per device.

v0:
```python
import jax
import jax.numpy as jnp
from jax import lax
from jax.sharding import PartitionSpec as P


def per_device(attention, out_proj, residual, gain, grad_normed, grad_residual):
    partial_value = jnp.dot(attention, out_proj, preferred_element_type=jnp.float32)
    share = lax.psum_scatter(
        partial_value.astype(jnp.bfloat16), "tensor", scatter_dimension=0, tiled=True
    ).astype(jnp.float32)
    mixed = residual.astype(jnp.float32) + share
    rms = jnp.sqrt(jnp.mean(mixed * mixed, axis=-1, keepdims=True) + 1e-05)
    unit = mixed / rms
    normed = (unit * gain).astype(jnp.bfloat16)
    scaled = grad_normed.astype(jnp.float32) * gain
    inner = jnp.mean(scaled * unit, axis=-1, keepdims=True)
    grad_mixed = (grad_residual.astype(jnp.float32) + (scaled - unit * inner) / rms).astype(
        jnp.bfloat16
    )
    whole_grad = lax.all_gather(grad_mixed, "tensor", axis=0, tiled=True)
    grad_attention = lax.dot_general(
        whole_grad, out_proj, (((1,), (1,)), ((), ())), preferred_element_type=jnp.float32
    ).astype(jnp.bfloat16)
    term = lax.dot_general(
        attention, whole_grad, (((0,), (0,)), ((), ())), preferred_element_type=jnp.float32
    )
    grad_out_proj = lax.psum_scatter(
        term.astype(jnp.bfloat16), "dp", scatter_dimension=1, tiled=True
    ).astype(jnp.float32)
    return (normed, grad_mixed, grad_attention, grad_out_proj)


def solution(mesh):
    placed = (
        P("dp", "tensor"),
        P("tensor", None),
        P(("dp", "tensor"), None),
        P(),
        P(("dp", "tensor"), None),
        P(("dp", "tensor"), None),
    )
    return jax.shard_map(
        per_device,
        mesh=mesh,
        in_specs=placed,
        out_specs=(
            P(("dp", "tensor"), None),
            P(("dp", "tensor"), None),
            P("dp", "tensor"),
            P("tensor", "dp"),
        ),
        check_vma=False,
    )
```

profile of v0, /device:TPU:2, one launch (start us, length us, event | category | flops | bytes accessed | tf_op | source)
XLA Modules:
  0.0 530.5 jit_solution(17036324451204981044)
XLA Ops:
  7.2 0.0 copy-start
  7.2 0.0 copy-start.2
  7.2 0.0 copy-start.3
  7.2 0.0 copy-start.5
  7.2 0.0 copy-start.4
  7.2 0.0 reduce-scatter.3.cloned.1.call-start
  7.3 0.8 copy-done
  8.1 4.8 convolution_convert_fusion.1
  12.9 0.0 reduce-scatter.3.cloned.1.call-update
  12.9 0.0 all-gather.2.cloned.1.call-start
  13.0 168.5 %reduce-scatter.3.cloned.1.call-done = bf16[8,8192]{1,0:T(8,128)(2,1)} async-done(((bf16[192,8192]{1,0:T(8,128)(2,1)}), bf16[8,8192]{1,0:T(8,128)(2,1)}) %reduce-scatter.3.cloned.1.call-update) | async-done | bytes 131088 | tf_op jit(solution)/shard_map/reduce_scatter | solution.py:9
  181.4 0.0 copy-done.2
  181.4 1.1 multiply_reduce_fusion.1
  182.5 0.0 copy-done.3
  182.5 0.0 copy-done.5
  182.6 1.2 multiply_reduce_fusion
  183.7 0.0 copy-done.4
  183.7 1.7 add_convert_fusion
  185.5 0.0 all-gather.2.cloned.1.call-update
  185.5 0.0 reduce-scatter.5.cloned.1.call-start
  185.6 154.6 %all-gather.2.cloned.1.call-done = bf16[192,8192]{1,0:T(8,128)(2,1)} async-done(((bf16[8,8192]{1,0:T(8,128)(2,1)}), bf16[192,8192]{1,0:T(8,128)(2,1)}) %all-gather.2.cloned.1.call-update) | async-done | bytes 3145744 | tf_op jit(solution)/shard_map/all_gather | solution.py:21
  340.2 5.2 fusion
  345.3 0.0 copy-start.1
  345.3 0.0 reduce-scatter.5.cloned.1.call-update
  345.4 1.9 copy-done.1
  347.2 4.4 convolution_convert_fusion.2
  351.6 170.7 %reduce-scatter.5.cloned.1.call-done = bf16[256,256]{0,1:T(8,128)(2,1)} async-done(((bf16[256,8192]{0,1:T(8,128)(2,1)}), bf16[256,256]{0,1:T(8,128)(2,1)}) %reduce-scatter.5.cloned.1.call-update) | async-done | bytes 131088 | tf_op jit(solution)/shard_map/reduce_scatter | solution.py:28
  522.3 1.7 copy.10
  (2 shorter events, 0.0 us)
Async XLA Ops:
  7.2 0.9 copy-start
  7.2 174.3 %copy-start.2 = (bf16[8,8192]{1,0:T(8,128)(2,1)S(1)}, bf16[8,8192]{1,0:T(8,128)(2,1)}, u32[]{:S(2)}) copy-start(bf16[8,8192]{1,0:T(8,128)(2,1)} %param.8) | copy-start | bytes 393220
  7.2 175.3 %copy-start.3 = (bf16[8,8192]{1,0:T(8,128)(2,1)S(1)}, bf16[8,8192]{1,0:T(8,128)(2,1)}, u32[]{:S(2)}) copy-start(bf16[8,8192]{1,0:T(8,128)(2,1)} %param.10) | copy-start | bytes 393220
  7.2 175.3 %copy-start.5 = (f32[8192]{0:T(1024)S(1)}, f32[8192]{0:T(1024)}, u32[]{:S(2)}) copy-start(f32[8192]{0:T(1024)} %param.9) | copy-start | bytes 98308
  7.2 176.5 %copy-start.4 = (bf16[8,8192]{1,0:T(8,128)(2,1)S(1)}, bf16[8,8192]{1,0:T(8,128)(2,1)}, u32[]{:S(2)}) copy-start(bf16[8,8192]{1,0:T(8,128)(2,1)} %param.11) | copy-start | bytes 393220
  7.2 174.2 %reduce-scatter.3.cloned.1.call-start = ((), (), s32[]{:S(2)}) async-start(), calls=%async_computation.2 | async-start | bytes 3276800 | tf_op jit(solution)/shard_map/reduce_scatter | solution.py:9
  12.9 327.3 %all-gather.2.cloned.1.call-start = ((), (), s32[]{:S(2)}) async-start(), calls=%async_computation.3 | async-start | bytes 3276800 | tf_op jit(solution)/shard_map/all_gather | solution.py:21
  185.5 336.8 %reduce-scatter.5.cloned.1.call-start = ((), (), s32[]{:S(2)}) async-start(), calls=%async_computation.4 | async-start | bytes 4325376 | tf_op jit(solution)/shard_map/reduce_scatter | solution.py:28
  345.3 1.9 copy-start.1
Sparse Core Ops, SparseCore 0:
  13.0 168.3 reduce-scatter.2
  185.6 154.4 all-gather.1
  345.5 176.7 reduce-scatter.4
where the time goes:
time: 531 us
  waiting for transfers between devices  494 us (93%)
  matrix products  14.4 us (3%)
  between operations  13.8 us (3%)
    reduce_scatter x1, waiting for transfers between devices, per_device(): lax.psum_scatter(term.astype(jnp.bfloat16), 'dp', scatter_dimension=1, ti...  171 us
    reduce_scatter x1, waiting for transfers between devices, per_device(): lax.psum_scatter(partial_value.astype(jnp.bfloat16), 'tensor', scatter_di...  168 us
    all_gather x1, waiting for transfers between devices, per_device(): whole_grad = lax.all_gather(grad_mixed, 'tensor', axis=0, tiled=True)  155 us
  transfers between devices with their start and end apart: 3, of which 3 were waited for; matrix products, arithmetic and copies ran while one was open for 1% of the time, Pallas kernels for 0%

commit v1 on v0

v1 whole, which is shorter than its diff:
```python
import jax
import jax.numpy as jnp
from jax import lax
from jax.experimental import pallas as pl
from jax.experimental.pallas import tpu as pltpu
from jax.sharding import Mesh, PartitionSpec as P

ZH, Y, CORE, ZL, X = 2, 8, 2, 6, 4
BF, F32 = jnp.bfloat16, jnp.float32
D = 8192
CHUNKS = 2
VMEM = 48 * 1024 * 1024


def shift(value, axis, size, move):
    return lax.ppermute(value, axis, [(i, move(i)) for i in range(size)])


def to_x(value, r):
    return shift(value, "x", X, lambda i: (i - r) % X)


def to_q(value):
    return shift(value, "zl", ZL, lambda i: i ^ 1)


def to_p(value, r):
    return shift(value, "zl", ZL, lambda i: ((i // 2 - r) % 3) * 2 + i % 2)


def to_v(value):
    return shift(value, "y", Y, lambda i: i ^ 1)


def to_u(value, r):
    return shift(value, "y", Y, lambda i: ((i // 2 - r) % 4) * 2 + i % 2)


def to_core(value):
    return shift(value, "core", CORE, lambda i: i ^ 1)


def to_zh(value):
    return shift(value, "zh", ZH, lambda i: i ^ 1)


def norm_kernel(place, *refs):
    sums = refs[: 3 * CHUNKS]
    residual, gain, grad_normed, grad_residual, normed, grad_mixed, mine, other = refs[3 * CHUNKS :]
    share = jnp.concatenate(
        [
            sums[3 * c][...] + sums[3 * c + 1][...].astype(F32) + sums[3 * c + 2][...].astype(F32)
            for c in range(CHUNKS)
        ],
        axis=1,
    )
    mixed = residual[...].astype(F32) + share
    rms = jnp.sqrt(jnp.mean(mixed * mixed, axis=-1, keepdims=True) + 1e-05)
    unit = mixed / rms
    normed[...] = (unit * gain[...]).astype(BF)
    scaled = grad_normed[...].astype(F32) * gain[...]
    inner = jnp.mean(scaled * unit, axis=-1, keepdims=True)
    grad_mixed[...] = (grad_residual[...].astype(F32) + (scaled - unit * inner) / rms).astype(BF)
    core, zh = place[0], place[1]
    for k in range(2):
        half = (1 - zh) if k == 0 else zh
        for y in range(Y):
            at = (half * Y + y) * 2
            put = pl.ds(k * 2048 + y * 256, 256)
            mine[:, put] = grad_mixed[:, pl.ds(pl.multiple_of((at + core) * 256, 256), 256)]
            other[:, put] = grad_mixed[:, pl.ds(pl.multiple_of((at + 1 - core) * 256, 256), 256)]


def norm(place, sums, residual, gain, grad_normed, grad_residual):
    whole = pl.BlockSpec(memory_space=pltpu.VMEM)
    count = len(sums) + 4
    return pl.pallas_call(
        norm_kernel,
        out_shape=(
            jax.ShapeDtypeStruct((8, D), BF),
            jax.ShapeDtypeStruct((8, D), BF),
            jax.ShapeDtypeStruct((8, D // 2), BF),
            jax.ShapeDtypeStruct((8, D // 2), BF),
        ),
        in_specs=[pl.BlockSpec(memory_space=pltpu.SMEM)] + [whole] * count,
        out_specs=(whole,) * 4,
        compiler_params=pltpu.CompilerParams(vmem_limit_bytes=16 * 1024 * 1024),
        cost_estimate=pl.CostEstimate(flops=8 * D * 20, bytes_accessed=8 * D * 20, transcendentals=0),
        name="norm",
    )(place, *sums, residual, gain, grad_normed, grad_residual)


def term_kernel(blocks, turned, *refs):
    pieces, send, keep = refs[:X], refs[X], refs[X + 1]
    for r in range(Y):
        at = pl.ds(pl.multiple_of(blocks[r] * 256, 256), 256)
        total = jnp.zeros((256, 256), F32)
        for x in range(X):
            total += jnp.dot(
                turned[:, x * 96 : (x + 1) * 96], pieces[x][:, at], preferred_element_type=F32
            )
        out = keep if r < 4 else send
        out[(r % 4) * 256 : (r % 4 + 1) * 256, :] = total.astype(BF)


def term_parts(blocks, turned, pieces):
    whole = pl.BlockSpec(memory_space=pltpu.VMEM)
    return pl.pallas_call(
        term_kernel,
        out_shape=(jax.ShapeDtypeStruct((1024, 256), BF),) * 2,
        in_specs=[pl.BlockSpec(memory_space=pltpu.SMEM)] + [whole] * 5,
        out_specs=(whole,) * 2,
        compiler_params=pltpu.CompilerParams(vmem_limit_bytes=VMEM),
        cost_estimate=pl.CostEstimate(
            flops=2 * 256 * 384 * 2048, bytes_accessed=3 * 1024 * 1024, transcendentals=0
        ),
        name="term",
    )(blocks, turned, *pieces)


def back_kernel(at, *refs):
    pieces, weight, out = refs[:X], refs[X], refs[X + 1]

    @pl.when(pl.program_id(0) == 0)
    def _():
        out[...] = jnp.zeros_like(out)

    for x in range(X):
        out[x * 96 : (x + 1) * 96, :] += lax.dot_general(
            pieces[x][...], weight[...], (((1,), (1,)), ((), ())), preferred_element_type=F32
        )


def back(first, pieces, weight):
    return pl.pallas_call(
        back_kernel,
        out_shape=jax.ShapeDtypeStruct((384, 256), F32),
        grid_spec=pltpu.PrefetchScalarGridSpec(
            num_scalar_prefetch=1,
            grid=(Y,),
            in_specs=[pl.BlockSpec((96, 256), lambda y, at: (0, y))] * X
            + [pl.BlockSpec((256, 256), lambda y, at: (0, at[0] + 2 * y))],
            out_specs=pl.BlockSpec((384, 256), lambda y, at: (0, 0)),
        ),
        compiler_params=pltpu.CompilerParams(vmem_limit_bytes=16 * 1024 * 1024),
        cost_estimate=pl.CostEstimate(
            flops=2 * 256 * 384 * 2048, bytes_accessed=3 * 1024 * 1024, transcendentals=0
        ),
        name="back",
    )(first, *pieces, weight)


def per_device(attention, out_proj, residual, gain, grad_normed, grad_residual):
    x, zl, y = lax.axis_index("x"), lax.axis_index("zl"), lax.axis_index("y")
    core, zh = lax.axis_index("core"), lax.axis_index("zh")

    r = jnp.arange(24, dtype=jnp.int32)
    owner_x = (x - r // 6 + X) % X
    owner_q = (zl % 2) ^ ((r // 3) % 2)
    owner_p = (zl // 2 - r % 3 + 3) % 3
    owner = (owner_p * 2 + owner_q) * X + owner_x
    token = jnp.repeat(owner * 8, 8) + jnp.tile(jnp.arange(8, dtype=jnp.int32), 24)
    order = (token[:, None] == jnp.arange(192, dtype=jnp.int32)[None, :]).astype(BF)
    near = jnp.dot(order, attention, preferred_element_type=F32).astype(BF)

    width = D // CHUNKS
    sums = []
    for c in range(CHUNKS):
        weight = out_proj[:, c * width : (c + 1) * width]

        def product(r):
            return jnp.dot(near[r * 48 : (r + 1) * 48], weight, preferred_element_type=F32)

        got = [to_x(product(r).astype(BF), r) for r in (2, 1, 3)]
        summed = product(0) + got[0].astype(F32) + got[1].astype(F32) + got[2].astype(F32)
        pair = to_q(summed[24:].astype(BF))
        summed = summed[:24] + pair.astype(F32)
        sums += [summed[:8]] + [to_p(summed[r * 8 : (r + 1) * 8].astype(BF), r) for r in (1, 2)]

    far = to_core(near)
    both = jnp.stack([near.reshape(24, 8, 256), far.reshape(24, 8, 256)], axis=1).reshape(384, 256)
    turned = both.T

    place = jnp.stack([core, zh]).astype(jnp.int32)
    normed, grad_mixed, mine, other = norm(
        place, sums, residual, gain.reshape(1, D), grad_normed, grad_residual
    )
    other = to_core(other)
    s = jnp.arange(Y, dtype=jnp.int32)
    blocks = ((y // 2 - s % 4 + 4) % 4) * 2 + ((y % 2) ^ (s // 4))

    grads, terms = 0.0, []
    for k in range(2):
        half = (1 - zh) if k == 0 else zh
        at = slice(k * 2048, (k + 1) * 2048)
        own = jnp.concatenate([mine[:, at], other[:, at]], axis=0)
        line = jnp.concatenate([own, to_p(own, -1), to_p(own, -2)], axis=0)
        line = jnp.concatenate([line, to_q(line)], axis=0)
        pieces = [line] + [to_x(line, -r) for r in (1, 2, 3)]
        send, keep = term_parts(blocks, turned, pieces)
        kept = keep.astype(F32) + to_v(send).astype(F32)
        total = kept[:256]
        for r in (1, 2, 3):
            total = total + to_u(kept[r * 256 : (r + 1) * 256].astype(BF), r).astype(F32)
        terms.append(total)
        first = (half * 16 + core).reshape(1).astype(jnp.int32)
        grads = grads + back(first, pieces, out_proj)
    grad_out_proj = terms[1] + to_zh(terms[0].astype(BF)).astype(F32)

    grads = grads.reshape(24, 2, 8, 256)
    ours = grads[:, 0].reshape(192, 256) + to_core(grads[:, 1].reshape(192, 256))
    grad_attention = lax.dot_general(
        order, ours.astype(BF), (((0,), (0,)), ((), ())), preferred_element_type=F32
    ).astype(BF)
    return (normed, grad_mixed, grad_attention, grad_out_proj)


def solution(mesh):
    dp, tensor = ("zh", "y", "core"), ("zl", "x")
    fine = Mesh(mesh.devices.reshape(ZH, Y, CORE, ZL, X), dp + tensor)
    rows = P(dp + tensor, None)
    return jax.shard_map(
        per_device,
        mesh=fine,
        in_specs=(P(dp, tensor), P(tensor, None), rows, P(), rows, rows),
        out_specs=(rows, rows, P(dp, tensor), P(tensor, dp)),
        check_vma=False,
    )
```

time: 531 us -> 221 us (0.42)
  the two profiles are of different devices: /device:TPU:2 before, /device:TPU:14 now
where the time goes in v1:
time: 221 us; the launch traced here: 220 us
  starting transfers between devices  145 us (66%)
  waiting for transfers between devices  41.9 us (19%)
  Pallas kernels  12 us (5%)
  matrix products  11.2 us (5%)
  local copies, waits for them, and re-layouts  5.1 us (2%)
  other arithmetic  3.25 us (1%)
    ppermute x36, starting transfers between devices, shift(): return lax.ppermute(value, axis, [(i, move(i)) for i in range(size)])  145 us
    ppermute x36, waiting for transfers between devices, shift(): return lax.ppermute(value, axis, [(i, move(i)) for i in range(size)])  41.9 us
    dot_general x8, matrix products, product(): jnp.dot(near[r * 48:(r + 1) * 48], weight, preferred_element_type=F32)  10 us
    pallas_call x2, Pallas kernels, back(): pl.pallas_call(back_kernel, out_shape=jax.ShapeDtypeStruct((384, 256), F3...  5.91 us
    pallas_call x2, Pallas kernels, term_parts(): pl.pallas_call(term_kernel, out_shape=(jax.ShapeDtypeStruct((1024, 256),...  4.48 us
  transfers between devices with their start and end apart: 36, of which 10 were waited for; matrix products, arithmetic and copies ran while one was open for 6% of the time, Pallas kernels for 5%

profile of v1, /device:TPU:14, one launch (start us, length us, event | category | flops | bytes accessed | tf_op | source)
XLA Modules:
  0.0 219.6 jit_solution(9482253828064522562)
XLA Ops:
  8.5 3.5 %collective-permute-start.1 = (bf16[48,4096]{1,0:T(8,128)(2,1)S(1)}, bf16[48,4096]{1,0:T(8,128)(2,1)}, u32[]{:S(2)}, u32[]{:S(2)}) collective-permute-start(bf16[48,4096]{1,0:T(8,128)(2,1)S(1)} %convolution_convert_fusion.4), channel_id=1, source_target_pairs={{0,3},{1,0},{2,1},{3,2},{4,7},{5,4},{6,5},{7,6},{8,11},{9,8},{10,9... | collective-permute-start | bytes 1179656 | tf_op jit(solution)/shard_map/ppermute | solution.py:16
  12.4 3.3 %collective-permute-start = (bf16[48,4096]{1,0:T(8,128)(2,1)S(1)}, bf16[48,4096]{1,0:T(8,128)(2,1)}, u32[]{:S(2)}, u32[]{:S(2)}) collective-permute-start(bf16[48,4096]{1,0:T(8,128)(2,1)S(1)} %convolution_convert_fusion.5), channel_id=1, source_target_pairs={{0,2},{1,3},{2,0},{3,1},{4,6},{5,7},{6,4},{7,5},{8,10},{9,11},{10,... | collective-permute-start | bytes 1179656 | tf_op jit(solution)/shard_map/ppermute | solution.py:16
  16.2 4.0 %collective-permute-start.8 = (bf16[48,4096]{1,0:T(8,128)(2,1)S(1)}, bf16[48,4096]{1,0:T(8,128)(2,1)S(1)}, u32[]{:S(2)}, u32[]{:S(2)}) collective-permute-start(bf16[48,4096]{1,0:T(8,128)(2,1)S(1)} %convolution_convert_fusion), channel_id=1, source_target_pairs={{0,1},{1,2},{2,3},{3,0},{4,5},{5,6},{6,7},{7,4},{8,9},{9,10},{10,1... | collective-permute-start | bytes 1179656 | tf_op jit(solution)/shard_map/ppermute | solution.py:16
  23.1 3.9 %collective-permute-start.6 = (bf16[48,4096]{1,0:T(8,128)(2,1)S(1)}, bf16[48,4096]{1,0:T(8,128)(2,1)}, u32[]{:S(2)}, u32[]{:S(2)}) collective-permute-start(bf16[48,4096]{1,0:T(8,128)(2,1)S(1)} %convolution_convert_fusion.2), channel_id=1, source_target_pairs={{0,2},{1,3},{2,0},{3,1},{4,6},{5,7},{6,4},{7,5},{8,10},{9,11},{10,... | collective-permute-start | bytes 1179656 | tf_op jit(solution)/shard_map/ppermute | solution.py:16
  34.3 4.4 %collective-permute-start.3 = (bf16[24,4096]{1,0:T(8,128)(2,1)S(1)}, bf16[24,4096]{1,0:T(8,128)(2,1)S(1)}, u32[]{:S(2)}, u32[]{:S(2)}) collective-permute-start(bf16[24,4096]{1,0:T(8,128)(2,1)S(1)} %slice.232), channel_id=1, source_target_pairs={{0,4},{4,0},{8,12},{12,8},{16,20},{20,16},{1,5},{5,1},{9,13},{13,9... | collective-permute-start | bytes 589832 | tf_op jit(solution)/shard_map/ppermute | solution.py:16
  38.7 8.7 %collective-permute-done.7 = bf16[48,4096]{1,0:T(8,128)(2,1)S(1)} collective-permute-done((bf16[48,4096]{1,0:T(8,128)(2,1)S(1)}, bf16[48,4096]{1,0:T(8,128)(2,1)S(1)}, u32[]{:S(2)}, u32[]{:S(2)}) %collective-permute-start.7) | collective-permute-done | bytes 393248 | tf_op jit(solution)/shard_map/ppermute | solution.py:16
  49.0 4.3 %collective-permute-start.9 = (bf16[24,4096]{1,0:T(8,128)(2,1)S(1)}, bf16[24,4096]{1,0:T(8,128)(2,1)S(1)}, u32[]{:S(2)}, u32[]{:S(2)}) collective-permute-start(bf16[24,4096]{1,0:T(8,128)(2,1)S(1)} %slice.231), channel_id=1, source_target_pairs={{0,4},{4,0},{8,12},{12,8},{16,20},{20,16},{1,5},{5,1},{9,13},{13,9... | collective-permute-start | bytes 589832 | tf_op jit(solution)/shard_map/ppermute | solution.py:16
  53.4 10.9 %collective-permute-start.4 = (bf16[8,4096]{1,0:T(8,128)(2,1)S(1)}, bf16[8,4096]{1,0:T(8,128)(2,1)S(1)}, u32[]{:S(2)}, u32[]{:S(2)}) collective-permute-start(bf16[8,4096]{1,0:T(8,128)(2,1)S(1)} %get-tuple-element.37), channel_id=1, source_target_pairs={{0,16},{4,20},{8,0},{12,4},{16,8},{20,12},{1,17},{5,21},{9,1},{13,... | collective-permute-start | bytes 196616 | tf_op jit(solution)/shard_map/ppermute | solution.py:16
  66.3 7.8 %collective-permute-start.10 = (bf16[8,4096]{1,0:T(8,128)(2,1)S(1)}, bf16[8,4096]{1,0:T(8,128)(2,1)S(1)}, u32[]{:S(2)}, u32[]{:S(2)}) collective-permute-start(bf16[8,4096]{1,0:T(8,128)(2,1)S(1)} %get-tuple-element.35), channel_id=1, source_target_pairs={{0,16},{4,20},{8,0},{12,4},{16,8},{20,12},{1,17},{5,21},{9,1},{13,... | collective-permute-start | bytes 196616 | tf_op jit(solution)/shard_map/ppermute | solution.py:16
  76.7 7.7 %collective-permute-done.11.refs_5_ = bf16[8,4096]{1,0:T(8,128)(2,1)S(1)} collective-permute-done((bf16[8,4096]{1,0:T(8,128)(2,1)S(1)}, bf16[8,4096]{1,0:T(8,128)(2,1)S(1)}, u32[]{:S(2)}, u32[]{:S(2)}) %collective-permute-start.11) | collective-permute-done | bytes 65568 | tf_op jit(solution)/shard_map/ppermute | solution.py:16
  91.1 7.8 %collective-permute-start.14 = (bf16[16,2048]{1,0:T(8,128)(2,1)S(1)}, bf16[16,2048]{1,0:T(8,128)(2,1)S(1)}, u32[]{:S(2)}, u32[]{:S(2)}) collective-permute-start(bf16[16,2048]{1,0:T(8,128)(2,1)S(1)} %pad_maximum_fusion.3), channel_id=1, source_target_pairs={{0,16},{4,20},{8,0},{12,4},{16,8},{20,12},{1,17},{5,21},{9,1},{13,... | collective-permute-start | bytes 196616 | tf_op jit(solution)/shard_map/ppermute | solution.py:16
  100.9 7.8 %collective-permute-start.20 = (bf16[16,2048]{1,0:T(8,128)(2,1)S(1)}, bf16[16,2048]{1,0:T(8,128)(2,1)S(1)}, u32[]{:S(2)}, u32[]{:S(2)}) collective-permute-start(bf16[16,2048]{1,0:T(8,128)(2,1)S(1)} %pad_maximum_fusion.4), channel_id=1, source_target_pairs={{0,16},{4,20},{8,0},{12,4},{16,8},{20,12},{1,17},{5,21},{9,1},{13,... | collective-permute-start | bytes 196616 | tf_op jit(solution)/shard_map/ppermute | solution.py:16
  111.2 3.4 %collective-permute-start.21 = (bf16[48,2048]{1,0:T(8,128)(2,1)S(1)}, bf16[48,2048]{1,0:T(8,128)(2,1)S(1)}, u32[]{:S(2)}, u32[]{:S(2)}) collective-permute-start(bf16[48,2048]{1,0:T(8,128)(2,1)S(1)} %pad_maximum_fusion.1), channel_id=1, source_target_pairs={{0,4},{4,0},{8,12},{12,8},{16,20},{20,16},{1,5},{5,1},{9,13},{13,9... | collective-permute-start | bytes 589832 | tf_op jit(solution)/shard_map/ppermute | solution.py:16
  114.7 3.8 %collective-permute-done.15 = bf16[48,2048]{1,0:T(8,128)(2,1)S(1)} collective-permute-done((bf16[48,2048]{1,0:T(8,128)(2,1)S(1)}, bf16[48,2048]{1,0:T(8,128)(2,1)S(1)}, u32[]{:S(2)}, u32[]{:S(2)}) %collective-permute-start.15) | collective-permute-done | bytes 196640 | tf_op jit(solution)/shard_map/ppermute | solution.py:16
  120.4 3.9 %collective-permute-start.17 = (bf16[96,2048]{1,0:T(8,128)(2,1)S(1)}, bf16[96,2048]{1,0:T(8,128)(2,1)S(1)}, u32[]{:S(2)}, u32[]{:S(2)}) collective-permute-start(bf16[96,2048]{1,0:T(8,128)(2,1)S(1)} %constant_dynamic-update-slice_fusion.refs_0_), channel_id=1, source_target_pairs={{0,2},{1,3},{2,0},{3,1},{4,6},{5,7},{6,4},{7,5},{8,10},{9,11},{10,... | collective-permute-start | bytes 1179656 | tf_op jit(solution)/shard_map/ppermute | solution.py:16
  124.3 3.3 %collective-permute-start.18 = (bf16[96,2048]{1,0:T(8,128)(2,1)S(1)}, bf16[96,2048]{1,0:T(8,128)(2,1)S(1)}, u32[]{:S(2)}, u32[]{:S(2)}) collective-permute-start(bf16[96,2048]{1,0:T(8,128)(2,1)S(1)} %constant_dynamic-update-slice_fusion.refs_0_), channel_id=1, source_target_pairs={{0,3},{1,0},{2,1},{3,2},{4,7},{5,4},{6,5},{7,6},{8,11},{9,8},{10,9... | collective-permute-start | bytes 1179656 | tf_op jit(solution)/shard_map/ppermute | solution.py:16
  127.7 3.7 %collective-permute-start.22 = (bf16[96,2048]{1,0:T(8,128)(2,1)S(1)}, bf16[96,2048]{1,0:T(8,128)(2,1)S(1)}, u32[]{:S(2)}, u32[]{:S(2)}) collective-permute-start(bf16[96,2048]{1,0:T(8,128)(2,1)S(1)} %constant_dynamic-update-slice_fusion.5.refs_0_), channel_id=1, source_target_pairs={{0,1},{1,2},{2,3},{3,0},{4,5},{5,6},{6,7},{7,4},{8,9},{9,10},{10,1... | collective-permute-start | bytes 1179656 | tf_op jit(solution)/shard_map/ppermute | solution.py:16
  131.5 2.9 %collective-permute-start.23 = (bf16[96,2048]{1,0:T(8,128)(2,1)S(1)}, bf16[96,2048]{1,0:T(8,128)(2,1)S(1)}, u32[]{:S(2)}, u32[]{:S(2)}) collective-permute-start(bf16[96,2048]{1,0:T(8,128)(2,1)S(1)} %constant_dynamic-update-slice_fusion.5.refs_0_), channel_id=1, source_target_pairs={{0,2},{1,3},{2,0},{3,1},{4,6},{5,7},{6,4},{7,5},{8,10},{9,11},{10,... | collective-permute-start | bytes 1179656 | tf_op jit(solution)/shard_map/ppermute | solution.py:16
  134.3 3.3 %collective-permute-start.24 = (bf16[96,2048]{1,0:T(8,128)(2,1)S(1)}, bf16[96,2048]{1,0:T(8,128)(2,1)S(1)}, u32[]{:S(2)}, u32[]{:S(2)}) collective-permute-start(bf16[96,2048]{1,0:T(8,128)(2,1)S(1)} %constant_dynamic-update-slice_fusion.5.refs_0_), channel_id=1, source_target_pairs={{0,3},{1,0},{2,1},{3,2},{4,7},{5,4},{6,5},{7,6},{8,11},{9,8},{10,9... | collective-permute-start | bytes 1179656 | tf_op jit(solution)/shard_map/ppermute | solution.py:16
  139.5 8.5 %collective-permute-done.18.refs_3_ = bf16[96,2048]{1,0:T(8,128)(2,1)S(1)} collective-permute-done((bf16[96,2048]{1,0:T(8,128)(2,1)S(1)}, bf16[96,2048]{1,0:T(8,128)(2,1)S(1)}, u32[]{:S(2)}, u32[]{:S(2)}) %collective-permute-start.18) | collective-permute-done | bytes 393248 | tf_op jit(solution)/shard_map/ppermute | solution.py:16
  148.0 2.6 %term.3 = (bf16[1024,256]{1,0:T(8,128)(2,1)}, bf16[1024,256]{1,0:T(8,128)(2,1)S(1)}) custom-call(s32[8]{0:T(128)S(1)} %fusion.49.blocks, bf16[256,384]{1,0:T(8,128)(2,1)S(1)} %bitcast.24, bf16[96,2048]{1,0:T(8,128)(2,1)S(1)} %constant_dynamic-update-slice_fusion.refs_0_, bf16[96,2048]{1,0:T(8,128)(2,1)S(1)} %collective-permute-done.16.refs_1_, ...), custom_call_target="tpu_custom_call" | custom-call | flops 402653184 | bytes 3145728 | tf_op jit(solution)/shard_map/term/pallas_call | solution.py:108
  156.0 2.9 %back.2 = f32[384,256]{1,0:T(8,128)S(1)} custom-call(s32[1]{0:T(128)} %bitcast.3.at, bf16[96,2048]{1,0:T(8,128)(2,1)S(1)} %constant_dynamic-update-slice_fusion.refs_0_, bf16[96,2048]{1,0:T(8,128)(2,1)S(1)} %collective-permute-done.16.refs_1_, bf16[96,2048]{1,0:T(8,128)(2,1)S(1)} %collective-permute-done.17.refs_2_, ...), custom_call_target="tpu_custom_call" | custom-call | flops 402653184 | bytes 3145728 | tf_op jit(solution)/shard_map/back/pallas_call | solution.py:135
  159.0 3.0 %back.3 = f32[384,256]{1,0:T(8,128)S(1)} custom-call(s32[1]{0:T(128)} %bitcast.4.at, bf16[96,2048]{1,0:T(8,128)(2,1)S(1)} %constant_dynamic-update-slice_fusion.5.refs_0_, bf16[96,2048]{1,0:T(8,128)(2,1)S(1)} %collective-permute-done.22.refs_1_, bf16[96,2048]{1,0:T(8,128)(2,1)S(1)} %collective-permute-done.23.refs_2_, ...), custom_call_target="tpu_custom_call" | custom-call | flops 402653184 | bytes 3145728 | tf_op jit(solution)/shard_map/back/pallas_call | solution.py:135
  165.8 3.5 %collective-permute-start.27 = (bf16[1024,256]{1,0:T(8,128)(2,1)S(1)}, bf16[1024,256]{1,0:T(8,128)(2,1)S(1)}, u32[]{:S(2)}, u32[]{:S(2)}) collective-permute-start(bf16[1024,256]{1,0:T(8,128)(2,1)S(1)} %get-tuple-element.17), channel_id=1, source_target_pairs={{0,48},{48,0},{96,144},{144,96},{192,240},{240,192},{288,336},{336... | collective-permute-start | bytes 1572872 | tf_op jit(solution)/shard_map/ppermute | solution.py:16
  170.5 4.5 %collective-permute-start.34 = (bf16[256,256]{1,0:T(8,128)(2,1)S(1)}, bf16[256,256]{1,0:T(8,128)(2,1)S(1)}, u32[]{:S(2)}, u32[]{:S(2)}) collective-permute-start(bf16[256,256]{1,0:T(8,128)(2,1)S(1)} %get-tuple-element.32), channel_id=1, source_target_pairs={{0,96},{48,144},{96,192},{144,240},{192,288},{240,336},{288,0},{33... | collective-permute-start | bytes 393224 | tf_op jit(solution)/shard_map/ppermute | solution.py:16
  175.0 5.0 %collective-permute-start.33 = (bf16[256,256]{1,0:T(8,128)(2,1)S(1)}, bf16[256,256]{1,0:T(8,128)(2,1)S(1)}, u32[]{:S(2)}, u32[]{:S(2)}) collective-permute-start(bf16[256,256]{1,0:T(8,128)(2,1)S(1)} %get-tuple-element.33), channel_id=1, source_target_pairs={{0,192},{48,240},{96,288},{144,336},{192,0},{240,48},{288,96},{336... | collective-permute-start | bytes 393224 | tf_op jit(solution)/shard_map/ppermute | solution.py:16
  180.1 5.3 %collective-permute-start.32 = (bf16[256,256]{1,0:T(8,128)(2,1)S(1)}, bf16[256,256]{1,0:T(8,128)(2,1)S(1)}, u32[]{:S(2)}, u32[]{:S(2)}) collective-permute-start(bf16[256,256]{1,0:T(8,128)(2,1)S(1)} %get-tuple-element.31), channel_id=1, source_target_pairs={{0,288},{48,336},{96,0},{144,48},{192,96},{240,144},{288,192},{336... | collective-permute-start | bytes 393224 | tf_op jit(solution)/shard_map/ppermute | solution.py:16
  185.6 4.4 %collective-permute-start.30 = (bf16[256,256]{1,0:T(8,128)(2,1)S(1)}, bf16[256,256]{1,0:T(8,128)(2,1)S(1)}, u32[]{:S(2)}, u32[]{:S(2)}) collective-permute-start(bf16[256,256]{1,0:T(8,128)(2,1)S(1)} %get-tuple-element.29), channel_id=1, source_target_pairs={{0,96},{48,144},{96,192},{144,240},{192,288},{240,336},{288,0},{33... | collective-permute-start | bytes 393224 | tf_op jit(solution)/shard_map/ppermute | solution.py:16
  189.9 5.9 %collective-permute-start.29 = (bf16[256,256]{1,0:T(8,128)(2,1)S(1)}, bf16[256,256]{1,0:T(8,128)(2,1)S(1)}, u32[]{:S(2)}, u32[]{:S(2)}) collective-permute-start(bf16[256,256]{1,0:T(8,128)(2,1)S(1)} %get-tuple-element.30), channel_id=1, source_target_pairs={{0,192},{48,240},{96,288},{144,336},{192,0},{240,48},{288,96},{336... | collective-permute-start | bytes 393224 | tf_op jit(solution)/shard_map/ppermute | solution.py:16
  195.9 5.2 %collective-permute-start.28 = (bf16[256,256]{1,0:T(8,128)(2,1)S(1)}, bf16[256,256]{1,0:T(8,128)(2,1)S(1)}, u32[]{:S(2)}, u32[]{:S(2)}) collective-permute-start(bf16[256,256]{1,0:T(8,128)(2,1)S(1)} %get-tuple-element.28), channel_id=1, source_target_pairs={{0,288},{48,336},{96,0},{144,48},{192,96},{240,144},{288,192},{336... | collective-permute-start | bytes 393224 | tf_op jit(solution)/shard_map/ppermute | solution.py:16
  201.2 8.6 %collective-permute-start.35 = (bf16[256,256]{1,0:T(8,128)(2,1)S(1)}, bf16[256,256]{1,0:T(8,128)(2,1)S(1)}, u32[]{:S(2)}, u32[]{:S(2)}) collective-permute-start(bf16[256,256]{1,0:T(8,128)(2,1)S(1)} %fusion.12), channel_id=1, source_target_pairs={{0,384},{384,0},{1,385},{385,1},{2,386},{386,2},{3,387},{387,3},{4... | collective-permute-start | bytes 393224 | tf_op jit(solution)/shard_map/ppermute | solution.py:16
  210.8 8.1 %collective-permute-done.35 = bf16[256,256]{1,0:T(8,128)(2,1)S(1)} collective-permute-done((bf16[256,256]{1,0:T(8,128)(2,1)S(1)}, bf16[256,256]{1,0:T(8,128)(2,1)S(1)}, u32[]{:S(2)}, u32[]{:S(2)}) %collective-permute-start.35) | collective-permute-done | bytes 131104 | tf_op jit(solution)/shard_map/ppermute | solution.py:16
  (110 shorter events, 52.0 us)
Async XLA Ops:
  4.0 19.2 %collective-permute-start.2 = (bf16[48,4096]{1,0:T(8,128)(2,1)S(1)}, bf16[48,4096]{1,0:T(8,128)(2,1)S(1)}, u32[]{:S(2)}, u32[]{:S(2)}) collective-permute-start(bf16[48,4096]{1,0:T(8,128)(2,1)S(1)} %convolution_convert_fusion.3), channel_id=1, source_target_pairs={{0,1},{1,2},{2,3},{3,0},{4,5},{5,6},{6,7},{7,4},{8,9},{9,10},{10,1... | collective-permute-start | bytes 1179656 | tf_op jit(solution)/shard_map/ppermute | solution.py:16
  8.5 21.2 %collective-permute-start.1 = (bf16[48,4096]{1,0:T(8,128)(2,1)S(1)}, bf16[48,4096]{1,0:T(8,128)(2,1)}, u32[]{:S(2)}, u32[]{:S(2)}) collective-permute-start(bf16[48,4096]{1,0:T(8,128)(2,1)S(1)} %convolution_convert_fusion.4), channel_id=1, source_target_pairs={{0,3},{1,0},{2,1},{3,2},{4,7},{5,4},{6,5},{7,6},{8,11},{9,8},{10,9... | collective-permute-start | bytes 1179656 | tf_op jit(solution)/shard_map/ppermute | solution.py:16
  12.4 19.5 %collective-permute-start = (bf16[48,4096]{1,0:T(8,128)(2,1)S(1)}, bf16[48,4096]{1,0:T(8,128)(2,1)}, u32[]{:S(2)}, u32[]{:S(2)}) collective-permute-start(bf16[48,4096]{1,0:T(8,128)(2,1)S(1)} %convolution_convert_fusion.5), channel_id=1, source_target_pairs={{0,2},{1,3},{2,0},{3,1},{4,6},{5,7},{6,4},{7,5},{8,10},{9,11},{10,... | collective-permute-start | bytes 1179656 | tf_op jit(solution)/shard_map/ppermute | solution.py:16
  16.2 22.5 %collective-permute-start.8 = (bf16[48,4096]{1,0:T(8,128)(2,1)S(1)}, bf16[48,4096]{1,0:T(8,128)(2,1)S(1)}, u32[]{:S(2)}, u32[]{:S(2)}) collective-permute-start(bf16[48,4096]{1,0:T(8,128)(2,1)S(1)} %convolution_convert_fusion), channel_id=1, source_target_pairs={{0,1},{1,2},{2,3},{3,0},{4,5},{5,6},{6,7},{7,4},{8,9},{9,10},{10,1... | collective-permute-start | bytes 1179656 | tf_op jit(solution)/shard_map/ppermute | solution.py:16
  20.7 26.7 %collective-permute-start.7 = (bf16[48,4096]{1,0:T(8,128)(2,1)S(1)}, bf16[48,4096]{1,0:T(8,128)(2,1)S(1)}, u32[]{:S(2)}, u32[]{:S(2)}) collective-permute-start(bf16[48,4096]{1,0:T(8,128)(2,1)S(1)} %convolution_convert_fusion.1), channel_id=1, source_target_pairs={{0,3},{1,0},{2,1},{3,2},{4,7},{5,4},{6,5},{7,6},{8,11},{9,8},{10,9... | collective-permute-start | bytes 1179656 | tf_op jit(solution)/shard_map/ppermute | solution.py:16
  23.1 24.3 %collective-permute-start.6 = (bf16[48,4096]{1,0:T(8,128)(2,1)S(1)}, bf16[48,4096]{1,0:T(8,128)(2,1)}, u32[]{:S(2)}, u32[]{:S(2)}) collective-permute-start(bf16[48,4096]{1,0:T(8,128)(2,1)S(1)} %convolution_convert_fusion.2), channel_id=1, source_target_pairs={{0,2},{1,3},{2,0},{3,1},{4,6},{5,7},{6,4},{7,5},{8,10},{9,11},{10,... | collective-permute-start | bytes 1179656 | tf_op jit(solution)/shard_map/ppermute | solution.py:16
  29.7 101.8 %collective-permute-start.26 = (bf16[192,256]{1,0:T(8,128)(2,1)S(1)}, bf16[192,256]{1,0:T(8,128)(2,1)S(1)}, u32[]{:S(2)}, u32[]{:S(2)}) collective-permute-start(bf16[192,256]{1,0:T(8,128)(2,1)S(1)} %convolution_convert_fusion.7), channel_id=1, source_target_pairs={{0,24},{24,0},{1,25},{25,1},{2,26},{26,2},{3,27},{27,3},{4,28},{28... | collective-permute-start | bytes 294920 | tf_op jit(solution)/shard_map/ppermute | solution.py:16
  34.3 19.0 %collective-permute-start.3 = (bf16[24,4096]{1,0:T(8,128)(2,1)S(1)}, bf16[24,4096]{1,0:T(8,128)(2,1)S(1)}, u32[]{:S(2)}, u32[]{:S(2)}) collective-permute-start(bf16[24,4096]{1,0:T(8,128)(2,1)S(1)} %slice.232), channel_id=1, source_target_pairs={{0,4},{4,0},{8,12},{12,8},{16,20},{20,16},{1,5},{5,1},{9,13},{13,9... | collective-permute-start | bytes 589832 | tf_op jit(solution)/shard_map/ppermute | solution.py:16
  49.0 17.2 %collective-permute-start.9 = (bf16[24,4096]{1,0:T(8,128)(2,1)S(1)}, bf16[24,4096]{1,0:T(8,128)(2,1)S(1)}, u32[]{:S(2)}, u32[]{:S(2)}) collective-permute-start(bf16[24,4096]{1,0:T(8,128)(2,1)S(1)} %slice.231), channel_id=1, source_target_pairs={{0,4},{4,0},{8,12},{12,8},{16,20},{20,16},{1,5},{5,1},{9,13},{13,9... | collective-permute-start | bytes 589832 | tf_op jit(solution)/shard_map/ppermute | solution.py:16
  53.4 22.8 %collective-permute-start.4 = (bf16[8,4096]{1,0:T(8,128)(2,1)S(1)}, bf16[8,4096]{1,0:T(8,128)(2,1)S(1)}, u32[]{:S(2)}, u32[]{:S(2)}) collective-permute-start(bf16[8,4096]{1,0:T(8,128)(2,1)S(1)} %get-tuple-element.37), channel_id=1, source_target_pairs={{0,16},{4,20},{8,0},{12,4},{16,8},{20,12},{1,17},{5,21},{9,1},{13,... | collective-permute-start | bytes 196616 | tf_op jit(solution)/shard_map/ppermute | solution.py:16
  64.3 12.4 %collective-permute-start.5 = (bf16[8,4096]{1,0:T(8,128)(2,1)S(1)}, bf16[8,4096]{1,0:T(8,128)(2,1)S(1)}, u32[]{:S(2)}, u32[]{:S(2)}) collective-permute-start(bf16[8,4096]{1,0:T(8,128)(2,1)S(1)} %get-tuple-element.36), channel_id=1, source_target_pairs={{0,8},{4,12},{8,16},{12,20},{16,0},{20,4},{1,9},{5,13},{9,17},{13,... | collective-permute-start | bytes 196616 | tf_op jit(solution)/shard_map/ppermute | solution.py:16
  66.3 10.4 %collective-permute-start.10 = (bf16[8,4096]{1,0:T(8,128)(2,1)S(1)}, bf16[8,4096]{1,0:T(8,128)(2,1)S(1)}, u32[]{:S(2)}, u32[]{:S(2)}) collective-permute-start(bf16[8,4096]{1,0:T(8,128)(2,1)S(1)} %get-tuple-element.35), channel_id=1, source_target_pairs={{0,16},{4,20},{8,0},{12,4},{16,8},{20,12},{1,17},{5,21},{9,1},{13,... | collective-permute-start | bytes 196616 | tf_op jit(solution)/shard_map/ppermute | solution.py:16
  89.2 19.5 %collective-permute-start.13 = (bf16[16,2048]{1,0:T(8,128)(2,1)S(1)}, bf16[16,2048]{1,0:T(8,128)(2,1)S(1)}, u32[]{:S(2)}, u32[]{:S(2)}) collective-permute-start(bf16[16,2048]{1,0:T(8,128)(2,1)S(1)} %pad_maximum_fusion.3), channel_id=1, source_target_pairs={{0,8},{4,12},{8,16},{12,20},{16,0},{20,4},{1,9},{5,13},{9,17},{13,... | collective-permute-start | bytes 196616 | tf_op jit(solution)/shard_map/ppermute | solution.py:16
  91.1 17.6 %collective-permute-start.14 = (bf16[16,2048]{1,0:T(8,128)(2,1)S(1)}, bf16[16,2048]{1,0:T(8,128)(2,1)S(1)}, u32[]{:S(2)}, u32[]{:S(2)}) collective-permute-start(bf16[16,2048]{1,0:T(8,128)(2,1)S(1)} %pad_maximum_fusion.3), channel_id=1, source_target_pairs={{0,16},{4,20},{8,0},{12,4},{16,8},{20,12},{1,17},{5,21},{9,1},{13,... | collective-permute-start | bytes 196616 | tf_op jit(solution)/shard_map/ppermute | solution.py:16
  98.9 12.3 %collective-permute-start.19 = (bf16[16,2048]{1,0:T(8,128)(2,1)S(1)}, bf16[16,2048]{1,0:T(8,128)(2,1)S(1)}, u32[]{:S(2)}, u32[]{:S(2)}) collective-permute-start(bf16[16,2048]{1,0:T(8,128)(2,1)S(1)} %pad_maximum_fusion.4), channel_id=1, source_target_pairs={{0,8},{4,12},{8,16},{12,20},{16,0},{20,4},{1,9},{5,13},{9,17},{13,... | collective-permute-start | bytes 196616 | tf_op jit(solution)/shard_map/ppermute | solution.py:16
  111.2 16.4 %collective-permute-start.21 = (bf16[48,2048]{1,0:T(8,128)(2,1)S(1)}, bf16[48,2048]{1,0:T(8,128)(2,1)S(1)}, u32[]{:S(2)}, u32[]{:S(2)}) collective-permute-start(bf16[48,2048]{1,0:T(8,128)(2,1)S(1)} %pad_maximum_fusion.1), channel_id=1, source_target_pairs={{0,4},{4,0},{8,12},{12,8},{16,20},{20,16},{1,5},{5,1},{9,13},{13,9... | collective-permute-start | bytes 589832 | tf_op jit(solution)/shard_map/ppermute | solution.py:16
  118.5 15.8 %collective-permute-start.16 = (bf16[96,2048]{1,0:T(8,128)(2,1)S(1)}, bf16[96,2048]{1,0:T(8,128)(2,1)S(1)}, u32[]{:S(2)}, u32[]{:S(2)}) collective-permute-start(bf16[96,2048]{1,0:T(8,128)(2,1)S(1)} %constant_dynamic-update-slice_fusion.refs_0_), channel_id=1, source_target_pairs={{0,1},{1,2},{2,3},{3,0},{4,5},{5,6},{6,7},{7,4},{8,9},{9,10},{10,1... | collective-permute-start | bytes 1179656 | tf_op jit(solution)/shard_map/ppermute | solution.py:16
  120.4 19.0 %collective-permute-start.17 = (bf16[96,2048]{1,0:T(8,128)(2,1)S(1)}, bf16[96,2048]{1,0:T(8,128)(2,1)S(1)}, u32[]{:S(2)}, u32[]{:S(2)}) collective-permute-start(bf16[96,2048]{1,0:T(8,128)(2,1)S(1)} %constant_dynamic-update-slice_fusion.refs_0_), channel_id=1, source_target_pairs={{0,2},{1,3},{2,0},{3,1},{4,6},{5,7},{6,4},{7,5},{8,10},{9,11},{10,... | collective-permute-start | bytes 1179656 | tf_op jit(solution)/shard_map/ppermute | solution.py:16
  124.3 23.6 %collective-permute-start.18 = (bf16[96,2048]{1,0:T(8,128)(2,1)S(1)}, bf16[96,2048]{1,0:T(8,128)(2,1)S(1)}, u32[]{:S(2)}, u32[]{:S(2)}) collective-permute-start(bf16[96,2048]{1,0:T(8,128)(2,1)S(1)} %constant_dynamic-update-slice_fusion.refs_0_), channel_id=1, source_target_pairs={{0,3},{1,0},{2,1},{3,2},{4,7},{5,4},{6,5},{7,6},{8,11},{9,8},{10,9... | collective-permute-start | bytes 1179656 | tf_op jit(solution)/shard_map/ppermute | solution.py:16
  127.7 31.2 %collective-permute-start.22 = (bf16[96,2048]{1,0:T(8,128)(2,1)S(1)}, bf16[96,2048]{1,0:T(8,128)(2,1)S(1)}, u32[]{:S(2)}, u32[]{:S(2)}) collective-permute-start(bf16[96,2048]{1,0:T(8,128)(2,1)S(1)} %constant_dynamic-update-slice_fusion.5.refs_0_), channel_id=1, source_target_pairs={{0,1},{1,2},{2,3},{3,0},{4,5},{5,6},{6,7},{7,4},{8,9},{9,10},{10,1... | collective-permute-start | bytes 1179656 | tf_op jit(solution)/shard_map/ppermute | solution.py:16
  131.5 27.5 %collective-permute-start.23 = (bf16[96,2048]{1,0:T(8,128)(2,1)S(1)}, bf16[96,2048]{1,0:T(8,128)(2,1)S(1)}, u32[]{:S(2)}, u32[]{:S(2)}) collective-permute-start(bf16[96,2048]{1,0:T(8,128)(2,1)S(1)} %constant_dynamic-update-slice_fusion.5.refs_0_), channel_id=1, source_target_pairs={{0,2},{1,3},{2,0},{3,1},{4,6},{5,7},{6,4},{7,5},{8,10},{9,11},{10,... | collective-permute-start | bytes 1179656 | tf_op jit(solution)/shard_map/ppermute | solution.py:16
  134.3 24.6 %collective-permute-start.24 = (bf16[96,2048]{1,0:T(8,128)(2,1)S(1)}, bf16[96,2048]{1,0:T(8,128)(2,1)S(1)}, u32[]{:S(2)}, u32[]{:S(2)}) collective-permute-start(bf16[96,2048]{1,0:T(8,128)(2,1)S(1)} %constant_dynamic-update-slice_fusion.5.refs_0_), channel_id=1, source_target_pairs={{0,3},{1,0},{2,1},{3,2},{4,7},{5,4},{6,5},{7,6},{8,11},{9,8},{10,9... | collective-permute-start | bytes 1179656 | tf_op jit(solution)/shard_map/ppermute | solution.py:16
  151.4 17.9 %collective-permute-start.31 = (bf16[1024,256]{1,0:T(8,128)(2,1)}, bf16[1024,256]{1,0:T(8,128)(2,1)}, u32[]{:S(2)}, u32[]{:S(2)}) collective-permute-start(bf16[1024,256]{1,0:T(8,128)(2,1)} %get-tuple-element.19), channel_id=1, source_target_pairs={{0,48},{48,0},{96,144},{144,96},{192,240},{240,192},{288,336},{336... | collective-permute-start | bytes 1572872 | tf_op jit(solution)/shard_map/ppermute | solution.py:16
  162.0 47.8 %collective-permute-start.25 = (f32[192,256]{1,0:T(8,128)S(1)}, f32[192,256]{1,0:T(8,128)S(1)}, u32[]{:S(2)}, u32[]{:S(2)}) collective-permute-start(f32[192,256]{1,0:T(8,128)S(1)} %slice_bitcast_fusion), channel_id=1, source_target_pairs={{0,24},{24,0},{1,25},{25,1},{2,26},{26,2},{3,27},{27,3},{4,28},{28... | collective-permute-start | bytes 589832 | tf_op jit(solution)/shard_map/ppermute | solution.py:16
  165.8 19.5 %collective-permute-start.27 = (bf16[1024,256]{1,0:T(8,128)(2,1)S(1)}, bf16[1024,256]{1,0:T(8,128)(2,1)S(1)}, u32[]{:S(2)}, u32[]{:S(2)}) collective-permute-start(bf16[1024,256]{1,0:T(8,128)(2,1)S(1)} %get-tuple-element.17), channel_id=1, source_target_pairs={{0,48},{48,0},{96,144},{144,96},{192,240},{240,192},{288,336},{336... | collective-permute-start | bytes 1572872 | tf_op jit(solution)/shard_map/ppermute | solution.py:16
  170.5 19.4 %collective-permute-start.34 = (bf16[256,256]{1,0:T(8,128)(2,1)S(1)}, bf16[256,256]{1,0:T(8,128)(2,1)S(1)}, u32[]{:S(2)}, u32[]{:S(2)}) collective-permute-start(bf16[256,256]{1,0:T(8,128)(2,1)S(1)} %get-tuple-element.32), channel_id=1, source_target_pairs={{0,96},{48,144},{96,192},{144,240},{192,288},{240,336},{288,0},{33... | collective-permute-start | bytes 393224 | tf_op jit(solution)/shard_map/ppermute | solution.py:16
  175.0 20.9 %collective-permute-start.33 = (bf16[256,256]{1,0:T(8,128)(2,1)S(1)}, bf16[256,256]{1,0:T(8,128)(2,1)S(1)}, u32[]{:S(2)}, u32[]{:S(2)}) collective-permute-start(bf16[256,256]{1,0:T(8,128)(2,1)S(1)} %get-tuple-element.33), channel_id=1, source_target_pairs={{0,192},{48,240},{96,288},{144,336},{192,0},{240,48},{288,96},{336... | collective-permute-start | bytes 393224 | tf_op jit(solution)/shard_map/ppermute | solution.py:16
  180.1 21.1 %collective-permute-start.32 = (bf16[256,256]{1,0:T(8,128)(2,1)S(1)}, bf16[256,256]{1,0:T(8,128)(2,1)S(1)}, u32[]{:S(2)}, u32[]{:S(2)}) collective-permute-start(bf16[256,256]{1,0:T(8,128)(2,1)S(1)} %get-tuple-element.31), channel_id=1, source_target_pairs={{0,288},{48,336},{96,0},{144,48},{192,96},{240,144},{288,192},{336... | collective-permute-start | bytes 393224 | tf_op jit(solution)/shard_map/ppermute | solution.py:16
  185.6 25.2 %collective-permute-start.30 = (bf16[256,256]{1,0:T(8,128)(2,1)S(1)}, bf16[256,256]{1,0:T(8,128)(2,1)S(1)}, u32[]{:S(2)}, u32[]{:S(2)}) collective-permute-start(bf16[256,256]{1,0:T(8,128)(2,1)S(1)} %get-tuple-element.29), channel_id=1, source_target_pairs={{0,96},{48,144},{96,192},{144,240},{192,288},{240,336},{288,0},{33... | collective-permute-start | bytes 393224 | tf_op jit(solution)/shard_map/ppermute | solution.py:16
  189.9 20.8 %collective-permute-start.29 = (bf16[256,256]{1,0:T(8,128)(2,1)S(1)}, bf16[256,256]{1,0:T(8,128)(2,1)S(1)}, u32[]{:S(2)}, u32[]{:S(2)}) collective-permute-start(bf16[256,256]{1,0:T(8,128)(2,1)S(1)} %get-tuple-element.30), channel_id=1, source_target_pairs={{0,192},{48,240},{96,288},{144,336},{192,0},{240,48},{288,96},{336... | collective-permute-start | bytes 393224 | tf_op jit(solution)/shard_map/ppermute | solution.py:16
  195.9 14.9 %collective-permute-start.28 = (bf16[256,256]{1,0:T(8,128)(2,1)S(1)}, bf16[256,256]{1,0:T(8,128)(2,1)S(1)}, u32[]{:S(2)}, u32[]{:S(2)}) collective-permute-start(bf16[256,256]{1,0:T(8,128)(2,1)S(1)} %get-tuple-element.28), channel_id=1, source_target_pairs={{0,288},{48,336},{96,0},{144,48},{192,96},{240,144},{288,192},{336... | collective-permute-start | bytes 393224 | tf_op jit(solution)/shard_map/ppermute | solution.py:16
  201.2 17.6 %collective-permute-start.35 = (bf16[256,256]{1,0:T(8,128)(2,1)S(1)}, bf16[256,256]{1,0:T(8,128)(2,1)S(1)}, u32[]{:S(2)}, u32[]{:S(2)}) collective-permute-start(bf16[256,256]{1,0:T(8,128)(2,1)S(1)} %fusion.12), channel_id=1, source_target_pairs={{0,384},{384,0},{1,385},{385,1},{2,386},{386,2},{3,387},{387,3},{4... | collective-permute-start | bytes 393224 | tf_op jit(solution)/shard_map/ppermute | solution.py:16
  (14 other events, 278.9 us)

commit v2 on v1

v2 whole, which is shorter than its diff:
```python
import functools

import jax
import jax.numpy as jnp
from jax import lax
from jax.experimental import pallas as pl
from jax.experimental.pallas import tpu as pltpu
from jax.sharding import Mesh, PartitionSpec as P

ZH, Y, CORE, ZL, X = 2, 8, 2, 6, 4
BF, F32 = jnp.bfloat16, jnp.float32
D = 8192
PIECES = 10
VMEM = 24 * 1024 * 1024


def shift(value, axis, size, move):
    return lax.ppermute(value, axis, [(i, move(i)) for i in range(size)])


def to_x(value, r):
    return shift(value, "x", X, lambda i: (i - r) % X)


def to_q(value):
    return shift(value, "zl", ZL, lambda i: i ^ 1)


def to_p(value, r):
    return shift(value, "zl", ZL, lambda i: ((i // 2 - r) % 3) * 2 + i % 2)


def to_v(value):
    return shift(value, "y", Y, lambda i: i ^ 1)


def to_u(value, r):
    return shift(value, "y", Y, lambda i: ((i // 2 - r) % 4) * 2 + i % 2)


def to_core(value):
    return shift(value, "core", CORE, lambda i: i ^ 1)


def to_zh(value):
    return shift(value, "zh", ZH, lambda i: i ^ 1)


def product_kernel(near, weight, *refs):
    outs, held, sems = refs[:8], refs[8], refs[9]
    copies = [
        pltpu.make_async_copy(
            weight.at[:, c * 1024 : (c + 1) * 1024], held.at[:, c * 1024 : (c + 1) * 1024], sems.at[c]
        )
        for c in range(8)
    ]
    for copy in copies:
        copy.start()
    for c in range(8):
        copies[c].wait()
        at = slice(c * 1024, (c + 1) * 1024)
        total = jnp.dot(near[...], held[:, at], preferred_element_type=F32)
        for r in range(8):
            outs[r][:, at] = total[r * 24 : (r + 1) * 24].astype(BF)


def products(near, weight):
    whole = pl.BlockSpec(memory_space=pltpu.VMEM)
    return pl.pallas_call(
        product_kernel,
        out_shape=(jax.ShapeDtypeStruct((24, D), BF),) * 8,
        in_specs=[whole, pl.BlockSpec(memory_space=pltpu.HBM)],
        out_specs=(whole,) * 8,
        scratch_shapes=[pltpu.VMEM((256, D), BF), pltpu.SemaphoreType.DMA((8,))],
        compiler_params=pltpu.CompilerParams(vmem_limit_bytes=VMEM),
        cost_estimate=pl.CostEstimate(
            flops=2 * 192 * 256 * D, bytes_accessed=(256 + 192) * 2 * D, transcendentals=0
        ),
        name="products",
    )(near, weight)


def forward_kernel(value, arrived, held, near, out, held_out, near_out):
    out[...] = (value[...].astype(F32) + arrived[...].astype(F32)).astype(BF)
    held_out[...] = held[...]
    near_out[...] = near[...]


def forward(value, arrived, held, near):
    block = pl.BlockSpec((24, 4096), lambda c: (0, c))
    rows = pl.BlockSpec((192, 128), lambda c: (0, c))
    return pl.pallas_call(
        forward_kernel,
        out_shape=(jax.ShapeDtypeStruct((24, D), BF),) * 2 + (jax.ShapeDtypeStruct((192, 256), BF),),
        grid=(2,),
        in_specs=[block] * 3 + [rows],
        out_specs=(block, block, rows),
        compiler_params=pltpu.CompilerParams(vmem_limit_bytes=16 * 1024 * 1024),
        cost_estimate=pl.CostEstimate(flops=24 * D, bytes_accessed=24 * D * 10, transcendentals=0),
        name="forward",
    )(value, arrived, held, near)


def after_q_kernel(keep, left, right, pair, own, one, two):
    total = keep[...].astype(F32) + left[...].astype(F32)
    total = total + right[...].astype(F32) + pair[...].astype(F32)
    own[...] = total[:8]
    one[...] = total[8:16].astype(BF)
    two[...] = total[16:].astype(BF)


def after_q(keep, left, right, pair):
    block = pl.BlockSpec((24, 2048), lambda c: (0, c))
    rows = pl.BlockSpec((8, 2048), lambda c: (0, c))
    return pl.pallas_call(
        after_q_kernel,
        out_shape=tuple(jax.ShapeDtypeStruct((8, D), kind) for kind in (F32, BF, BF)),
        grid=(D // 2048,),
        in_specs=[block] * 4,
        out_specs=(rows,) * 3,
        compiler_params=pltpu.CompilerParams(vmem_limit_bytes=16 * 1024 * 1024),
        cost_estimate=pl.CostEstimate(flops=24 * D * 4, bytes_accessed=24 * D * 10, transcendentals=0),
        name="after_q",
    )(keep, left, right, pair)


def norm_kernel(place, first, second, third, *refs):
    residual, gain, grad_normed, grad_residual, late, normed, grad_mixed, mine, other = refs
    share = first[...] + second[...].astype(F32) + third[...].astype(F32)
    mixed = residual[...].astype(F32) + share
    rms = jnp.sqrt(jnp.mean(mixed * mixed, axis=-1, keepdims=True) + 1e-05)
    unit = mixed / rms
    normed[...] = (unit * gain[...]).astype(BF)
    scaled = grad_normed[...].astype(F32) * gain[...]
    inner = jnp.mean(scaled * unit, axis=-1, keepdims=True)
    grad_mixed[...] = (grad_residual[...].astype(F32) + (scaled - unit * inner) / rms).astype(BF)
    core, zh, v = place[0], place[1], place[2]
    for side in range(2):
        for k in range(2):
            for u in range(4):
                half = (1 - zh) if k == 0 else zh
                at = (half * Y + u * 2 + (v if side == 0 else 1 - v)) * 2
                put = pl.ds(side * 2048 + k * 1024 + u * 256, 256)
                mine[:, put] = grad_mixed[:, pl.ds(pl.multiple_of((at + core) * 256, 256), 256)]
                other[:, put] = grad_mixed[:, pl.ds(pl.multiple_of((at + 1 - core) * 256, 256), 256)]


def norm(place, sums, residual, gain, grad_normed, grad_residual, late):
    whole = pl.BlockSpec(memory_space=pltpu.VMEM)
    count = len(sums) + 4
    return pl.pallas_call(
        norm_kernel,
        out_shape=(
            jax.ShapeDtypeStruct((8, D), BF),
            jax.ShapeDtypeStruct((8, D), BF),
            jax.ShapeDtypeStruct((8, D // 2), BF),
            jax.ShapeDtypeStruct((8, D // 2), BF),
        ),
        in_specs=[pl.BlockSpec(memory_space=pltpu.SMEM)]
        + [whole] * count
        + [pl.BlockSpec(memory_space=pl.ANY)],
        out_specs=(whole,) * 4,
        compiler_params=pltpu.CompilerParams(vmem_limit_bytes=16 * 1024 * 1024),
        cost_estimate=pl.CostEstimate(flops=8 * D * 20, bytes_accessed=8 * D * 20, transcendentals=0),
        name="norm",
    )(place, *sums, residual, gain, grad_normed, grad_residual, late)


def term_kernel(blocks, turned, *refs):
    pieces, outs = refs[:PIECES], refs[PIECES + 1 :]
    for k in range(2):
        for r in range(4):
            at = pl.ds(pl.multiple_of((k * 4 + blocks[r]) * 256, 256), 256)
            block = jnp.concatenate([piece[:, at] for piece in pieces], axis=0)
            total = jnp.dot(turned[...], block, preferred_element_type=F32)
            outs[k * 4 + r][...] = total.astype(outs[k * 4 + r].dtype)


def term_parts(blocks, turned, pieces, late):
    whole = pl.BlockSpec(memory_space=pltpu.VMEM)
    return pl.pallas_call(
        term_kernel,
        out_shape=tuple(jax.ShapeDtypeStruct((256, 256), kind) for kind in (F32, BF, BF, BF) * 2),
        grid=(1,),
        in_specs=[pl.BlockSpec(memory_space=pltpu.SMEM)]
        + [whole] * (1 + PIECES)
        + [pl.BlockSpec(memory_space=pl.ANY)],
        out_specs=(pl.BlockSpec((256, 256), lambda i: (0, 0)),) * 8,
        compiler_params=pltpu.CompilerParams(vmem_limit_bytes=VMEM),
        cost_estimate=pl.CostEstimate(
            flops=2 * 256 * 768 * 2048, bytes_accessed=5 * 1024 * 1024, transcendentals=0
        ),
        name="term",
    )(blocks, turned, *pieces, late)


def back_kernel(count, first, *refs):
    pieces, weight = refs[:count], refs[count]
    out, held, sems = refs[-3:]
    copies = []
    for c in range(8):
        at = pl.ds(pl.multiple_of((first[c // 4] + 4 * (c % 4)) * 256, 256), 256)
        copies.append(pltpu.make_async_copy(weight.at[:, at], held.at[c], sems.at[c]))
        copies[c].start()
    total = jnp.zeros(out.shape, F32)
    for c in range(8):
        copies[c].wait()
        block = jnp.concatenate([piece[:, c * 256 : (c + 1) * 256] for piece in pieces], axis=0)
        total += lax.dot_general(
            block, held[c], (((1,), (1,)), ((), ())), preferred_element_type=F32
        )
    out[...] = total


def back(first, pieces, weight, late):
    whole = pl.BlockSpec(memory_space=pltpu.VMEM)
    rows = sum(piece.shape[0] for piece in pieces)
    return pl.pallas_call(
        functools.partial(back_kernel, len(pieces)),
        out_shape=jax.ShapeDtypeStruct((rows, 256), F32),
        in_specs=[pl.BlockSpec(memory_space=pltpu.SMEM)]
        + [whole] * len(pieces)
        + [pl.BlockSpec(memory_space=pltpu.HBM), pl.BlockSpec(memory_space=pl.ANY)],
        out_specs=whole,
        scratch_shapes=[pltpu.VMEM((8, 256, 256), BF), pltpu.SemaphoreType.DMA((8,))],
        compiler_params=pltpu.CompilerParams(vmem_limit_bytes=VMEM),
        cost_estimate=pl.CostEstimate(
            flops=2 * 256 * rows * 2048, bytes_accessed=3 * 1024 * 1024, transcendentals=0
        ),
        name="back",
    )(first, *pieces, weight, late)


def apart_kernel(*refs):
    pieces, stay, go = refs[:-2], refs[-2], refs[-1]
    place = 0
    for piece in pieces:
        for r in range(piece.shape[0] // 32):
            for k in range(4):
                put = (k // 2) * 192 + place * 8
                out = (stay, go)[k % 2]
                out[put : put + 8, :] = piece[r * 32 + k * 8 : r * 32 + k * 8 + 8, :]
            place += 1


def apart(pieces):
    whole = pl.BlockSpec(memory_space=pltpu.VMEM)
    return pl.pallas_call(
        apart_kernel,
        out_shape=(jax.ShapeDtypeStruct((384, 256), F32),) * 2,
        in_specs=[whole] * len(pieces),
        out_specs=(whole,) * 2,
        compiler_params=pltpu.CompilerParams(vmem_limit_bytes=VMEM),
        cost_estimate=pl.CostEstimate(flops=0, bytes_accessed=1536 * 1024, transcendentals=0),
        name="apart",
    )(*pieces)


def per_device(attention, out_proj, residual, gain, grad_normed, grad_residual):
    x, zl, y = lax.axis_index("x"), lax.axis_index("zl"), lax.axis_index("y")
    core, zh = lax.axis_index("core"), lax.axis_index("zh")

    r = jnp.arange(24, dtype=jnp.int32)
    owner_x = (x - r // 6 + X) % X
    owner_q = (zl % 2) ^ ((r // 3) % 2)
    owner_p = (zl // 2 - r % 3 + 3) % 3
    owner = (owner_p * 2 + owner_q) * X + owner_x
    token = jnp.repeat(owner * 8, 8) + jnp.tile(jnp.arange(8, dtype=jnp.int32), 24)
    order = (token[:, None] == jnp.arange(192, dtype=jnp.int32)[None, :]).astype(BF)
    near = jnp.dot(order, attention, preferred_element_type=F32).astype(BF)

    keep, send, one_keep, one_send, left, right, three_keep, three_send = products(near, out_proj)
    left, right = to_x(left, 1), to_x(right, 3)
    right = to_x((three_send.astype(F32) + right.astype(F32)).astype(BF), 3)
    from_right = to_x(one_send, 1)
    left, three_keep, near_late = forward(one_keep, left, three_keep, near)
    left, from_left = to_x(left, 1), to_x(three_keep, 3)
    send = send.astype(F32) + from_right.astype(F32) + right.astype(F32)
    pair = to_q(send.astype(BF))

    far = to_core(near_late)
    both = jnp.concatenate([near.reshape(24, 8, 256), far.reshape(24, 8, 256)], axis=1)
    both = jnp.concatenate([both, to_v(both)], axis=1)
    turned = both.reshape(768, 256).T
    mine, one, two = after_q(keep, left, from_left, pair)
    sums = (mine, to_p(one, 1), to_p(two, 2))

    u, v = y // 2, y % 2
    place = jnp.stack([core, zh, v]).astype(jnp.int32)
    normed, grad_mixed, mine, other = norm(
        place, sums, residual, gain.reshape(1, D), grad_normed, grad_residual, turned
    )
    other = to_core(other)
    blocks = (u - jnp.arange(4, dtype=jnp.int32) + 4) % 4

    own = jnp.concatenate([mine, other], axis=0)
    own = jnp.concatenate([own[:, :2048], to_v(own[:, 2048:])], axis=0)
    line = jnp.concatenate([own, to_p(own, -1), to_p(own, -2)], axis=0)
    lines = (line, to_q(line))
    ones = [to_x(part, -1) for part in lines]
    threes = [to_x(part, -3) for part in lines]
    twos = [(to_x(one[:48], -1), to_x(three[48:], -3)) for one, three in zip(ones, threes)]
    pieces = [*lines, *ones, *twos[0], *twos[1], *threes]

    first = jnp.stack([1 - zh, zh]).astype(jnp.int32) * 16 + (v * 2 + core).astype(jnp.int32)
    early = back(first, [*lines, *ones, *threes], out_proj, blocks)
    parts = term_parts(blocks, turned, pieces, early)
    got = [[to_u(parts[k * 4 + r], r) for r in (1, 2, 3)] for k in range(2)]
    sums = [parts[k * 4] + sum(value.astype(F32) for value in got[k]) for k in range(2)]
    passing = sums[0].astype(BF)
    grad_out_proj = sums[1] + to_zh(passing).astype(F32)

    late = back(first, [*twos[0], *twos[1]], out_proj, parts[4])
    stay, go = apart([early[:384], late, early[384:]])
    stay = stay + to_core(go)
    ours = stay[:192] + to_v(stay[192:])
    grad_attention = lax.dot_general(
        order, ours.astype(BF), (((0,), (0,)), ((), ())), preferred_element_type=F32
    ).astype(BF)
    return (normed, grad_mixed, grad_attention, grad_out_proj)


def solution(mesh):
    dp, tensor = ("zh", "y", "core"), ("zl", "x")
    fine = Mesh(mesh.devices.reshape(ZH, Y, CORE, ZL, X), dp + tensor)
    rows = P(dp + tensor, None)
    return jax.shard_map(
        per_device,
        mesh=fine,
        in_specs=(P(dp, tensor), P(tensor, None), rows, P(), rows, rows),
        out_specs=(rows, rows, P(dp, tensor), P(tensor, dp)),
        check_vma=False,
    )
```

time: 221 us -> 190 us (0.86)
  the two profiles are of different devices: /device:TPU:14 before, /device:TPU:16 now
where the time goes in v2:
time: 190 us; the launch traced here: 189 us
  starting transfers between devices  124 us (65%)
  waiting for transfers between devices  39.1 us (21%)
  Pallas kernels  12.2 us (6%)
  local copies, waits for them, and re-layouts  8.18 us (4%)
  other arithmetic  3.15 us (2%)
    ppermute x33, starting transfers between devices, shift(): return lax.ppermute(value, axis, [(i, move(i)) for i in range(size)])  124 us
    ppermute x33, waiting for transfers between devices, shift(): return lax.ppermute(value, axis, [(i, move(i)) for i in range(size)])  39.1 us
    pallas_call x2, Pallas kernels, back(): pl.pallas_call(functools.partial(back_kernel, len(pieces)), out_shape=jax...  5.1 us
    unnamed x17, local copies, waits for them, and re-layouts  5.08 us
  transfers between devices with their start and end apart: 33, of which 16 were waited for; matrix products, arithmetic and copies ran while one was open for 3% of the time, Pallas kernels for 3%

profile of v2, /device:TPU:16, one launch (start us, length us, event | category | flops | bytes accessed | tf_op | source)
XLA Modules:
  0.0 188.9 jit_solution(10107668530539399604)
XLA Ops:
  3.9 2.7 %products.1 = (bf16[24,8192]{1,0:T(8,128)(2,1)S(1)}, bf16[24,8192]{1,0:T(8,128)(2,1)S(1)}, bf16[24,8192]{1,0:T(8,128)(2,1)S(1)}, bf16[24,8192]{1,0:T(8,128)(2,1)...) custom-call(bf16[192,256]{1,0:T(8,128)(2,1)S(1)} %convolution_conver, ...), custom_call_target="tpu_custom_call" | custom-call | flops 805306368 | bytes 7340032 | tf_op jit(solution)/shard_map/products/pallas_call | solution.py:69
  6.7 3.5 %collective-permute-start.4 = (bf16[24,8192]{1,0:T(8,128)(2,1)S(1)}, bf16[24,8192]{1,0:T(8,128)(2,1)S(1)}, u32[]{:S(2)}, u32[]{:S(2)}) collective-permute-start(bf16[24,8192]{1,0:T(8,128)(2,1)S(1)} %get-tuple-element.41), channel_id=1, source_target_pairs={{0,1},{1,2},{2,3},{3,0},{4,5},{5,6},{6,7},{7,4},{8,9},{9,10},{10,1... | collective-permute-start | bytes 1179656 | tf_op jit(solution)/shard_map/ppermute | solution.py:18
  10.2 3.7 %collective-permute-start = (bf16[24,8192]{1,0:T(8,128)(2,1)S(1)}, bf16[24,8192]{1,0:T(8,128)(2,1)S(1)}, u32[]{:S(2)}, u32[]{:S(2)}) collective-permute-start(bf16[24,8192]{1,0:T(8,128)(2,1)S(1)} %get-tuple-element.34), channel_id=1, source_target_pairs={{0,3},{1,0},{2,1},{3,2},{4,7},{5,4},{6,5},{7,6},{8,11},{9,8},{10,9... | collective-permute-start | bytes 1179656 | tf_op jit(solution)/shard_map/ppermute | solution.py:18
  13.9 3.5 %collective-permute-start.3 = (bf16[24,8192]{1,0:T(8,128)(2,1)S(1)}, bf16[24,8192]{1,0:T(8,128)(2,1)S(1)}, u32[]{:S(2)}, u32[]{:S(2)}) collective-permute-start(bf16[24,8192]{1,0:T(8,128)(2,1)S(1)} %get-tuple-element.39), channel_id=1, source_target_pairs={{0,3},{1,0},{2,1},{3,2},{4,7},{5,4},{6,5},{7,6},{8,11},{9,8},{10,9... | collective-permute-start | bytes 1179656 | tf_op jit(solution)/shard_map/ppermute | solution.py:18
  17.4 3.4 %collective-permute-done.4 = bf16[24,8192]{1,0:T(8,128)(2,1)S(1)} collective-permute-done((bf16[24,8192]{1,0:T(8,128)(2,1)S(1)}, bf16[24,8192]{1,0:T(8,128)(2,1)S(1)}, u32[]{:S(2)}, u32[]{:S(2)}) %collective-permute-start.4) | collective-permute-done | bytes 393248 | tf_op jit(solution)/shard_map/ppermute | solution.py:18
  24.5 4.9 %collective-permute-start.1 = (bf16[24,8192]{1,0:T(8,128)(2,1)S(1)}, bf16[24,8192]{1,0:T(8,128)(2,1)S(1)}, u32[]{:S(2)}, u32[]{:S(2)}) collective-permute-start(bf16[24,8192]{1,0:T(8,128)(2,1)S(1)} %get-tuple-element.36), channel_id=1, source_target_pairs={{0,3},{1,0},{2,1},{3,2},{4,7},{5,4},{6,5},{7,6},{8,11},{9,8},{10,9... | collective-permute-start | bytes 1179656 | tf_op jit(solution)/shard_map/ppermute | solution.py:18
  32.6 2.9 %collective-permute-done.5 = bf16[24,8192]{1,0:T(8,128)(2,1)S(1)} collective-permute-done((bf16[24,8192]{1,0:T(8,128)(2,1)S(1)}, bf16[24,8192]{1,0:T(8,128)(2,1)S(1)}, u32[]{:S(2)}, u32[]{:S(2)}) %collective-permute-start.5) | collective-permute-done | bytes 393248 | tf_op jit(solution)/shard_map/ppermute | solution.py:18
  36.3 4.3 %collective-permute-start.6 = (bf16[24,8192]{1,0:T(8,128)(2,1)}, bf16[24,8192]{1,0:T(8,128)(2,1)S(1)}, u32[]{:S(2)}, u32[]{:S(2)}) collective-permute-start(bf16[24,8192]{1,0:T(8,128)(2,1)} %add_convert_fusion), channel_id=1, source_target_pairs={{0,4},{4,0},{8,12},{12,8},{16,20},{20,16},{1,5},{5,1},{9,13},{13,9... | collective-permute-start | bytes 1179656 | tf_op jit(solution)/shard_map/ppermute | solution.py:18
  43.8 3.5 %collective-permute-start.10 = (bf16[24,16,256]{2,1,0:T(8,128)(2,1)S(1)}, bf16[24,16,256]{2,1,0:T(8,128)(2,1)}, u32[]{:S(2)}, u32[]{:S(2)}) collective-permute-start(bf16[24,16,256]{2,1,0:T(8,128)(2,1)S(1)} %pad_maximum_fusion.2), channel_id=1, source_target_pairs={{0,48},{48,0},{96,144},{144,96},{192,240},{240,192},{288,336},{336... | collective-permute-start | bytes 589832 | tf_op jit(solution)/shard_map/ppermute | solution.py:18
  47.8 10.9 %collective-permute-start.7 = (bf16[8,8192]{1,0:T(8,128)(2,1)S(1)}, bf16[8,8192]{1,0:T(8,128)(2,1)S(1)}, u32[]{:S(2)}, u32[]{:S(2)}) collective-permute-start(bf16[8,8192]{1,0:T(8,128)(2,1)S(1)} %get-tuple-element.43), channel_id=1, source_target_pairs={{0,16},{4,20},{8,0},{12,4},{16,8},{20,12},{1,17},{5,21},{9,1},{13,... | collective-permute-start | bytes 393224 | tf_op jit(solution)/shard_map/ppermute | solution.py:18
  62.5 9.3 %collective-permute-done.8.third = bf16[8,8192]{1,0:T(8,128)(2,1)S(1)} collective-permute-done((bf16[8,8192]{1,0:T(8,128)(2,1)S(1)}, bf16[8,8192]{1,0:T(8,128)(2,1)S(1)}, u32[]{:S(2)}, u32[]{:S(2)}) %collective-permute-start.8) | collective-permute-done | bytes 131104 | tf_op jit(solution)/shard_map/ppermute | solution.py:18
  76.6 2.4 %collective-permute-start.12 = (bf16[16,2048]{1,0:T(8,128)(2,1)S(1)}, bf16[16,2048]{1,0:T(8,128)(2,1)S(1)}, u32[]{:S(2)}, u32[]{:S(2)}) collective-permute-start(bf16[16,2048]{1,0:T(8,128)(2,1)S(1)} %get-tuple-element.61), channel_id=1, source_target_pairs={{0,48},{48,0},{96,144},{144,96},{192,240},{240,192},{288,336},{336... | collective-permute-start | bytes 196616 | tf_op jit(solution)/shard_map/ppermute | solution.py:18
  79.0 3.8 %collective-permute-done.12 = bf16[16,2048]{1,0:T(8,128)(2,1)S(1)} collective-permute-done((bf16[16,2048]{1,0:T(8,128)(2,1)S(1)}, bf16[16,2048]{1,0:T(8,128)(2,1)S(1)}, u32[]{:S(2)}, u32[]{:S(2)}) %collective-permute-start.12) | collective-permute-done | bytes 65568 | tf_op jit(solution)/shard_map/ppermute | solution.py:18
  84.7 4.8 %collective-permute-start.13 = (bf16[32,2048]{1,0:T(8,128)(2,1)S(1)}, bf16[32,2048]{1,0:T(8,128)(2,1)S(1)}, u32[]{:S(2)}, u32[]{:S(2)}) collective-permute-start(bf16[32,2048]{1,0:T(8,128)(2,1)S(1)} %pad_maximum_fusion.3), channel_id=1, source_target_pairs={{0,8},{4,12},{8,16},{12,20},{16,0},{20,4},{1,9},{5,13},{9,17},{13,... | collective-permute-start | bytes 393224 | tf_op jit(solution)/shard_map/ppermute | solution.py:18
  89.5 4.3 %collective-permute-done.14 = bf16[32,2048]{1,0:T(8,128)(2,1)S(1)} collective-permute-done((bf16[32,2048]{1,0:T(8,128)(2,1)S(1)}, bf16[32,2048]{1,0:T(8,128)(2,1)S(1)}, u32[]{:S(2)}, u32[]{:S(2)}) %collective-permute-start.14) | collective-permute-done | bytes 131104 | tf_op jit(solution)/shard_map/ppermute | solution.py:18
  95.5 6.4 %collective-permute-start.15 = (bf16[96,2048]{1,0:T(8,128)(2,1)S(1)}, bf16[96,2048]{1,0:T(8,128)(2,1)S(1)}, u32[]{:S(2)}, u32[]{:S(2)}) collective-permute-start(bf16[96,2048]{1,0:T(8,128)(2,1)S(1)} %pad_maximum_fusion.1.refs_0_), channel_id=1, source_target_pairs={{0,4},{4,0},{8,12},{12,8},{16,20},{20,16},{1,5},{5,1},{9,13},{13,9... | collective-permute-start | bytes 1179656 | tf_op jit(solution)/shard_map/ppermute | solution.py:18
  101.9 2.8 %collective-permute-start.18 = (bf16[96,2048]{1,0:T(8,128)(2,1)S(1)}, bf16[96,2048]{1,0:T(8,128)(2,1)S(1)}, u32[]{:S(2)}, u32[]{:S(2)}) collective-permute-start(bf16[96,2048]{1,0:T(8,128)(2,1)S(1)} %pad_maximum_fusion.1.refs_0_), channel_id=1, source_target_pairs={{0,3},{1,0},{2,1},{3,2},{4,7},{5,4},{6,5},{7,6},{8,11},{9,8},{10,9... | collective-permute-start | bytes 1179656 | tf_op jit(solution)/shard_map/ppermute | solution.py:18
  104.8 3.0 %collective-permute-start.16 = (bf16[96,2048]{1,0:T(8,128)(2,1)S(1)}, bf16[96,2048]{1,0:T(8,128)(2,1)S(1)}, u32[]{:S(2)}, u32[]{:S(2)}) collective-permute-start(bf16[96,2048]{1,0:T(8,128)(2,1)S(1)} %pad_maximum_fusion.1.refs_0_), channel_id=1, source_target_pairs={{0,1},{1,2},{2,3},{3,0},{4,5},{5,6},{6,7},{7,4},{8,9},{9,10},{10,1... | collective-permute-start | bytes 1179656 | tf_op jit(solution)/shard_map/ppermute | solution.py:18
  108.8 3.1 %collective-permute-start.19 = (bf16[96,2048]{1,0:T(8,128)(2,1)S(1)}, bf16[96,2048]{1,0:T(8,128)(2,1)S(1)}, u32[]{:S(2)}, u32[]{:S(2)}) collective-permute-start(bf16[96,2048]{1,0:T(8,128)(2,1)S(1)} %collective-permute-done.15.refs_1_), channel_id=1, source_target_pairs={{0,3},{1,0},{2,1},{3,2},{4,7},{5,4},{6,5},{7,6},{8,11},{9,8},{10,9... | collective-permute-start | bytes 1179656 | tf_op jit(solution)/shard_map/ppermute | solution.py:18
  111.9 2.8 %collective-permute-start.17 = (bf16[96,2048]{1,0:T(8,128)(2,1)S(1)}, bf16[96,2048]{1,0:T(8,128)(2,1)S(1)}, u32[]{:S(2)}, u32[]{:S(2)}) collective-permute-start(bf16[96,2048]{1,0:T(8,128)(2,1)S(1)} %collective-permute-done.15.refs_1_), channel_id=1, source_target_pairs={{0,1},{1,2},{2,3},{3,0},{4,5},{5,6},{6,7},{7,4},{8,9},{9,10},{10,1... | collective-permute-start | bytes 1179656 | tf_op jit(solution)/shard_map/ppermute | solution.py:18
  115.3 4.3 %collective-permute-start.21 = (bf16[48,2048]{1,0:T(8,128)(2,1)}, bf16[48,2048]{1,0:T(8,128)(2,1)S(1)}, u32[]{:S(2)}, u32[]{:S(2)}) collective-permute-start(bf16[48,2048]{1,0:T(8,128)(2,1)} %slice.44), channel_id=1, source_target_pairs={{0,3},{1,0},{2,1},{3,2},{4,7},{5,4},{6,5},{7,6},{8,11},{9,8},{10,9... | collective-permute-start | bytes 589832 | tf_op jit(solution)/shard_map/ppermute | solution.py:18
  123.4 4.7 %collective-permute-start.23 = (bf16[48,2048]{1,0:T(8,128)(2,1)}, bf16[48,2048]{1,0:T(8,128)(2,1)S(1)}, u32[]{:S(2)}, u32[]{:S(2)}) collective-permute-start(bf16[48,2048]{1,0:T(8,128)(2,1)} %slice.46), channel_id=1, source_target_pairs={{0,3},{1,0},{2,1},{3,2},{4,7},{5,4},{6,5},{7,6},{8,11},{9,8},{10,9... | collective-permute-start | bytes 589832 | tf_op jit(solution)/shard_map/ppermute | solution.py:18
  133.0 2.8 %back.2.refs_10_ = f32[576,256]{1,0:T(8,128)S(1)} custom-call(s32[2]{0:T(128)S(1)} %fusion.18.first, bf16[96,2048]{1,0:T(8,128)(2,1)S(1)} %pad_maximum_fusion.1.refs_0_, bf16[96,2048]{1,0:T(8,128)(2,1)S(1)} %collective-permute-done.15.refs_1_, bf16[96,2048]{1,0:T(8,128)(2,1)S(1)} %collective-permute-done.16.refs_2_, ...), custom_call_target="tpu_custom_call" | custom-call | flops 603979776 | bytes 3145728 | tf_op jit(solution)/shard_map/back/pallas_call | solution.py:218
  142.1 6.8 %collective-permute-start.30 = (bf16[256,256]{1,0:T(8,128)(2,1)S(1)}, bf16[256,256]{1,0:T(8,128)(2,1)S(1)}, u32[]{:S(2)}, u32[]{:S(2)}) collective-permute-start(bf16[256,256]{1,0:T(8,128)(2,1)S(1)} %get-tuple-element.58), channel_id=1, source_target_pairs={{0,192},{48,240},{96,288},{144,336},{192,0},{240,48},{288,96},{336... | collective-permute-start | bytes 393224 | tf_op jit(solution)/shard_map/ppermute | solution.py:18
  148.9 3.9 %collective-permute-start.31 = (bf16[256,256]{1,0:T(8,128)(2,1)S(1)}, bf16[256,256]{1,0:T(8,128)(2,1)S(1)}, u32[]{:S(2)}, u32[]{:S(2)}) collective-permute-start(bf16[256,256]{1,0:T(8,128)(2,1)S(1)} %get-tuple-element.59), channel_id=1, source_target_pairs={{0,96},{48,144},{96,192},{144,240},{192,288},{240,336},{288,0},{33... | collective-permute-start | bytes 393224 | tf_op jit(solution)/shard_map/ppermute | solution.py:18
  152.9 2.3 %back.3.refs_1_ = f32[192,256]{1,0:T(8,128)S(1)} custom-call(s32[2]{0:T(128)S(1)} %fusion.18.first, bf16[48,2048]{1,0:T(8,128)(2,1)S(1)} %collective-permute-done.20.refs_4_.refs_0_, bf16[48,2048]{1,0:T(8,128)(2,1)S(1)} %collective-permute-done.21.refs_5_.refs_1_, bf16[48,2048]{1,0:T(8,128)(2,1)} %collective-permute-done.22.refs_6_.refs_2_, ...), custom_call_target="tpu_custom_call" | custom-call | flops 201326592 | bytes 3145728 | tf_op jit(solution)/shard_map/back/pallas_call | solution.py:218
  157.3 2.8 %collective-permute-start.26 = (bf16[256,256]{1,0:T(8,128)(2,1)S(1)}, bf16[256,256]{1,0:T(8,128)(2,1)S(1)}, u32[]{:S(2)}, u32[]{:S(2)}) collective-permute-start(bf16[256,256]{1,0:T(8,128)(2,1)S(1)} %get-tuple-element.53), channel_id=1, source_target_pairs={{0,288},{48,336},{96,0},{144,48},{192,96},{240,144},{288,192},{336... | collective-permute-start | bytes 393224 | tf_op jit(solution)/shard_map/ppermute | solution.py:18
  160.1 3.8 %collective-permute-start.27 = (bf16[256,256]{1,0:T(8,128)(2,1)S(1)}, bf16[256,256]{1,0:T(8,128)(2,1)S(1)}, u32[]{:S(2)}, u32[]{:S(2)}) collective-permute-start(bf16[256,256]{1,0:T(8,128)(2,1)S(1)} %get-tuple-element.54), channel_id=1, source_target_pairs={{0,192},{48,240},{96,288},{144,336},{192,0},{240,48},{288,96},{336... | collective-permute-start | bytes 393224 | tf_op jit(solution)/shard_map/ppermute | solution.py:18
  163.9 6.0 %collective-permute-start.28 = (bf16[256,256]{1,0:T(8,128)(2,1)S(1)}, bf16[256,256]{1,0:T(8,128)(2,1)S(1)}, u32[]{:S(2)}, u32[]{:S(2)}) collective-permute-start(bf16[256,256]{1,0:T(8,128)(2,1)S(1)} %get-tuple-element.55), channel_id=1, source_target_pairs={{0,96},{48,144},{96,192},{144,240},{192,288},{240,336},{288,0},{33... | collective-permute-start | bytes 393224 | tf_op jit(solution)/shard_map/ppermute | solution.py:18
  170.0 9.8 %collective-permute-start.32 = (bf16[256,256]{1,0:T(8,128)(2,1)S(1)}, bf16[256,256]{1,0:T(8,128)(2,1)S(1)}, u32[]{:S(2)}, u32[]{:S(2)}) collective-permute-start(bf16[256,256]{1,0:T(8,128)(2,1)S(1)} %add_convert_fusion.2), channel_id=1, source_target_pairs={{0,384},{384,0},{1,385},{385,1},{2,386},{386,2},{3,387},{387,3},{4... | collective-permute-start | bytes 393224 | tf_op jit(solution)/shard_map/ppermute | solution.py:18
  179.9 2.5 %collective-permute-start.25 = (f32[192,256]{1,0:T(8,128)S(1)}, f32[192,256]{1,0:T(8,128)S(1)}, u32[]{:S(2)}, u32[]{:S(2)}) collective-permute-start(f32[192,256]{1,0:T(8,128)S(1)} %slice.49), channel_id=1, source_target_pairs={{0,48},{48,0},{96,144},{144,96},{192,240},{240,192},{288,336},{336... | collective-permute-start | bytes 589832 | tf_op jit(solution)/shard_map/ppermute | solution.py:18
  184.3 3.7 %collective-permute-done.25 = f32[192,256]{1,0:T(8,128)S(1)} collective-permute-done((f32[192,256]{1,0:T(8,128)S(1)}, f32[192,256]{1,0:T(8,128)S(1)}, u32[]{:S(2)}, u32[]{:S(2)}) %collective-permute-start.25) | collective-permute-done | bytes 196640 | tf_op jit(solution)/shard_map/ppermute | solution.py:18
  (86 shorter events, 48.3 us)
Async XLA Ops:
  6.7 14.1 %collective-permute-start.4 = (bf16[24,8192]{1,0:T(8,128)(2,1)S(1)}, bf16[24,8192]{1,0:T(8,128)(2,1)S(1)}, u32[]{:S(2)}, u32[]{:S(2)}) collective-permute-start(bf16[24,8192]{1,0:T(8,128)(2,1)S(1)} %get-tuple-element.41), channel_id=1, source_target_pairs={{0,1},{1,2},{2,3},{3,0},{4,5},{5,6},{6,7},{7,4},{8,9},{9,10},{10,1... | collective-permute-start | bytes 1179656 | tf_op jit(solution)/shard_map/ppermute | solution.py:18
  10.2 13.9 %collective-permute-start = (bf16[24,8192]{1,0:T(8,128)(2,1)S(1)}, bf16[24,8192]{1,0:T(8,128)(2,1)S(1)}, u32[]{:S(2)}, u32[]{:S(2)}) collective-permute-start(bf16[24,8192]{1,0:T(8,128)(2,1)S(1)} %get-tuple-element.34), channel_id=1, source_target_pairs={{0,3},{1,0},{2,1},{3,2},{4,7},{5,4},{6,5},{7,6},{8,11},{9,8},{10,9... | collective-permute-start | bytes 1179656 | tf_op jit(solution)/shard_map/ppermute | solution.py:18
  13.9 18.7 %collective-permute-start.3 = (bf16[24,8192]{1,0:T(8,128)(2,1)S(1)}, bf16[24,8192]{1,0:T(8,128)(2,1)S(1)}, u32[]{:S(2)}, u32[]{:S(2)}) collective-permute-start(bf16[24,8192]{1,0:T(8,128)(2,1)S(1)} %get-tuple-element.39), channel_id=1, source_target_pairs={{0,3},{1,0},{2,1},{3,2},{4,7},{5,4},{6,5},{7,6},{8,11},{9,8},{10,9... | collective-permute-start | bytes 1179656 | tf_op jit(solution)/shard_map/ppermute | solution.py:18
  20.9 14.6 %collective-permute-start.5 = (bf16[24,8192]{1,0:T(8,128)(2,1)S(1)}, bf16[24,8192]{1,0:T(8,128)(2,1)S(1)}, u32[]{:S(2)}, u32[]{:S(2)}) collective-permute-start(bf16[24,8192]{1,0:T(8,128)(2,1)S(1)} %add_convert_fusion.1), channel_id=1, source_target_pairs={{0,1},{1,2},{2,3},{3,0},{4,5},{5,6},{6,7},{7,4},{8,9},{9,10},{10,1... | collective-permute-start | bytes 1179656 | tf_op jit(solution)/shard_map/ppermute | solution.py:18
  24.5 22.8 %collective-permute-start.1 = (bf16[24,8192]{1,0:T(8,128)(2,1)S(1)}, bf16[24,8192]{1,0:T(8,128)(2,1)S(1)}, u32[]{:S(2)}, u32[]{:S(2)}) collective-permute-start(bf16[24,8192]{1,0:T(8,128)(2,1)S(1)} %get-tuple-element.36), channel_id=1, source_target_pairs={{0,3},{1,0},{2,1},{3,2},{4,7},{5,4},{6,5},{7,6},{8,11},{9,8},{10,9... | collective-permute-start | bytes 1179656 | tf_op jit(solution)/shard_map/ppermute | solution.py:18
  29.4 18.0 %collective-permute-start.2 = (bf16[24,8192]{1,0:T(8,128)(2,1)S(1)}, bf16[24,8192]{1,0:T(8,128)(2,1)S(1)}, u32[]{:S(2)}, u32[]{:S(2)}) collective-permute-start(bf16[24,8192]{1,0:T(8,128)(2,1)S(1)} %get-tuple-element.37), channel_id=1, source_target_pairs={{0,1},{1,2},{2,3},{3,0},{4,5},{5,6},{6,7},{7,4},{8,9},{9,10},{10,1... | collective-permute-start | bytes 1179656 | tf_op jit(solution)/shard_map/ppermute | solution.py:18
  36.3 11.0 %collective-permute-start.6 = (bf16[24,8192]{1,0:T(8,128)(2,1)}, bf16[24,8192]{1,0:T(8,128)(2,1)S(1)}, u32[]{:S(2)}, u32[]{:S(2)}) collective-permute-start(bf16[24,8192]{1,0:T(8,128)(2,1)} %add_convert_fusion), channel_id=1, source_target_pairs={{0,4},{4,0},{8,12},{12,8},{16,20},{20,16},{1,5},{5,1},{9,13},{13,9... | collective-permute-start | bytes 1179656 | tf_op jit(solution)/shard_map/ppermute | solution.py:18
  40.6 3.2 %collective-permute-start.9 = (bf16[192,256]{1,0:T(8,128)(2,1)S(1)}, bf16[192,256]{1,0:T(8,128)(2,1)S(1)}, u32[]{:S(2)}, u32[]{:S(2)}) collective-permute-start(bf16[192,256]{1,0:T(8,128)(2,1)S(1)} %get-tuple-element.45), channel_id=1, source_target_pairs={{0,24},{24,0},{1,25},{25,1},{2,26},{26,2},{3,27},{27,3},{4,28},{28... | collective-permute-start | bytes 294920 | tf_op jit(solution)/shard_map/ppermute | solution.py:18
  43.8 16.9 %collective-permute-start.10 = (bf16[24,16,256]{2,1,0:T(8,128)(2,1)S(1)}, bf16[24,16,256]{2,1,0:T(8,128)(2,1)}, u32[]{:S(2)}, u32[]{:S(2)}) collective-permute-start(bf16[24,16,256]{2,1,0:T(8,128)(2,1)S(1)} %pad_maximum_fusion.2), channel_id=1, source_target_pairs={{0,48},{48,0},{96,144},{144,96},{192,240},{240,192},{288,336},{336... | collective-permute-start | bytes 589832 | tf_op jit(solution)/shard_map/ppermute | solution.py:18
  47.8 14.7 %collective-permute-start.7 = (bf16[8,8192]{1,0:T(8,128)(2,1)S(1)}, bf16[8,8192]{1,0:T(8,128)(2,1)S(1)}, u32[]{:S(2)}, u32[]{:S(2)}) collective-permute-start(bf16[8,8192]{1,0:T(8,128)(2,1)S(1)} %get-tuple-element.43), channel_id=1, source_target_pairs={{0,16},{4,20},{8,0},{12,4},{16,8},{20,12},{1,17},{5,21},{9,1},{13,... | collective-permute-start | bytes 393224 | tf_op jit(solution)/shard_map/ppermute | solution.py:18
  58.7 13.1 %collective-permute-start.8 = (bf16[8,8192]{1,0:T(8,128)(2,1)S(1)}, bf16[8,8192]{1,0:T(8,128)(2,1)S(1)}, u32[]{:S(2)}, u32[]{:S(2)}) collective-permute-start(bf16[8,8192]{1,0:T(8,128)(2,1)S(1)} %get-tuple-element.44), channel_id=1, source_target_pairs={{0,8},{4,12},{8,16},{12,20},{16,0},{20,4},{1,9},{5,13},{9,17},{13,... | collective-permute-start | bytes 393224 | tf_op jit(solution)/shard_map/ppermute | solution.py:18
  76.6 6.2 %collective-permute-start.12 = (bf16[16,2048]{1,0:T(8,128)(2,1)S(1)}, bf16[16,2048]{1,0:T(8,128)(2,1)S(1)}, u32[]{:S(2)}, u32[]{:S(2)}) collective-permute-start(bf16[16,2048]{1,0:T(8,128)(2,1)S(1)} %get-tuple-element.61), channel_id=1, source_target_pairs={{0,48},{48,0},{96,144},{144,96},{192,240},{240,192},{288,336},{336... | collective-permute-start | bytes 196616 | tf_op jit(solution)/shard_map/ppermute | solution.py:18
  82.8 11.1 %collective-permute-start.14 = (bf16[32,2048]{1,0:T(8,128)(2,1)S(1)}, bf16[32,2048]{1,0:T(8,128)(2,1)S(1)}, u32[]{:S(2)}, u32[]{:S(2)}) collective-permute-start(bf16[32,2048]{1,0:T(8,128)(2,1)S(1)} %pad_maximum_fusion.3), channel_id=1, source_target_pairs={{0,16},{4,20},{8,0},{12,4},{16,8},{20,12},{1,17},{5,21},{9,1},{13,... | collective-permute-start | bytes 393224 | tf_op jit(solution)/shard_map/ppermute | solution.py:18
  84.7 10.8 %collective-permute-start.13 = (bf16[32,2048]{1,0:T(8,128)(2,1)S(1)}, bf16[32,2048]{1,0:T(8,128)(2,1)S(1)}, u32[]{:S(2)}, u32[]{:S(2)}) collective-permute-start(bf16[32,2048]{1,0:T(8,128)(2,1)S(1)} %pad_maximum_fusion.3), channel_id=1, source_target_pairs={{0,8},{4,12},{8,16},{12,20},{16,0},{20,4},{1,9},{5,13},{9,17},{13,... | collective-permute-start | bytes 393224 | tf_op jit(solution)/shard_map/ppermute | solution.py:18
  95.5 13.3 %collective-permute-start.15 = (bf16[96,2048]{1,0:T(8,128)(2,1)S(1)}, bf16[96,2048]{1,0:T(8,128)(2,1)S(1)}, u32[]{:S(2)}, u32[]{:S(2)}) collective-permute-start(bf16[96,2048]{1,0:T(8,128)(2,1)S(1)} %pad_maximum_fusion.1.refs_0_), channel_id=1, source_target_pairs={{0,4},{4,0},{8,12},{12,8},{16,20},{20,16},{1,5},{5,1},{9,13},{13,9... | collective-permute-start | bytes 1179656 | tf_op jit(solution)/shard_map/ppermute | solution.py:18
  101.9 12.7 %collective-permute-start.18 = (bf16[96,2048]{1,0:T(8,128)(2,1)S(1)}, bf16[96,2048]{1,0:T(8,128)(2,1)S(1)}, u32[]{:S(2)}, u32[]{:S(2)}) collective-permute-start(bf16[96,2048]{1,0:T(8,128)(2,1)S(1)} %pad_maximum_fusion.1.refs_0_), channel_id=1, source_target_pairs={{0,3},{1,0},{2,1},{3,2},{4,7},{5,4},{6,5},{7,6},{8,11},{9,8},{10,9... | collective-permute-start | bytes 1179656 | tf_op jit(solution)/shard_map/ppermute | solution.py:18
  104.8 14.9 %collective-permute-start.16 = (bf16[96,2048]{1,0:T(8,128)(2,1)S(1)}, bf16[96,2048]{1,0:T(8,128)(2,1)S(1)}, u32[]{:S(2)}, u32[]{:S(2)}) collective-permute-start(bf16[96,2048]{1,0:T(8,128)(2,1)S(1)} %pad_maximum_fusion.1.refs_0_), channel_id=1, source_target_pairs={{0,1},{1,2},{2,3},{3,0},{4,5},{5,6},{6,7},{7,4},{8,9},{9,10},{10,1... | collective-permute-start | bytes 1179656 | tf_op jit(solution)/shard_map/ppermute | solution.py:18
  108.8 13.9 %collective-permute-start.19 = (bf16[96,2048]{1,0:T(8,128)(2,1)S(1)}, bf16[96,2048]{1,0:T(8,128)(2,1)S(1)}, u32[]{:S(2)}, u32[]{:S(2)}) collective-permute-start(bf16[96,2048]{1,0:T(8,128)(2,1)S(1)} %collective-permute-done.15.refs_1_), channel_id=1, source_target_pairs={{0,3},{1,0},{2,1},{3,2},{4,7},{5,4},{6,5},{7,6},{8,11},{9,8},{10,9... | collective-permute-start | bytes 1179656 | tf_op jit(solution)/shard_map/ppermute | solution.py:18
  111.9 16.2 %collective-permute-start.17 = (bf16[96,2048]{1,0:T(8,128)(2,1)S(1)}, bf16[96,2048]{1,0:T(8,128)(2,1)S(1)}, u32[]{:S(2)}, u32[]{:S(2)}) collective-permute-start(bf16[96,2048]{1,0:T(8,128)(2,1)S(1)} %collective-permute-done.15.refs_1_), channel_id=1, source_target_pairs={{0,1},{1,2},{2,3},{3,0},{4,5},{5,6},{6,7},{7,4},{8,9},{9,10},{10,1... | collective-permute-start | bytes 1179656 | tf_op jit(solution)/shard_map/ppermute | solution.py:18
  115.3 20.4 %collective-permute-start.21 = (bf16[48,2048]{1,0:T(8,128)(2,1)}, bf16[48,2048]{1,0:T(8,128)(2,1)S(1)}, u32[]{:S(2)}, u32[]{:S(2)}) collective-permute-start(bf16[48,2048]{1,0:T(8,128)(2,1)} %slice.44), channel_id=1, source_target_pairs={{0,3},{1,0},{2,1},{3,2},{4,7},{5,4},{6,5},{7,6},{8,11},{9,8},{10,9... | collective-permute-start | bytes 589832 | tf_op jit(solution)/shard_map/ppermute | solution.py:18
  120.3 15.5 %collective-permute-start.20 = (bf16[48,2048]{1,0:T(8,128)(2,1)}, bf16[48,2048]{1,0:T(8,128)(2,1)S(1)}, u32[]{:S(2)}, u32[]{:S(2)}) collective-permute-start(bf16[48,2048]{1,0:T(8,128)(2,1)} %slice.43), channel_id=1, source_target_pairs={{0,1},{1,2},{2,3},{3,0},{4,5},{5,6},{6,7},{7,4},{8,9},{9,10},{10,1... | collective-permute-start | bytes 589832 | tf_op jit(solution)/shard_map/ppermute | solution.py:18
  123.4 12.4 %collective-permute-start.23 = (bf16[48,2048]{1,0:T(8,128)(2,1)}, bf16[48,2048]{1,0:T(8,128)(2,1)S(1)}, u32[]{:S(2)}, u32[]{:S(2)}) collective-permute-start(bf16[48,2048]{1,0:T(8,128)(2,1)} %slice.46), channel_id=1, source_target_pairs={{0,3},{1,0},{2,1},{3,2},{4,7},{5,4},{6,5},{7,6},{8,11},{9,8},{10,9... | collective-permute-start | bytes 589832 | tf_op jit(solution)/shard_map/ppermute | solution.py:18
  128.8 9.1 %collective-permute-start.22 = (bf16[48,2048]{1,0:T(8,128)(2,1)}, bf16[48,2048]{1,0:T(8,128)(2,1)}, u32[]{:S(2)}, u32[]{:S(2)}) collective-permute-start(bf16[48,2048]{1,0:T(8,128)(2,1)} %slice.45), channel_id=1, source_target_pairs={{0,1},{1,2},{2,3},{3,0},{4,5},{5,6},{6,7},{7,4},{8,9},{9,10},{10,1... | collective-permute-start | bytes 589832 | tf_op jit(solution)/shard_map/ppermute | solution.py:18
  139.8 20.3 %collective-permute-start.29 = (bf16[256,256]{1,0:T(8,128)(2,1)S(1)}, bf16[256,256]{1,0:T(8,128)(2,1)S(1)}, u32[]{:S(2)}, u32[]{:S(2)}) collective-permute-start(bf16[256,256]{1,0:T(8,128)(2,1)S(1)} %get-tuple-element.57), channel_id=1, source_target_pairs={{0,288},{48,336},{96,0},{144,48},{192,96},{240,144},{288,192},{336... | collective-permute-start | bytes 393224 | tf_op jit(solution)/shard_map/ppermute | solution.py:18
  142.1 21.8 %collective-permute-start.30 = (bf16[256,256]{1,0:T(8,128)(2,1)S(1)}, bf16[256,256]{1,0:T(8,128)(2,1)S(1)}, u32[]{:S(2)}, u32[]{:S(2)}) collective-permute-start(bf16[256,256]{1,0:T(8,128)(2,1)S(1)} %get-tuple-element.58), channel_id=1, source_target_pairs={{0,192},{48,240},{96,288},{144,336},{192,0},{240,48},{288,96},{336... | collective-permute-start | bytes 393224 | tf_op jit(solution)/shard_map/ppermute | solution.py:18
  148.9 21.0 %collective-permute-start.31 = (bf16[256,256]{1,0:T(8,128)(2,1)S(1)}, bf16[256,256]{1,0:T(8,128)(2,1)S(1)}, u32[]{:S(2)}, u32[]{:S(2)}) collective-permute-start(bf16[256,256]{1,0:T(8,128)(2,1)S(1)} %get-tuple-element.59), channel_id=1, source_target_pairs={{0,96},{48,144},{96,192},{144,240},{192,288},{240,336},{288,0},{33... | collective-permute-start | bytes 393224 | tf_op jit(solution)/shard_map/ppermute | solution.py:18
  155.3 24.5 %collective-permute-start.24 = (f32[384,256]{1,0:T(8,128)S(1)}, f32[384,256]{1,0:T(8,128)S(1)}, u32[]{:S(2)}, u32[]{:S(2)}) collective-permute-start(f32[384,256]{1,0:T(8,128)S(1)} %get-tuple-element.52), channel_id=1, source_target_pairs={{0,24},{24,0},{1,25},{25,1},{2,26},{26,2},{3,27},{27,3},{4,28},{28... | collective-permute-start | bytes 1179656 | tf_op jit(solution)/shard_map/ppermute | solution.py:18
  157.3 25.1 %collective-permute-start.26 = (bf16[256,256]{1,0:T(8,128)(2,1)S(1)}, bf16[256,256]{1,0:T(8,128)(2,1)S(1)}, u32[]{:S(2)}, u32[]{:S(2)}) collective-permute-start(bf16[256,256]{1,0:T(8,128)(2,1)S(1)} %get-tuple-element.53), channel_id=1, source_target_pairs={{0,288},{48,336},{96,0},{144,48},{192,96},{240,144},{288,192},{336... | collective-permute-start | bytes 393224 | tf_op jit(solution)/shard_map/ppermute | solution.py:18
  160.1 22.3 %collective-permute-start.27 = (bf16[256,256]{1,0:T(8,128)(2,1)S(1)}, bf16[256,256]{1,0:T(8,128)(2,1)S(1)}, u32[]{:S(2)}, u32[]{:S(2)}) collective-permute-start(bf16[256,256]{1,0:T(8,128)(2,1)S(1)} %get-tuple-element.54), channel_id=1, source_target_pairs={{0,192},{48,240},{96,288},{144,336},{192,0},{240,48},{288,96},{336... | collective-permute-start | bytes 393224 | tf_op jit(solution)/shard_map/ppermute | solution.py:18
  163.9 18.5 %collective-permute-start.28 = (bf16[256,256]{1,0:T(8,128)(2,1)S(1)}, bf16[256,256]{1,0:T(8,128)(2,1)S(1)}, u32[]{:S(2)}, u32[]{:S(2)}) collective-permute-start(bf16[256,256]{1,0:T(8,128)(2,1)S(1)} %get-tuple-element.55), channel_id=1, source_target_pairs={{0,96},{48,144},{96,192},{144,240},{192,288},{240,336},{288,0},{33... | collective-permute-start | bytes 393224 | tf_op jit(solution)/shard_map/ppermute | solution.py:18
  170.0 13.5 %collective-permute-start.32 = (bf16[256,256]{1,0:T(8,128)(2,1)S(1)}, bf16[256,256]{1,0:T(8,128)(2,1)S(1)}, u32[]{:S(2)}, u32[]{:S(2)}) collective-permute-start(bf16[256,256]{1,0:T(8,128)(2,1)S(1)} %add_convert_fusion.2), channel_id=1, source_target_pairs={{0,384},{384,0},{1,385},{385,1},{2,386},{386,2},{3,387},{387,3},{4... | collective-permute-start | bytes 393224 | tf_op jit(solution)/shard_map/ppermute | solution.py:18
  179.9 8.1 %collective-permute-start.25 = (f32[192,256]{1,0:T(8,128)S(1)}, f32[192,256]{1,0:T(8,128)S(1)}, u32[]{:S(2)}, u32[]{:S(2)}) collective-permute-start(f32[192,256]{1,0:T(8,128)S(1)} %slice.49), channel_id=1, source_target_pairs={{0,48},{48,0},{96,144},{144,96},{192,240},{240,192},{288,336},{336... | collective-permute-start | bytes 589832 | tf_op jit(solution)/shard_map/ppermute | solution.py:18
  (9 other events, 286.1 us)

commit v3 on v2

--- a/solution.py
+++ b/solution.py
@@ -10,7 +10,7 @@
 ZH, Y, CORE, ZL, X = 2, 8, 2, 6, 4
 BF, F32 = jnp.bfloat16, jnp.float32
 D = 8192
-PIECES = 10
+PIECES = 8
 VMEM = 24 * 1024 * 1024
 
 
@@ -256,6 +256,23 @@
     )(*pieces)
 
 
+def tie_kernel(value, late, out):
+    out[...] = value[...]
+
+
+def tie(value, late):
+    whole = pl.BlockSpec(memory_space=pltpu.VMEM)
+    return pl.pallas_call(
+        tie_kernel,
+        out_shape=jax.ShapeDtypeStruct(value.shape, value.dtype),
+        in_specs=[whole] * 2,
+        out_specs=whole,
+        compiler_params=pltpu.CompilerParams(vmem_limit_bytes=VMEM),
+        cost_estimate=pl.CostEstimate(flops=0, bytes_accessed=768 * 1024, transcendentals=0),
+        name="tie",
+    )(value, late)
+
+
 def per_device(attention, out_proj, residual, gain, grad_normed, grad_residual):
     x, zl, y = lax.axis_index("x"), lax.axis_index("zl"), lax.axis_index("y")
     core, zh = lax.axis_index("core"), lax.axis_index("zh")
@@ -299,19 +316,20 @@
     lines = (line, to_q(line))
     ones = [to_x(part, -1) for part in lines]
     threes = [to_x(part, -3) for part in lines]
-    twos = [(to_x(one[:48], -1), to_x(three[48:], -3)) for one, three in zip(ones, threes)]
-    pieces = [*lines, *ones, *twos[0], *twos[1], *threes]
+    ones[0] = tie(ones[0], threes[0])
+    twos = (to_x(ones[0], -1), to_x(threes[1], -3))
+    pieces = [*lines, *ones, *twos, *threes]
 
     first = jnp.stack([1 - zh, zh]).astype(jnp.int32) * 16 + (v * 2 + core).astype(jnp.int32)
-    early = back(first, [*lines, *ones, *threes], out_proj, blocks)
+    early = back(first, [*lines, *ones, twos[0], *threes], out_proj, blocks)
     parts = term_parts(blocks, turned, pieces, early)
     got = [[to_u(parts[k * 4 + r], r) for r in (1, 2, 3)] for k in range(2)]
     sums = [parts[k * 4] + sum(value.astype(F32) for value in got[k]) for k in range(2)]
     passing = sums[0].astype(BF)
     grad_out_proj = sums[1] + to_zh(passing).astype(F32)
 
-    late = back(first, [*twos[0], *twos[1]], out_proj, parts[4])
-    stay, go = apart([early[:384], late, early[384:]])
+    late = back(first, twos[1:], out_proj, parts[4])
+    stay, go = apart([early[:480], late, early[480:]])
     stay = stay + to_core(go)
     ours = stay[:192] + to_v(stay[192:])
     grad_attention = lax.dot_general(

time: 190 us -> 192 us (1.011)
  the two profiles are of different devices: /device:TPU:16 before, /device:TPU:144 now
where the time goes in v3:
time: 192 us; the launch traced here: 191 us
  starting transfers between devices  119 us (62%)
  waiting for transfers between devices  49.1 us (26%)
  Pallas kernels  12.5 us (7%)
  local copies, waits for them, and re-layouts  5.42 us (3%)
  other arithmetic  3.16 us (2%)
    ppermute x31, starting transfers between devices, shift(): return lax.ppermute(value, axis, [(i, move(i)) for i in range(size)])  119 us
    ppermute x31, waiting for transfers between devices, shift(): return lax.ppermute(value, axis, [(i, move(i)) for i in range(size)])  49.1 us
    pallas_call x2, Pallas kernels, back(): pl.pallas_call(functools.partial(back_kernel, len(pieces)), out_shape=jax...  5.2 us
    unnamed x17, local copies, waits for them, and re-layouts  5.08 us
  transfers between devices with their start and end apart: 31, of which 19 were waited for; matrix products, arithmetic and copies ran while one was open for 2% of the time, Pallas kernels for 3%

profile of v3, /device:TPU:144, one launch (start us, length us, event | category | flops | bytes accessed | tf_op | source)
XLA Modules:
  0.0 191.3 jit_solution(17509705680052470099)
XLA Ops:
  4.0 2.7 %products.1 = (bf16[24,8192]{1,0:T(8,128)(2,1)S(1)}, bf16[24,8192]{1,0:T(8,128)(2,1)S(1)}, bf16[24,8192]{1,0:T(8,128)(2,1)S(1)}, bf16[24,8192]{1,0:T(8,128)(2,1)...) custom-call(bf16[192,256]{1,0:T(8,128)(2,1)S(1)} %convolution_conver, ...), custom_call_target="tpu_custom_call" | custom-call | flops 805306368 | bytes 7340032 | tf_op jit(solution)/shard_map/products/pallas_call | solution.py:69
  6.7 3.5 %collective-permute-start.4 = (bf16[24,8192]{1,0:T(8,128)(2,1)S(1)}, bf16[24,8192]{1,0:T(8,128)(2,1)S(1)}, u32[]{:S(2)}, u32[]{:S(2)}) collective-permute-start(bf16[24,8192]{1,0:T(8,128)(2,1)S(1)} %get-tuple-element.41), channel_id=1, source_target_pairs={{0,1},{1,2},{2,3},{3,0},{4,5},{5,6},{6,7},{7,4},{8,9},{9,10},{10,1... | collective-permute-start | bytes 1179656 | tf_op jit(solution)/shard_map/ppermute | solution.py:18
  10.2 3.7 %collective-permute-start = (bf16[24,8192]{1,0:T(8,128)(2,1)S(1)}, bf16[24,8192]{1,0:T(8,128)(2,1)S(1)}, u32[]{:S(2)}, u32[]{:S(2)}) collective-permute-start(bf16[24,8192]{1,0:T(8,128)(2,1)S(1)} %get-tuple-element.34), channel_id=1, source_target_pairs={{0,3},{1,0},{2,1},{3,2},{4,7},{5,4},{6,5},{7,6},{8,11},{9,8},{10,9... | collective-permute-start | bytes 1179656 | tf_op jit(solution)/shard_map/ppermute | solution.py:18
  13.9 3.5 %collective-permute-start.3 = (bf16[24,8192]{1,0:T(8,128)(2,1)S(1)}, bf16[24,8192]{1,0:T(8,128)(2,1)S(1)}, u32[]{:S(2)}, u32[]{:S(2)}) collective-permute-start(bf16[24,8192]{1,0:T(8,128)(2,1)S(1)} %get-tuple-element.39), channel_id=1, source_target_pairs={{0,3},{1,0},{2,1},{3,2},{4,7},{5,4},{6,5},{7,6},{8,11},{9,8},{10,9... | collective-permute-start | bytes 1179656 | tf_op jit(solution)/shard_map/ppermute | solution.py:18
  17.4 3.4 %collective-permute-done.4 = bf16[24,8192]{1,0:T(8,128)(2,1)S(1)} collective-permute-done((bf16[24,8192]{1,0:T(8,128)(2,1)S(1)}, bf16[24,8192]{1,0:T(8,128)(2,1)S(1)}, u32[]{:S(2)}, u32[]{:S(2)}) %collective-permute-start.4) | collective-permute-done | bytes 393248 | tf_op jit(solution)/shard_map/ppermute | solution.py:18
  24.5 4.9 %collective-permute-start.1 = (bf16[24,8192]{1,0:T(8,128)(2,1)S(1)}, bf16[24,8192]{1,0:T(8,128)(2,1)S(1)}, u32[]{:S(2)}, u32[]{:S(2)}) collective-permute-start(bf16[24,8192]{1,0:T(8,128)(2,1)S(1)} %get-tuple-element.36), channel_id=1, source_target_pairs={{0,3},{1,0},{2,1},{3,2},{4,7},{5,4},{6,5},{7,6},{8,11},{9,8},{10,9... | collective-permute-start | bytes 1179656 | tf_op jit(solution)/shard_map/ppermute | solution.py:18
  32.6 2.9 %collective-permute-done.5 = bf16[24,8192]{1,0:T(8,128)(2,1)S(1)} collective-permute-done((bf16[24,8192]{1,0:T(8,128)(2,1)S(1)}, bf16[24,8192]{1,0:T(8,128)(2,1)S(1)}, u32[]{:S(2)}, u32[]{:S(2)}) %collective-permute-start.5) | collective-permute-done | bytes 393248 | tf_op jit(solution)/shard_map/ppermute | solution.py:18
  36.3 4.3 %collective-permute-start.6 = (bf16[24,8192]{1,0:T(8,128)(2,1)}, bf16[24,8192]{1,0:T(8,128)(2,1)S(1)}, u32[]{:S(2)}, u32[]{:S(2)}) collective-permute-start(bf16[24,8192]{1,0:T(8,128)(2,1)} %add_convert_fusion), channel_id=1, source_target_pairs={{0,4},{4,0},{8,12},{12,8},{16,20},{20,16},{1,5},{5,1},{9,13},{13,9... | collective-permute-start | bytes 1179656 | tf_op jit(solution)/shard_map/ppermute | solution.py:18
  43.8 3.5 %collective-permute-start.10 = (bf16[24,16,256]{2,1,0:T(8,128)(2,1)S(1)}, bf16[24,16,256]{2,1,0:T(8,128)(2,1)}, u32[]{:S(2)}, u32[]{:S(2)}) collective-permute-start(bf16[24,16,256]{2,1,0:T(8,128)(2,1)S(1)} %pad_maximum_fusion.2), channel_id=1, source_target_pairs={{0,48},{48,0},{96,144},{144,96},{192,240},{240,192},{288,336},{336... | collective-permute-start | bytes 589832 | tf_op jit(solution)/shard_map/ppermute | solution.py:18
  49.7 7.3 %collective-permute-start.8 = (bf16[8,8192]{1,0:T(8,128)(2,1)S(1)}, bf16[8,8192]{1,0:T(8,128)(2,1)S(1)}, u32[]{:S(2)}, u32[]{:S(2)}) collective-permute-start(bf16[8,8192]{1,0:T(8,128)(2,1)S(1)} %get-tuple-element.44), channel_id=1, source_target_pairs={{0,8},{4,12},{8,16},{12,20},{16,0},{20,4},{1,9},{5,13},{9,17},{13,... | collective-permute-start | bytes 393224 | tf_op jit(solution)/shard_map/ppermute | solution.py:18
  58.3 2.6 %collective-permute-done.7.second = bf16[8,8192]{1,0:T(8,128)(2,1)S(1)} collective-permute-done((bf16[8,8192]{1,0:T(8,128)(2,1)S(1)}, bf16[8,8192]{1,0:T(8,128)(2,1)S(1)}, u32[]{:S(2)}, u32[]{:S(2)}) %collective-permute-start.7) | collective-permute-done | bytes 131104 | tf_op jit(solution)/shard_map/ppermute | solution.py:18
  60.9 2.8 %collective-permute-done.8.third = bf16[8,8192]{1,0:T(8,128)(2,1)S(1)} collective-permute-done((bf16[8,8192]{1,0:T(8,128)(2,1)S(1)}, bf16[8,8192]{1,0:T(8,128)(2,1)S(1)}, u32[]{:S(2)}, u32[]{:S(2)}) %collective-permute-start.8) | collective-permute-done | bytes 131104 | tf_op jit(solution)/shard_map/ppermute | solution.py:18
  70.8 3.8 %collective-permute-done.12 = bf16[16,2048]{1,0:T(8,128)(2,1)S(1)} collective-permute-done((bf16[16,2048]{1,0:T(8,128)(2,1)S(1)}, bf16[16,2048]{1,0:T(8,128)(2,1)S(1)}, u32[]{:S(2)}, u32[]{:S(2)}) %collective-permute-start.12) | collective-permute-done | bytes 65568 | tf_op jit(solution)/shard_map/ppermute | solution.py:18
  74.6 8.8 %collective-permute-start.14 = (bf16[32,2048]{1,0:T(8,128)(2,1)S(1)}, bf16[32,2048]{1,0:T(8,128)(2,1)S(1)}, u32[]{:S(2)}, u32[]{:S(2)}) collective-permute-start(bf16[32,2048]{1,0:T(8,128)(2,1)S(1)} %pad_maximum_fusion.3), channel_id=1, source_target_pairs={{0,16},{4,20},{8,0},{12,4},{16,8},{20,12},{1,17},{5,21},{9,1},{13,... | collective-permute-start | bytes 393224 | tf_op jit(solution)/shard_map/ppermute | solution.py:18
  85.3 2.5 %collective-permute-done.14 = bf16[32,2048]{1,0:T(8,128)(2,1)S(1)} collective-permute-done((bf16[32,2048]{1,0:T(8,128)(2,1)S(1)}, bf16[32,2048]{1,0:T(8,128)(2,1)S(1)}, u32[]{:S(2)}, u32[]{:S(2)}) %collective-permute-start.14) | collective-permute-done | bytes 131104 | tf_op jit(solution)/shard_map/ppermute | solution.py:18
  87.9 3.4 %collective-permute-done.13 = bf16[32,2048]{1,0:T(8,128)(2,1)S(1)} collective-permute-done((bf16[32,2048]{1,0:T(8,128)(2,1)S(1)}, bf16[32,2048]{1,0:T(8,128)(2,1)S(1)}, u32[]{:S(2)}, u32[]{:S(2)}) %collective-permute-start.13) | collective-permute-done | bytes 131104 | tf_op jit(solution)/shard_map/ppermute | solution.py:18
  91.3 6.9 %collective-permute-start.15 = (bf16[96,2048]{1,0:T(8,128)(2,1)S(1)}, bf16[96,2048]{1,0:T(8,128)(2,1)S(1)}, u32[]{:S(2)}, u32[]{:S(2)}) collective-permute-start(bf16[96,2048]{1,0:T(8,128)(2,1)S(1)} %pad_maximum_fusion.1.refs_0_), channel_id=1, source_target_pairs={{0,4},{4,0},{8,12},{12,8},{16,20},{20,16},{1,5},{5,1},{9,13},{13,9... | collective-permute-start | bytes 1179656 | tf_op jit(solution)/shard_map/ppermute | solution.py:18
  98.2 2.8 %collective-permute-start.17 = (bf16[96,2048]{1,0:T(8,128)(2,1)S(1)}, bf16[96,2048]{1,0:T(8,128)(2,1)S(1)}, u32[]{:S(2)}, u32[]{:S(2)}) collective-permute-start(bf16[96,2048]{1,0:T(8,128)(2,1)S(1)} %pad_maximum_fusion.1.refs_0_), channel_id=1, source_target_pairs={{0,3},{1,0},{2,1},{3,2},{4,7},{5,4},{6,5},{7,6},{8,11},{9,8},{10,9... | collective-permute-start | bytes 1179656 | tf_op jit(solution)/shard_map/ppermute | solution.py:18
  101.1 3.0 %collective-permute-start.16 = (bf16[96,2048]{1,0:T(8,128)(2,1)S(1)}, bf16[96,2048]{1,0:T(8,128)(2,1)S(1)}, u32[]{:S(2)}, u32[]{:S(2)}) collective-permute-start(bf16[96,2048]{1,0:T(8,128)(2,1)S(1)} %pad_maximum_fusion.1.refs_0_), channel_id=1, source_target_pairs={{0,1},{1,2},{2,3},{3,0},{4,5},{5,6},{6,7},{7,4},{8,9},{9,10},{10,1... | collective-permute-start | bytes 1179656 | tf_op jit(solution)/shard_map/ppermute | solution.py:18
  106.3 2.8 %collective-permute-start.20 = (bf16[96,2048]{1,0:T(8,128)(2,1)S(1)}, bf16[96,2048]{1,0:T(8,128)(2,1)S(1)}, u32[]{:S(2)}, u32[]{:S(2)}) collective-permute-start(bf16[96,2048]{1,0:T(8,128)(2,1)S(1)} %collective-permute-done.15.refs_1_), channel_id=1, source_target_pairs={{0,3},{1,0},{2,1},{3,2},{4,7},{5,4},{6,5},{7,6},{8,11},{9,8},{10,9... | collective-permute-start | bytes 1179656 | tf_op jit(solution)/shard_map/ppermute | solution.py:18
  110.3 3.1 %collective-permute-done.16.value = bf16[96,2048]{1,0:T(8,128)(2,1)S(1)} collective-permute-done((bf16[96,2048]{1,0:T(8,128)(2,1)S(1)}, bf16[96,2048]{1,0:T(8,128)(2,1)S(1)}, u32[]{:S(2)}, u32[]{:S(2)}) %collective-permute-start.16) | collective-permute-done | bytes 393248 | tf_op jit(solution)/shard_map/ppermute | solution.py:18
  118.1 4.4 %collective-permute-start.21 = (bf16[96,2048]{1,0:T(8,128)(2,1)S(1)}, bf16[96,2048]{1,0:T(8,128)(2,1)}, u32[]{:S(2)}, u32[]{:S(2)}) collective-permute-start(bf16[96,2048]{1,0:T(8,128)(2,1)S(1)} %collective-permute-done.20.refs_6_.refs_7_), channel_id=1, source_target_pairs={{0,3},{1,0},{2,1},{3,2},{4,7},{5,4},{6,5},{7,6},{8,11},{9,8},{10,9... | collective-permute-start | bytes 1179656 | tf_op jit(solution)/shard_map/ppermute | solution.py:18
  122.6 6.0 %collective-permute-done.19.refs_4_ = bf16[96,2048]{1,0:T(8,128)(2,1)S(1)} collective-permute-done((bf16[96,2048]{1,0:T(8,128)(2,1)S(1)}, bf16[96,2048]{1,0:T(8,128)(2,1)S(1)}, u32[]{:S(2)}, u32[]{:S(2)}) %collective-permute-start.19) | collective-permute-done | bytes 393248 | tf_op jit(solution)/shard_map/ppermute | solution.py:18
  128.6 4.7 %collective-permute-done.18.refs_3_ = bf16[96,2048]{1,0:T(8,128)(2,1)S(1)} collective-permute-done((bf16[96,2048]{1,0:T(8,128)(2,1)S(1)}, bf16[96,2048]{1,0:T(8,128)(2,1)S(1)}, u32[]{:S(2)}, u32[]{:S(2)}) %collective-permute-start.18) | collective-permute-done | bytes 393248 | tf_op jit(solution)/shard_map/ppermute | solution.py:18
  135.5 3.0 %back.2.refs_8_ = f32[672,256]{1,0:T(8,128)S(1)} custom-call(s32[2]{0:T(128)S(1)} %fusion.18.first, bf16[96,2048]{1,0:T(8,128)(2,1)S(1)} %pad_maximum_fusion.1.refs_0_, bf16[96,2048]{1,0:T(8,128)(2,1)S(1)} %collective-permute-done.15.refs_1_, bf16[96,2048]{1,0:T(8,128)(2,1)S(1)} %tie.1.refs_2_, bf16[96,2048]{1,0:T(8,128)(2,1)S(1)} %collective-permute-done.18.refs_3_, ...), custom_call_target="tpu_custom_call" | custom-call | flops 704643072 | bytes 3145728 | tf_op jit(solution)/shard_map/back/pallas_call | solution.py:218
  143.0 6.8 %collective-permute-start.28 = (bf16[256,256]{1,0:T(8,128)(2,1)S(1)}, bf16[256,256]{1,0:T(8,128)(2,1)S(1)}, u32[]{:S(2)}, u32[]{:S(2)}) collective-permute-start(bf16[256,256]{1,0:T(8,128)(2,1)S(1)} %get-tuple-element.58), channel_id=1, source_target_pairs={{0,192},{48,240},{96,288},{144,336},{192,0},{240,48},{288,96},{336... | collective-permute-start | bytes 393224 | tf_op jit(solution)/shard_map/ppermute | solution.py:18
  149.8 3.9 %collective-permute-start.29 = (bf16[256,256]{1,0:T(8,128)(2,1)S(1)}, bf16[256,256]{1,0:T(8,128)(2,1)S(1)}, u32[]{:S(2)}, u32[]{:S(2)}) collective-permute-start(bf16[256,256]{1,0:T(8,128)(2,1)S(1)} %get-tuple-element.59), channel_id=1, source_target_pairs={{0,96},{48,144},{96,192},{144,240},{192,288},{240,336},{288,0},{33... | collective-permute-start | bytes 393224 | tf_op jit(solution)/shard_map/ppermute | solution.py:18
  158.0 2.8 %collective-permute-start.24 = (bf16[256,256]{1,0:T(8,128)(2,1)S(1)}, bf16[256,256]{1,0:T(8,128)(2,1)S(1)}, u32[]{:S(2)}, u32[]{:S(2)}) collective-permute-start(bf16[256,256]{1,0:T(8,128)(2,1)S(1)} %get-tuple-element.53), channel_id=1, source_target_pairs={{0,288},{48,336},{96,0},{144,48},{192,96},{240,144},{288,192},{336... | collective-permute-start | bytes 393224 | tf_op jit(solution)/shard_map/ppermute | solution.py:18
  160.9 3.8 %collective-permute-start.25 = (bf16[256,256]{1,0:T(8,128)(2,1)S(1)}, bf16[256,256]{1,0:T(8,128)(2,1)S(1)}, u32[]{:S(2)}, u32[]{:S(2)}) collective-permute-start(bf16[256,256]{1,0:T(8,128)(2,1)S(1)} %get-tuple-element.54), channel_id=1, source_target_pairs={{0,192},{48,240},{96,288},{144,336},{192,0},{240,48},{288,96},{336... | collective-permute-start | bytes 393224 | tf_op jit(solution)/shard_map/ppermute | solution.py:18
  164.7 6.0 %collective-permute-start.26 = (bf16[256,256]{1,0:T(8,128)(2,1)S(1)}, bf16[256,256]{1,0:T(8,128)(2,1)S(1)}, u32[]{:S(2)}, u32[]{:S(2)}) collective-permute-start(bf16[256,256]{1,0:T(8,128)(2,1)S(1)} %get-tuple-element.55), channel_id=1, source_target_pairs={{0,96},{48,144},{96,192},{144,240},{192,288},{240,336},{288,0},{33... | collective-permute-start | bytes 393224 | tf_op jit(solution)/shard_map/ppermute | solution.py:18
  170.9 11.4 %collective-permute-start.30 = (bf16[256,256]{1,0:T(8,128)(2,1)S(1)}, bf16[256,256]{1,0:T(8,128)(2,1)S(1)}, u32[]{:S(2)}, u32[]{:S(2)}) collective-permute-start(bf16[256,256]{1,0:T(8,128)(2,1)S(1)} %add_convert_fusion.2), channel_id=1, source_target_pairs={{0,384},{384,0},{1,385},{385,1},{2,386},{386,2},{3,387},{387,3},{4... | collective-permute-start | bytes 393224 | tf_op jit(solution)/shard_map/ppermute | solution.py:18
  187.3 3.1 %collective-permute-done.23 = f32[192,256]{1,0:T(8,128)S(1)} collective-permute-done((f32[192,256]{1,0:T(8,128)S(1)}, f32[192,256]{1,0:T(8,128)S(1)}, u32[]{:S(2)}, u32[]{:S(2)}) %collective-permute-start.23) | collective-permute-done | bytes 196640 | tf_op jit(solution)/shard_map/ppermute | solution.py:18
  (79 shorter events, 52.0 us)
Async XLA Ops:
  6.6 57.0 %copy-start.4 = (bf16[8,8192]{1,0:T(8,128)(2,1)S(1)}, bf16[8,8192]{1,0:T(8,128)(2,1)}, u32[]{:S(2)}) copy-start(bf16[8,8192]{1,0:T(8,128)(2,1)} %refs_0_.1) | copy-start | bytes 393220
  6.7 14.1 %collective-permute-start.4 = (bf16[24,8192]{1,0:T(8,128)(2,1)S(1)}, bf16[24,8192]{1,0:T(8,128)(2,1)S(1)}, u32[]{:S(2)}, u32[]{:S(2)}) collective-permute-start(bf16[24,8192]{1,0:T(8,128)(2,1)S(1)} %get-tuple-element.41), channel_id=1, source_target_pairs={{0,1},{1,2},{2,3},{3,0},{4,5},{5,6},{6,7},{7,4},{8,9},{9,10},{10,1... | collective-permute-start | bytes 1179656 | tf_op jit(solution)/shard_map/ppermute | solution.py:18
  10.2 13.9 %collective-permute-start = (bf16[24,8192]{1,0:T(8,128)(2,1)S(1)}, bf16[24,8192]{1,0:T(8,128)(2,1)S(1)}, u32[]{:S(2)}, u32[]{:S(2)}) collective-permute-start(bf16[24,8192]{1,0:T(8,128)(2,1)S(1)} %get-tuple-element.34), channel_id=1, source_target_pairs={{0,3},{1,0},{2,1},{3,2},{4,7},{5,4},{6,5},{7,6},{8,11},{9,8},{10,9... | collective-permute-start | bytes 1179656 | tf_op jit(solution)/shard_map/ppermute | solution.py:18
  13.9 18.7 %collective-permute-start.3 = (bf16[24,8192]{1,0:T(8,128)(2,1)S(1)}, bf16[24,8192]{1,0:T(8,128)(2,1)S(1)}, u32[]{:S(2)}, u32[]{:S(2)}) collective-permute-start(bf16[24,8192]{1,0:T(8,128)(2,1)S(1)} %get-tuple-element.39), channel_id=1, source_target_pairs={{0,3},{1,0},{2,1},{3,2},{4,7},{5,4},{6,5},{7,6},{8,11},{9,8},{10,9... | collective-permute-start | bytes 1179656 | tf_op jit(solution)/shard_map/ppermute | solution.py:18
  20.9 14.6 %collective-permute-start.5 = (bf16[24,8192]{1,0:T(8,128)(2,1)S(1)}, bf16[24,8192]{1,0:T(8,128)(2,1)S(1)}, u32[]{:S(2)}, u32[]{:S(2)}) collective-permute-start(bf16[24,8192]{1,0:T(8,128)(2,1)S(1)} %add_convert_fusion.1), channel_id=1, source_target_pairs={{0,1},{1,2},{2,3},{3,0},{4,5},{5,6},{6,7},{7,4},{8,9},{9,10},{10,1... | collective-permute-start | bytes 1179656 | tf_op jit(solution)/shard_map/ppermute | solution.py:18
  24.5 22.8 %collective-permute-start.1 = (bf16[24,8192]{1,0:T(8,128)(2,1)S(1)}, bf16[24,8192]{1,0:T(8,128)(2,1)S(1)}, u32[]{:S(2)}, u32[]{:S(2)}) collective-permute-start(bf16[24,8192]{1,0:T(8,128)(2,1)S(1)} %get-tuple-element.36), channel_id=1, source_target_pairs={{0,3},{1,0},{2,1},{3,2},{4,7},{5,4},{6,5},{7,6},{8,11},{9,8},{10,9... | collective-permute-start | bytes 1179656 | tf_op jit(solution)/shard_map/ppermute | solution.py:18
  29.4 18.0 %collective-permute-start.2 = (bf16[24,8192]{1,0:T(8,128)(2,1)S(1)}, bf16[24,8192]{1,0:T(8,128)(2,1)S(1)}, u32[]{:S(2)}, u32[]{:S(2)}) collective-permute-start(bf16[24,8192]{1,0:T(8,128)(2,1)S(1)} %get-tuple-element.37), channel_id=1, source_target_pairs={{0,1},{1,2},{2,3},{3,0},{4,5},{5,6},{6,7},{7,4},{8,9},{9,10},{10,1... | collective-permute-start | bytes 1179656 | tf_op jit(solution)/shard_map/ppermute | solution.py:18
  36.3 11.0 %collective-permute-start.6 = (bf16[24,8192]{1,0:T(8,128)(2,1)}, bf16[24,8192]{1,0:T(8,128)(2,1)S(1)}, u32[]{:S(2)}, u32[]{:S(2)}) collective-permute-start(bf16[24,8192]{1,0:T(8,128)(2,1)} %add_convert_fusion), channel_id=1, source_target_pairs={{0,4},{4,0},{8,12},{12,8},{16,20},{20,16},{1,5},{5,1},{9,13},{13,9... | collective-permute-start | bytes 1179656 | tf_op jit(solution)/shard_map/ppermute | solution.py:18
  40.6 3.2 %collective-permute-start.9 = (bf16[192,256]{1,0:T(8,128)(2,1)S(1)}, bf16[192,256]{1,0:T(8,128)(2,1)S(1)}, u32[]{:S(2)}, u32[]{:S(2)}) collective-permute-start(bf16[192,256]{1,0:T(8,128)(2,1)S(1)} %get-tuple-element.45), channel_id=1, source_target_pairs={{0,24},{24,0},{1,25},{25,1},{2,26},{26,2},{3,27},{27,3},{4,28},{28... | collective-permute-start | bytes 294920 | tf_op jit(solution)/shard_map/ppermute | solution.py:18
  43.8 13.3 %collective-permute-start.10 = (bf16[24,16,256]{2,1,0:T(8,128)(2,1)S(1)}, bf16[24,16,256]{2,1,0:T(8,128)(2,1)}, u32[]{:S(2)}, u32[]{:S(2)}) collective-permute-start(bf16[24,16,256]{2,1,0:T(8,128)(2,1)S(1)} %pad_maximum_fusion.2), channel_id=1, source_target_pairs={{0,48},{48,0},{96,144},{144,96},{192,240},{240,192},{288,336},{336... | collective-permute-start | bytes 589832 | tf_op jit(solution)/shard_map/ppermute | solution.py:18
  47.8 13.1 %collective-permute-start.7 = (bf16[8,8192]{1,0:T(8,128)(2,1)S(1)}, bf16[8,8192]{1,0:T(8,128)(2,1)S(1)}, u32[]{:S(2)}, u32[]{:S(2)}) collective-permute-start(bf16[8,8192]{1,0:T(8,128)(2,1)S(1)} %get-tuple-element.43), channel_id=1, source_target_pairs={{0,16},{4,20},{8,0},{12,4},{16,8},{20,12},{1,17},{5,21},{9,1},{13,... | collective-permute-start | bytes 393224 | tf_op jit(solution)/shard_map/ppermute | solution.py:18
  49.7 13.9 %collective-permute-start.8 = (bf16[8,8192]{1,0:T(8,128)(2,1)S(1)}, bf16[8,8192]{1,0:T(8,128)(2,1)S(1)}, u32[]{:S(2)}, u32[]{:S(2)}) collective-permute-start(bf16[8,8192]{1,0:T(8,128)(2,1)S(1)} %get-tuple-element.44), channel_id=1, source_target_pairs={{0,8},{4,12},{8,16},{12,20},{16,0},{20,4},{1,9},{5,13},{9,17},{13,... | collective-permute-start | bytes 393224 | tf_op jit(solution)/shard_map/ppermute | solution.py:18
  65.3 3.1 %collective-permute-start.11 = (bf16[8,4096]{1,0:T(8,128)(2,1)S(1)}, bf16[8,4096]{1,0:T(8,128)(2,1)S(1)}, u32[]{:S(2)}, u32[]{:S(2)}) collective-permute-start(bf16[8,4096]{1,0:T(8,128)(2,1)S(1)} %get-tuple-element.49), channel_id=1, source_target_pairs={{0,24},{24,0},{1,25},{25,1},{2,26},{26,2},{3,27},{27,3},{4,28},{28... | collective-permute-start | bytes 196616 | tf_op jit(solution)/shard_map/ppermute | solution.py:18
  68.5 6.2 %collective-permute-start.12 = (bf16[16,2048]{1,0:T(8,128)(2,1)S(1)}, bf16[16,2048]{1,0:T(8,128)(2,1)S(1)}, u32[]{:S(2)}, u32[]{:S(2)}) collective-permute-start(bf16[16,2048]{1,0:T(8,128)(2,1)S(1)} %get-tuple-element.61), channel_id=1, source_target_pairs={{0,48},{48,0},{96,144},{144,96},{192,240},{240,192},{288,336},{336... | collective-permute-start | bytes 196616 | tf_op jit(solution)/shard_map/ppermute | solution.py:18
  74.6 13.2 %collective-permute-start.14 = (bf16[32,2048]{1,0:T(8,128)(2,1)S(1)}, bf16[32,2048]{1,0:T(8,128)(2,1)S(1)}, u32[]{:S(2)}, u32[]{:S(2)}) collective-permute-start(bf16[32,2048]{1,0:T(8,128)(2,1)S(1)} %pad_maximum_fusion.3), channel_id=1, source_target_pairs={{0,16},{4,20},{8,0},{12,4},{16,8},{20,12},{1,17},{5,21},{9,1},{13,... | collective-permute-start | bytes 393224 | tf_op jit(solution)/shard_map/ppermute | solution.py:18
  83.4 7.9 %collective-permute-start.13 = (bf16[32,2048]{1,0:T(8,128)(2,1)S(1)}, bf16[32,2048]{1,0:T(8,128)(2,1)S(1)}, u32[]{:S(2)}, u32[]{:S(2)}) collective-permute-start(bf16[32,2048]{1,0:T(8,128)(2,1)S(1)} %pad_maximum_fusion.3), channel_id=1, source_target_pairs={{0,8},{4,12},{8,16},{12,20},{16,0},{20,4},{1,9},{5,13},{9,17},{13,... | collective-permute-start | bytes 393224 | tf_op jit(solution)/shard_map/ppermute | solution.py:18
  91.3 15.0 %collective-permute-start.15 = (bf16[96,2048]{1,0:T(8,128)(2,1)S(1)}, bf16[96,2048]{1,0:T(8,128)(2,1)S(1)}, u32[]{:S(2)}, u32[]{:S(2)}) collective-permute-start(bf16[96,2048]{1,0:T(8,128)(2,1)S(1)} %pad_maximum_fusion.1.refs_0_), channel_id=1, source_target_pairs={{0,4},{4,0},{8,12},{12,8},{16,20},{20,16},{1,5},{5,1},{9,13},{13,9... | collective-permute-start | bytes 1179656 | tf_op jit(solution)/shard_map/ppermute | solution.py:18
  98.2 12.1 %collective-permute-start.17 = (bf16[96,2048]{1,0:T(8,128)(2,1)S(1)}, bf16[96,2048]{1,0:T(8,128)(2,1)S(1)}, u32[]{:S(2)}, u32[]{:S(2)}) collective-permute-start(bf16[96,2048]{1,0:T(8,128)(2,1)S(1)} %pad_maximum_fusion.1.refs_0_), channel_id=1, source_target_pairs={{0,3},{1,0},{2,1},{3,2},{4,7},{5,4},{6,5},{7,6},{8,11},{9,8},{10,9... | collective-permute-start | bytes 1179656 | tf_op jit(solution)/shard_map/ppermute | solution.py:18
  101.1 12.4 %collective-permute-start.16 = (bf16[96,2048]{1,0:T(8,128)(2,1)S(1)}, bf16[96,2048]{1,0:T(8,128)(2,1)S(1)}, u32[]{:S(2)}, u32[]{:S(2)}) collective-permute-start(bf16[96,2048]{1,0:T(8,128)(2,1)S(1)} %pad_maximum_fusion.1.refs_0_), channel_id=1, source_target_pairs={{0,1},{1,2},{2,3},{3,0},{4,5},{5,6},{6,7},{7,4},{8,9},{9,10},{10,1... | collective-permute-start | bytes 1179656 | tf_op jit(solution)/shard_map/ppermute | solution.py:18
  106.3 11.8 %collective-permute-start.20 = (bf16[96,2048]{1,0:T(8,128)(2,1)S(1)}, bf16[96,2048]{1,0:T(8,128)(2,1)S(1)}, u32[]{:S(2)}, u32[]{:S(2)}) collective-permute-start(bf16[96,2048]{1,0:T(8,128)(2,1)S(1)} %collective-permute-done.15.refs_1_), channel_id=1, source_target_pairs={{0,3},{1,0},{2,1},{3,2},{4,7},{5,4},{6,5},{7,6},{8,11},{9,8},{10,9... | collective-permute-start | bytes 1179656 | tf_op jit(solution)/shard_map/ppermute | solution.py:18
  113.5 15.2 %collective-permute-start.19 = (bf16[96,2048]{1,0:T(8,128)(2,1)S(1)}, bf16[96,2048]{1,0:T(8,128)(2,1)S(1)}, u32[]{:S(2)}, u32[]{:S(2)}) collective-permute-start(bf16[96,2048]{1,0:T(8,128)(2,1)S(1)} %tie.1.refs_2_), channel_id=1, source_target_pairs={{0,1},{1,2},{2,3},{3,0},{4,5},{5,6},{6,7},{7,4},{8,9},{9,10},{10,1... | collective-permute-start | bytes 1179656 | tf_op jit(solution)/shard_map/ppermute | solution.py:18
  115.4 18.0 %collective-permute-start.18 = (bf16[96,2048]{1,0:T(8,128)(2,1)S(1)}, bf16[96,2048]{1,0:T(8,128)(2,1)S(1)}, u32[]{:S(2)}, u32[]{:S(2)}) collective-permute-start(bf16[96,2048]{1,0:T(8,128)(2,1)S(1)} %collective-permute-done.15.refs_1_), channel_id=1, source_target_pairs={{0,1},{1,2},{2,3},{3,0},{4,5},{5,6},{6,7},{7,4},{8,9},{9,10},{10,1... | collective-permute-start | bytes 1179656 | tf_op jit(solution)/shard_map/ppermute | solution.py:18
  118.1 20.4 %collective-permute-start.21 = (bf16[96,2048]{1,0:T(8,128)(2,1)S(1)}, bf16[96,2048]{1,0:T(8,128)(2,1)}, u32[]{:S(2)}, u32[]{:S(2)}) collective-permute-start(bf16[96,2048]{1,0:T(8,128)(2,1)S(1)} %collective-permute-done.20.refs_6_.refs_7_), channel_id=1, source_target_pairs={{0,3},{1,0},{2,1},{3,2},{4,7},{5,4},{6,5},{7,6},{8,11},{9,8},{10,9... | collective-permute-start | bytes 1179656 | tf_op jit(solution)/shard_map/ppermute | solution.py:18
  140.7 20.2 %collective-permute-start.27 = (bf16[256,256]{1,0:T(8,128)(2,1)S(1)}, bf16[256,256]{1,0:T(8,128)(2,1)S(1)}, u32[]{:S(2)}, u32[]{:S(2)}) collective-permute-start(bf16[256,256]{1,0:T(8,128)(2,1)S(1)} %get-tuple-element.57), channel_id=1, source_target_pairs={{0,288},{48,336},{96,0},{144,48},{192,96},{240,144},{288,192},{336... | collective-permute-start | bytes 393224 | tf_op jit(solution)/shard_map/ppermute | solution.py:18
  143.0 21.7 %collective-permute-start.28 = (bf16[256,256]{1,0:T(8,128)(2,1)S(1)}, bf16[256,256]{1,0:T(8,128)(2,1)S(1)}, u32[]{:S(2)}, u32[]{:S(2)}) collective-permute-start(bf16[256,256]{1,0:T(8,128)(2,1)S(1)} %get-tuple-element.58), channel_id=1, source_target_pairs={{0,192},{48,240},{96,288},{144,336},{192,0},{240,48},{288,96},{336... | collective-permute-start | bytes 393224 | tf_op jit(solution)/shard_map/ppermute | solution.py:18
  149.8 20.9 %collective-permute-start.29 = (bf16[256,256]{1,0:T(8,128)(2,1)S(1)}, bf16[256,256]{1,0:T(8,128)(2,1)S(1)}, u32[]{:S(2)}, u32[]{:S(2)}) collective-permute-start(bf16[256,256]{1,0:T(8,128)(2,1)S(1)} %get-tuple-element.59), channel_id=1, source_target_pairs={{0,96},{48,144},{96,192},{144,240},{192,288},{240,336},{288,0},{33... | collective-permute-start | bytes 393224 | tf_op jit(solution)/shard_map/ppermute | solution.py:18
  156.1 26.1 %collective-permute-start.22 = (f32[384,256]{1,0:T(8,128)S(1)}, f32[384,256]{1,0:T(8,128)S(1)}, u32[]{:S(2)}, u32[]{:S(2)}) collective-permute-start(f32[384,256]{1,0:T(8,128)S(1)} %get-tuple-element.52), channel_id=1, source_target_pairs={{0,24},{24,0},{1,25},{25,1},{2,26},{26,2},{3,27},{27,3},{4,28},{28... | collective-permute-start | bytes 1179656 | tf_op jit(solution)/shard_map/ppermute | solution.py:18
  158.0 26.6 %collective-permute-start.24 = (bf16[256,256]{1,0:T(8,128)(2,1)S(1)}, bf16[256,256]{1,0:T(8,128)(2,1)S(1)}, u32[]{:S(2)}, u32[]{:S(2)}) collective-permute-start(bf16[256,256]{1,0:T(8,128)(2,1)S(1)} %get-tuple-element.53), channel_id=1, source_target_pairs={{0,288},{48,336},{96,0},{144,48},{192,96},{240,144},{288,192},{336... | collective-permute-start | bytes 393224 | tf_op jit(solution)/shard_map/ppermute | solution.py:18
  160.9 23.8 %collective-permute-start.25 = (bf16[256,256]{1,0:T(8,128)(2,1)S(1)}, bf16[256,256]{1,0:T(8,128)(2,1)S(1)}, u32[]{:S(2)}, u32[]{:S(2)}) collective-permute-start(bf16[256,256]{1,0:T(8,128)(2,1)S(1)} %get-tuple-element.54), channel_id=1, source_target_pairs={{0,192},{48,240},{96,288},{144,336},{192,0},{240,48},{288,96},{336... | collective-permute-start | bytes 393224 | tf_op jit(solution)/shard_map/ppermute | solution.py:18
  164.7 20.0 %collective-permute-start.26 = (bf16[256,256]{1,0:T(8,128)(2,1)S(1)}, bf16[256,256]{1,0:T(8,128)(2,1)S(1)}, u32[]{:S(2)}, u32[]{:S(2)}) collective-permute-start(bf16[256,256]{1,0:T(8,128)(2,1)S(1)} %get-tuple-element.55), channel_id=1, source_target_pairs={{0,96},{48,144},{96,192},{144,240},{192,288},{240,336},{288,0},{33... | collective-permute-start | bytes 393224 | tf_op jit(solution)/shard_map/ppermute | solution.py:18
  170.9 15.7 %collective-permute-start.30 = (bf16[256,256]{1,0:T(8,128)(2,1)S(1)}, bf16[256,256]{1,0:T(8,128)(2,1)S(1)}, u32[]{:S(2)}, u32[]{:S(2)}) collective-permute-start(bf16[256,256]{1,0:T(8,128)(2,1)S(1)} %add_convert_fusion.2), channel_id=1, source_target_pairs={{0,384},{384,0},{1,385},{385,1},{2,386},{386,2},{3,387},{387,3},{4... | collective-permute-start | bytes 393224 | tf_op jit(solution)/shard_map/ppermute | solution.py:18
  182.3 8.1 %collective-permute-start.23 = (f32[192,256]{1,0:T(8,128)S(1)}, f32[192,256]{1,0:T(8,128)S(1)}, u32[]{:S(2)}, u32[]{:S(2)}) collective-permute-start(f32[192,256]{1,0:T(8,128)S(1)} %slice.29), channel_id=1, source_target_pairs={{0,48},{48,0},{96,144},{144,96},{192,240},{240,192},{288,336},{336... | collective-permute-start | bytes 589832 | tf_op jit(solution)/shard_map/ppermute | solution.py:18
  (7 other events, 191.6 us)

commit v4 on v3

--- a/solution.py
+++ b/solution.py
@@ -46,20 +46,10 @@
     return shift(value, "zh", ZH, lambda i: i ^ 1)
 
 
-def product_kernel(near, weight, *refs):
-    outs, held, sems = refs[:8], refs[8], refs[9]
-    copies = [
-        pltpu.make_async_copy(
-            weight.at[:, c * 1024 : (c + 1) * 1024], held.at[:, c * 1024 : (c + 1) * 1024], sems.at[c]
-        )
-        for c in range(8)
-    ]
-    for copy in copies:
-        copy.start()
+def product_kernel(near, weight, *outs):
     for c in range(8):
-        copies[c].wait()
         at = slice(c * 1024, (c + 1) * 1024)
-        total = jnp.dot(near[...], held[:, at], preferred_element_type=F32)
+        total = jnp.dot(near[...], weight[:, at], preferred_element_type=F32)
         for r in range(8):
             outs[r][:, at] = total[r * 24 : (r + 1) * 24].astype(BF)
 
@@ -69,9 +59,8 @@
     return pl.pallas_call(
         product_kernel,
         out_shape=(jax.ShapeDtypeStruct((24, D), BF),) * 8,
-        in_specs=[whole, pl.BlockSpec(memory_space=pltpu.HBM)],
+        in_specs=[whole] * 2,
         out_specs=(whole,) * 8,
-        scratch_shapes=[pltpu.VMEM((256, D), BF), pltpu.SemaphoreType.DMA((8,))],
         compiler_params=pltpu.CompilerParams(vmem_limit_bytes=VMEM),
         cost_estimate=pl.CostEstimate(
             flops=2 * 192 * 256 * D, bytes_accessed=(256 + 192) * 2 * D, transcendentals=0
@@ -195,19 +184,13 @@
 
 
 def back_kernel(count, first, *refs):
-    pieces, weight = refs[:count], refs[count]
-    out, held, sems = refs[-3:]
-    copies = []
+    pieces, weight, out = refs[:count], refs[count], refs[-1]
+    total = jnp.zeros(out.shape, F32)
     for c in range(8):
         at = pl.ds(pl.multiple_of((first[c // 4] + 4 * (c % 4)) * 256, 256), 256)
-        copies.append(pltpu.make_async_copy(weight.at[:, at], held.at[c], sems.at[c]))
-        copies[c].start()
-    total = jnp.zeros(out.shape, F32)
-    for c in range(8):
-        copies[c].wait()
         block = jnp.concatenate([piece[:, c * 256 : (c + 1) * 256] for piece in pieces], axis=0)
         total += lax.dot_general(
-            block, held[c], (((1,), (1,)), ((), ())), preferred_element_type=F32
+            block, weight[:, at], (((1,), (1,)), ((), ())), preferred_element_type=F32
         )
     out[...] = total
 
@@ -219,10 +202,9 @@
         functools.partial(back_kernel, len(pieces)),
         out_shape=jax.ShapeDtypeStruct((rows, 256), F32),
         in_specs=[pl.BlockSpec(memory_space=pltpu.SMEM)]
-        + [whole] * len(pieces)
-        + [pl.BlockSpec(memory_space=pltpu.HBM), pl.BlockSpec(memory_space=pl.ANY)],
+        + [whole] * (len(pieces) + 1)
+        + [pl.BlockSpec(memory_space=pl.ANY)],
         out_specs=whole,
-        scratch_shapes=[pltpu.VMEM((8, 256, 256), BF), pltpu.SemaphoreType.DMA((8,))],
         compiler_params=pltpu.CompilerParams(vmem_limit_bytes=VMEM),
         cost_estimate=pl.CostEstimate(
             flops=2 * 256 * rows * 2048, bytes_accessed=3 * 1024 * 1024, transcendentals=0
@@ -321,15 +303,15 @@
     pieces = [*lines, *ones, *twos, *threes]
 
     first = jnp.stack([1 - zh, zh]).astype(jnp.int32) * 16 + (v * 2 + core).astype(jnp.int32)
-    early = back(first, [*lines, *ones, twos[0], *threes], out_proj, blocks)
+    early = back(first, [*lines, ones[0], *threes], out_proj, blocks)
     parts = term_parts(blocks, turned, pieces, early)
     got = [[to_u(parts[k * 4 + r], r) for r in (1, 2, 3)] for k in range(2)]
     sums = [parts[k * 4] + sum(value.astype(F32) for value in got[k]) for k in range(2)]
     passing = sums[0].astype(BF)
     grad_out_proj = sums[1] + to_zh(passing).astype(F32)
 
-    late = back(first, twos[1:], out_proj, parts[4])
-    stay, go = apart([early[:480], late, early[480:]])
+    late = back(first, [ones[1], *twos], out_proj, parts[4])
+    stay, go = apart([early[:288], late, early[288:]])
     stay = stay + to_core(go)
     ours = stay[:192] + to_v(stay[192:])
     grad_attention = lax.dot_general(

time: 192 us -> 185 us (0.964)
  Pallas kernels: 12.5 us -> 8.25 us
  waiting for transfers between devices: 49.1 us -> 45.6 us
    ppermute x31, waiting for transfers between devices: 49.1 us -> 45.6 us  [shift(): return lax.ppermute(value, axis, [(i, move(i)) for i in range(size)])]
    pallas_call x2, Pallas kernels: 5.2 us -> 2.78 us  [back(): pl.pallas_call(functools.partial(back_kernel, len(pieces)), out_shape=jax...]
  transfers between devices with their start and end apart: 31 -> 31, of which waited for: 19 -> 19; matrix products, arithmetic and copies ran while one was open for 2% -> 2% of each run, Pallas kernels for 3% -> 2%
where the time goes in v4:
time: 185 us; the launch traced here: 184 us
  starting transfers between devices  119 us (64%)
  waiting for transfers between devices  45.6 us (25%)
  Pallas kernels  8.25 us (4%)
  local copies, waits for them, and re-layouts  5.4 us (3%)
  other arithmetic  3.16 us (2%)
    ppermute x31, starting transfers between devices, shift(): return lax.ppermute(value, axis, [(i, move(i)) for i in range(size)])  119 us
    ppermute x31, waiting for transfers between devices, shift(): return lax.ppermute(value, axis, [(i, move(i)) for i in range(size)])  45.6 us
    unnamed x17, local copies, waits for them, and re-layouts  5.08 us
  transfers between devices with their start and end apart: 31, of which 19 were waited for; matrix products, arithmetic and copies ran while one was open for 2% of the time, Pallas kernels for 2%

profile of v4, /device:TPU:144, one launch (start us, length us, event | category | flops | bytes accessed | tf_op | source)
XLA Modules:
  0.0 183.6 jit_solution(12724637369241825607)
XLA Ops:
  5.0 3.5 %collective-permute-start.4 = (bf16[24,8192]{1,0:T(8,128)(2,1)S(1)}, bf16[24,8192]{1,0:T(8,128)(2,1)S(1)}, u32[]{:S(2)}, u32[]{:S(2)}) collective-permute-start(bf16[24,8192]{1,0:T(8,128)(2,1)S(1)} %get-tuple-element.41), channel_id=1, source_target_pairs={{0,1},{1,2},{2,3},{3,0},{4,5},{5,6},{6,7},{7,4},{8,9},{9,10},{10,1... | collective-permute-start | bytes 1179656 | tf_op jit(solution)/shard_map/ppermute | solution.py:18
  8.5 3.6 %collective-permute-start = (bf16[24,8192]{1,0:T(8,128)(2,1)S(1)}, bf16[24,8192]{1,0:T(8,128)(2,1)S(1)}, u32[]{:S(2)}, u32[]{:S(2)}) collective-permute-start(bf16[24,8192]{1,0:T(8,128)(2,1)S(1)} %get-tuple-element.34), channel_id=1, source_target_pairs={{0,3},{1,0},{2,1},{3,2},{4,7},{5,4},{6,5},{7,6},{8,11},{9,8},{10,9... | collective-permute-start | bytes 1179656 | tf_op jit(solution)/shard_map/ppermute | solution.py:18
  12.2 3.5 %collective-permute-start.3 = (bf16[24,8192]{1,0:T(8,128)(2,1)S(1)}, bf16[24,8192]{1,0:T(8,128)(2,1)S(1)}, u32[]{:S(2)}, u32[]{:S(2)}) collective-permute-start(bf16[24,8192]{1,0:T(8,128)(2,1)S(1)} %get-tuple-element.39), channel_id=1, source_target_pairs={{0,3},{1,0},{2,1},{3,2},{4,7},{5,4},{6,5},{7,6},{8,11},{9,8},{10,9... | collective-permute-start | bytes 1179656 | tf_op jit(solution)/shard_map/ppermute | solution.py:18
  15.7 3.4 %collective-permute-done.4 = bf16[24,8192]{1,0:T(8,128)(2,1)S(1)} collective-permute-done((bf16[24,8192]{1,0:T(8,128)(2,1)S(1)}, bf16[24,8192]{1,0:T(8,128)(2,1)S(1)}, u32[]{:S(2)}, u32[]{:S(2)}) %collective-permute-start.4) | collective-permute-done | bytes 393248 | tf_op jit(solution)/shard_map/ppermute | solution.py:18
  22.8 4.9 %collective-permute-start.1 = (bf16[24,8192]{1,0:T(8,128)(2,1)S(1)}, bf16[24,8192]{1,0:T(8,128)(2,1)S(1)}, u32[]{:S(2)}, u32[]{:S(2)}) collective-permute-start(bf16[24,8192]{1,0:T(8,128)(2,1)S(1)} %get-tuple-element.36), channel_id=1, source_target_pairs={{0,3},{1,0},{2,1},{3,2},{4,7},{5,4},{6,5},{7,6},{8,11},{9,8},{10,9... | collective-permute-start | bytes 1179656 | tf_op jit(solution)/shard_map/ppermute | solution.py:18
  30.9 2.8 %collective-permute-done.5 = bf16[24,8192]{1,0:T(8,128)(2,1)S(1)} collective-permute-done((bf16[24,8192]{1,0:T(8,128)(2,1)S(1)}, bf16[24,8192]{1,0:T(8,128)(2,1)S(1)}, u32[]{:S(2)}, u32[]{:S(2)}) %collective-permute-start.5) | collective-permute-done | bytes 393248 | tf_op jit(solution)/shard_map/ppermute | solution.py:18
  34.6 4.3 %collective-permute-start.6 = (bf16[24,8192]{1,0:T(8,128)(2,1)}, bf16[24,8192]{1,0:T(8,128)(2,1)S(1)}, u32[]{:S(2)}, u32[]{:S(2)}) collective-permute-start(bf16[24,8192]{1,0:T(8,128)(2,1)} %add_convert_fusion), channel_id=1, source_target_pairs={{0,4},{4,0},{8,12},{12,8},{16,20},{20,16},{1,5},{5,1},{9,13},{13,9... | collective-permute-start | bytes 1179656 | tf_op jit(solution)/shard_map/ppermute | solution.py:18
  42.1 3.5 %collective-permute-start.10 = (bf16[24,16,256]{2,1,0:T(8,128)(2,1)S(1)}, bf16[24,16,256]{2,1,0:T(8,128)(2,1)}, u32[]{:S(2)}, u32[]{:S(2)}) collective-permute-start(bf16[24,16,256]{2,1,0:T(8,128)(2,1)S(1)} %pad_maximum_fusion.2), channel_id=1, source_target_pairs={{0,48},{48,0},{96,144},{144,96},{192,240},{240,192},{288,336},{336... | collective-permute-start | bytes 589832 | tf_op jit(solution)/shard_map/ppermute | solution.py:18
  48.0 7.3 %collective-permute-start.8 = (bf16[8,8192]{1,0:T(8,128)(2,1)S(1)}, bf16[8,8192]{1,0:T(8,128)(2,1)S(1)}, u32[]{:S(2)}, u32[]{:S(2)}) collective-permute-start(bf16[8,8192]{1,0:T(8,128)(2,1)S(1)} %get-tuple-element.44), channel_id=1, source_target_pairs={{0,8},{4,12},{8,16},{12,20},{16,0},{20,4},{1,9},{5,13},{9,17},{13,... | collective-permute-start | bytes 393224 | tf_op jit(solution)/shard_map/ppermute | solution.py:18
  56.6 2.6 %collective-permute-done.7.second = bf16[8,8192]{1,0:T(8,128)(2,1)S(1)} collective-permute-done((bf16[8,8192]{1,0:T(8,128)(2,1)S(1)}, bf16[8,8192]{1,0:T(8,128)(2,1)S(1)}, u32[]{:S(2)}, u32[]{:S(2)}) %collective-permute-start.7) | collective-permute-done | bytes 131104 | tf_op jit(solution)/shard_map/ppermute | solution.py:18
  59.2 2.8 %collective-permute-done.8.third = bf16[8,8192]{1,0:T(8,128)(2,1)S(1)} collective-permute-done((bf16[8,8192]{1,0:T(8,128)(2,1)S(1)}, bf16[8,8192]{1,0:T(8,128)(2,1)S(1)}, u32[]{:S(2)}, u32[]{:S(2)}) %collective-permute-start.8) | collective-permute-done | bytes 131104 | tf_op jit(solution)/shard_map/ppermute | solution.py:18
  66.8 2.4 %collective-permute-start.12 = (bf16[16,2048]{1,0:T(8,128)(2,1)S(1)}, bf16[16,2048]{1,0:T(8,128)(2,1)S(1)}, u32[]{:S(2)}, u32[]{:S(2)}) collective-permute-start(bf16[16,2048]{1,0:T(8,128)(2,1)S(1)} %get-tuple-element.61), channel_id=1, source_target_pairs={{0,48},{48,0},{96,144},{144,96},{192,240},{240,192},{288,336},{336... | collective-permute-start | bytes 196616 | tf_op jit(solution)/shard_map/ppermute | solution.py:18
  69.1 3.8 %collective-permute-done.12 = bf16[16,2048]{1,0:T(8,128)(2,1)S(1)} collective-permute-done((bf16[16,2048]{1,0:T(8,128)(2,1)S(1)}, bf16[16,2048]{1,0:T(8,128)(2,1)S(1)}, u32[]{:S(2)}, u32[]{:S(2)}) %collective-permute-start.12) | collective-permute-done | bytes 65568 | tf_op jit(solution)/shard_map/ppermute | solution.py:18
  72.9 8.8 %collective-permute-start.14 = (bf16[32,2048]{1,0:T(8,128)(2,1)S(1)}, bf16[32,2048]{1,0:T(8,128)(2,1)S(1)}, u32[]{:S(2)}, u32[]{:S(2)}) collective-permute-start(bf16[32,2048]{1,0:T(8,128)(2,1)S(1)} %pad_maximum_fusion.3), channel_id=1, source_target_pairs={{0,16},{4,20},{8,0},{12,4},{16,8},{20,12},{1,17},{5,21},{9,1},{13,... | collective-permute-start | bytes 393224 | tf_op jit(solution)/shard_map/ppermute | solution.py:18
  83.6 2.5 %collective-permute-done.14 = bf16[32,2048]{1,0:T(8,128)(2,1)S(1)} collective-permute-done((bf16[32,2048]{1,0:T(8,128)(2,1)S(1)}, bf16[32,2048]{1,0:T(8,128)(2,1)S(1)}, u32[]{:S(2)}, u32[]{:S(2)}) %collective-permute-start.14) | collective-permute-done | bytes 131104 | tf_op jit(solution)/shard_map/ppermute | solution.py:18
  86.2 3.4 %collective-permute-done.13 = bf16[32,2048]{1,0:T(8,128)(2,1)S(1)} collective-permute-done((bf16[32,2048]{1,0:T(8,128)(2,1)S(1)}, bf16[32,2048]{1,0:T(8,128)(2,1)S(1)}, u32[]{:S(2)}, u32[]{:S(2)}) %collective-permute-start.13) | collective-permute-done | bytes 131104 | tf_op jit(solution)/shard_map/ppermute | solution.py:18
  89.6 6.9 %collective-permute-start.15 = (bf16[96,2048]{1,0:T(8,128)(2,1)S(1)}, bf16[96,2048]{1,0:T(8,128)(2,1)S(1)}, u32[]{:S(2)}, u32[]{:S(2)}) collective-permute-start(bf16[96,2048]{1,0:T(8,128)(2,1)S(1)} %pad_maximum_fusion.1.refs_0_), channel_id=1, source_target_pairs={{0,4},{4,0},{8,12},{12,8},{16,20},{20,16},{1,5},{5,1},{9,13},{13,9... | collective-permute-start | bytes 1179656 | tf_op jit(solution)/shard_map/ppermute | solution.py:18
  96.5 2.8 %collective-permute-start.17 = (bf16[96,2048]{1,0:T(8,128)(2,1)S(1)}, bf16[96,2048]{1,0:T(8,128)(2,1)S(1)}, u32[]{:S(2)}, u32[]{:S(2)}) collective-permute-start(bf16[96,2048]{1,0:T(8,128)(2,1)S(1)} %pad_maximum_fusion.1.refs_0_), channel_id=1, source_target_pairs={{0,3},{1,0},{2,1},{3,2},{4,7},{5,4},{6,5},{7,6},{8,11},{9,8},{10,9... | collective-permute-start | bytes 1179656 | tf_op jit(solution)/shard_map/ppermute | solution.py:18
  99.4 3.0 %collective-permute-start.16 = (bf16[96,2048]{1,0:T(8,128)(2,1)S(1)}, bf16[96,2048]{1,0:T(8,128)(2,1)S(1)}, u32[]{:S(2)}, u32[]{:S(2)}) collective-permute-start(bf16[96,2048]{1,0:T(8,128)(2,1)S(1)} %pad_maximum_fusion.1.refs_0_), channel_id=1, source_target_pairs={{0,1},{1,2},{2,3},{3,0},{4,5},{5,6},{6,7},{7,4},{8,9},{9,10},{10,1... | collective-permute-start | bytes 1179656 | tf_op jit(solution)/shard_map/ppermute | solution.py:18
  104.6 2.8 %collective-permute-start.18 = (bf16[96,2048]{1,0:T(8,128)(2,1)S(1)}, bf16[96,2048]{1,0:T(8,128)(2,1)S(1)}, u32[]{:S(2)}, u32[]{:S(2)}) collective-permute-start(bf16[96,2048]{1,0:T(8,128)(2,1)S(1)} %collective-permute-done.15.refs_1_), channel_id=1, source_target_pairs={{0,3},{1,0},{2,1},{3,2},{4,7},{5,4},{6,5},{7,6},{8,11},{9,8},{10,9... | collective-permute-start | bytes 1179656 | tf_op jit(solution)/shard_map/ppermute | solution.py:18
  108.6 3.1 %collective-permute-done.16.value = bf16[96,2048]{1,0:T(8,128)(2,1)S(1)} collective-permute-done((bf16[96,2048]{1,0:T(8,128)(2,1)S(1)}, bf16[96,2048]{1,0:T(8,128)(2,1)S(1)}, u32[]{:S(2)}, u32[]{:S(2)}) %collective-permute-start.16) | collective-permute-done | bytes 393248 | tf_op jit(solution)/shard_map/ppermute | solution.py:18
  116.4 4.4 %collective-permute-start.21 = (bf16[96,2048]{1,0:T(8,128)(2,1)S(1)}, bf16[96,2048]{1,0:T(8,128)(2,1)}, u32[]{:S(2)}, u32[]{:S(2)}) collective-permute-start(bf16[96,2048]{1,0:T(8,128)(2,1)S(1)} %collective-permute-done.18.refs_4_.refs_7_), channel_id=1, source_target_pairs={{0,3},{1,0},{2,1},{3,2},{4,7},{5,4},{6,5},{7,6},{8,11},{9,8},{10,9... | collective-permute-start | bytes 1179656 | tf_op jit(solution)/shard_map/ppermute | solution.py:18
  124.4 2.6 %collective-permute-done.20.refs_4_.refs_1_ = bf16[96,2048]{1,0:T(8,128)(2,1)S(1)} collective-permute-done((bf16[96,2048]{1,0:T(8,128)(2,1)S(1)}, bf16[96,2048]{1,0:T(8,128)(2,1)S(1)}, u32[]{:S(2)}, u32[]{:S(2)}) %collective-permute-start.20) | collective-permute-done | bytes 393248 | tf_op jit(solution)/shard_map/ppermute | solution.py:18
  126.9 4.7 %collective-permute-done.19.refs_3_.refs_0_ = bf16[96,2048]{1,0:T(8,128)(2,1)S(1)} collective-permute-done((bf16[96,2048]{1,0:T(8,128)(2,1)S(1)}, bf16[96,2048]{1,0:T(8,128)(2,1)S(1)}, u32[]{:S(2)}, u32[]{:S(2)}) %collective-permute-start.19) | collective-permute-done | bytes 393248 | tf_op jit(solution)/shard_map/ppermute | solution.py:18
  135.9 6.9 %collective-permute-start.28 = (bf16[256,256]{1,0:T(8,128)(2,1)S(1)}, bf16[256,256]{1,0:T(8,128)(2,1)S(1)}, u32[]{:S(2)}, u32[]{:S(2)}) collective-permute-start(bf16[256,256]{1,0:T(8,128)(2,1)S(1)} %get-tuple-element.58), channel_id=1, source_target_pairs={{0,192},{48,240},{96,288},{144,336},{192,0},{240,48},{288,96},{336... | collective-permute-start | bytes 393224 | tf_op jit(solution)/shard_map/ppermute | solution.py:18
  142.8 3.9 %collective-permute-start.29 = (bf16[256,256]{1,0:T(8,128)(2,1)S(1)}, bf16[256,256]{1,0:T(8,128)(2,1)S(1)}, u32[]{:S(2)}, u32[]{:S(2)}) collective-permute-start(bf16[256,256]{1,0:T(8,128)(2,1)S(1)} %get-tuple-element.59), channel_id=1, source_target_pairs={{0,96},{48,144},{96,192},{144,240},{192,288},{240,336},{288,0},{33... | collective-permute-start | bytes 393224 | tf_op jit(solution)/shard_map/ppermute | solution.py:18
  150.3 2.9 %collective-permute-start.24 = (bf16[256,256]{1,0:T(8,128)(2,1)S(1)}, bf16[256,256]{1,0:T(8,128)(2,1)S(1)}, u32[]{:S(2)}, u32[]{:S(2)}) collective-permute-start(bf16[256,256]{1,0:T(8,128)(2,1)S(1)} %get-tuple-element.53), channel_id=1, source_target_pairs={{0,288},{48,336},{96,0},{144,48},{192,96},{240,144},{288,192},{336... | collective-permute-start | bytes 393224 | tf_op jit(solution)/shard_map/ppermute | solution.py:18
  153.2 3.8 %collective-permute-start.25 = (bf16[256,256]{1,0:T(8,128)(2,1)S(1)}, bf16[256,256]{1,0:T(8,128)(2,1)S(1)}, u32[]{:S(2)}, u32[]{:S(2)}) collective-permute-start(bf16[256,256]{1,0:T(8,128)(2,1)S(1)} %get-tuple-element.54), channel_id=1, source_target_pairs={{0,192},{48,240},{96,288},{144,336},{192,0},{240,48},{288,96},{336... | collective-permute-start | bytes 393224 | tf_op jit(solution)/shard_map/ppermute | solution.py:18
  157.0 6.0 %collective-permute-start.26 = (bf16[256,256]{1,0:T(8,128)(2,1)S(1)}, bf16[256,256]{1,0:T(8,128)(2,1)S(1)}, u32[]{:S(2)}, u32[]{:S(2)}) collective-permute-start(bf16[256,256]{1,0:T(8,128)(2,1)S(1)} %get-tuple-element.55), channel_id=1, source_target_pairs={{0,96},{48,144},{96,192},{144,240},{192,288},{240,336},{288,0},{33... | collective-permute-start | bytes 393224 | tf_op jit(solution)/shard_map/ppermute | solution.py:18
  163.1 11.4 %collective-permute-start.30 = (bf16[256,256]{1,0:T(8,128)(2,1)S(1)}, bf16[256,256]{1,0:T(8,128)(2,1)S(1)}, u32[]{:S(2)}, u32[]{:S(2)}) collective-permute-start(bf16[256,256]{1,0:T(8,128)(2,1)S(1)} %add_convert_fusion.2), channel_id=1, source_target_pairs={{0,384},{384,0},{1,385},{385,1},{2,386},{386,2},{3,387},{387,3},{4... | collective-permute-start | bytes 393224 | tf_op jit(solution)/shard_map/ppermute | solution.py:18
  174.6 2.3 %collective-permute-start.23 = (f32[192,256]{1,0:T(8,128)S(1)}, f32[192,256]{1,0:T(8,128)S(1)}, u32[]{:S(2)}, u32[]{:S(2)}) collective-permute-start(f32[192,256]{1,0:T(8,128)S(1)} %slice.29), channel_id=1, source_target_pairs={{0,48},{48,0},{96,144},{144,96},{192,240},{240,192},{288,336},{336... | collective-permute-start | bytes 589832 | tf_op jit(solution)/shard_map/ppermute | solution.py:18
  179.6 3.1 %collective-permute-done.23 = f32[192,256]{1,0:T(8,128)S(1)} collective-permute-done((f32[192,256]{1,0:T(8,128)S(1)}, f32[192,256]{1,0:T(8,128)S(1)}, u32[]{:S(2)}, u32[]{:S(2)}) %collective-permute-start.23) | collective-permute-done | bytes 196640 | tf_op jit(solution)/shard_map/ppermute | solution.py:18
  (79 shorter events, 48.7 us)
Async XLA Ops:
  5.0 57.0 %copy-start.4 = (bf16[8,8192]{1,0:T(8,128)(2,1)S(1)}, bf16[8,8192]{1,0:T(8,128)(2,1)}, u32[]{:S(2)}) copy-start(bf16[8,8192]{1,0:T(8,128)(2,1)} %refs_0_.1) | copy-start | bytes 393220
  5.0 14.1 %collective-permute-start.4 = (bf16[24,8192]{1,0:T(8,128)(2,1)S(1)}, bf16[24,8192]{1,0:T(8,128)(2,1)S(1)}, u32[]{:S(2)}, u32[]{:S(2)}) collective-permute-start(bf16[24,8192]{1,0:T(8,128)(2,1)S(1)} %get-tuple-element.41), channel_id=1, source_target_pairs={{0,1},{1,2},{2,3},{3,0},{4,5},{5,6},{6,7},{7,4},{8,9},{9,10},{10,1... | collective-permute-start | bytes 1179656 | tf_op jit(solution)/shard_map/ppermute | solution.py:18
  8.5 13.9 %collective-permute-start = (bf16[24,8192]{1,0:T(8,128)(2,1)S(1)}, bf16[24,8192]{1,0:T(8,128)(2,1)S(1)}, u32[]{:S(2)}, u32[]{:S(2)}) collective-permute-start(bf16[24,8192]{1,0:T(8,128)(2,1)S(1)} %get-tuple-element.34), channel_id=1, source_target_pairs={{0,3},{1,0},{2,1},{3,2},{4,7},{5,4},{6,5},{7,6},{8,11},{9,8},{10,9... | collective-permute-start | bytes 1179656 | tf_op jit(solution)/shard_map/ppermute | solution.py:18
  12.2 18.7 %collective-permute-start.3 = (bf16[24,8192]{1,0:T(8,128)(2,1)S(1)}, bf16[24,8192]{1,0:T(8,128)(2,1)S(1)}, u32[]{:S(2)}, u32[]{:S(2)}) collective-permute-start(bf16[24,8192]{1,0:T(8,128)(2,1)S(1)} %get-tuple-element.39), channel_id=1, source_target_pairs={{0,3},{1,0},{2,1},{3,2},{4,7},{5,4},{6,5},{7,6},{8,11},{9,8},{10,9... | collective-permute-start | bytes 1179656 | tf_op jit(solution)/shard_map/ppermute | solution.py:18
  19.2 14.6 %collective-permute-start.5 = (bf16[24,8192]{1,0:T(8,128)(2,1)S(1)}, bf16[24,8192]{1,0:T(8,128)(2,1)S(1)}, u32[]{:S(2)}, u32[]{:S(2)}) collective-permute-start(bf16[24,8192]{1,0:T(8,128)(2,1)S(1)} %add_convert_fusion.1), channel_id=1, source_target_pairs={{0,1},{1,2},{2,3},{3,0},{4,5},{5,6},{6,7},{7,4},{8,9},{9,10},{10,1... | collective-permute-start | bytes 1179656 | tf_op jit(solution)/shard_map/ppermute | solution.py:18
  22.8 22.8 %collective-permute-start.1 = (bf16[24,8192]{1,0:T(8,128)(2,1)S(1)}, bf16[24,8192]{1,0:T(8,128)(2,1)S(1)}, u32[]{:S(2)}, u32[]{:S(2)}) collective-permute-start(bf16[24,8192]{1,0:T(8,128)(2,1)S(1)} %get-tuple-element.36), channel_id=1, source_target_pairs={{0,3},{1,0},{2,1},{3,2},{4,7},{5,4},{6,5},{7,6},{8,11},{9,8},{10,9... | collective-permute-start | bytes 1179656 | tf_op jit(solution)/shard_map/ppermute | solution.py:18
  27.7 18.0 %collective-permute-start.2 = (bf16[24,8192]{1,0:T(8,128)(2,1)S(1)}, bf16[24,8192]{1,0:T(8,128)(2,1)S(1)}, u32[]{:S(2)}, u32[]{:S(2)}) collective-permute-start(bf16[24,8192]{1,0:T(8,128)(2,1)S(1)} %get-tuple-element.37), channel_id=1, source_target_pairs={{0,1},{1,2},{2,3},{3,0},{4,5},{5,6},{6,7},{7,4},{8,9},{9,10},{10,1... | collective-permute-start | bytes 1179656 | tf_op jit(solution)/shard_map/ppermute | solution.py:18
  34.6 11.0 %collective-permute-start.6 = (bf16[24,8192]{1,0:T(8,128)(2,1)}, bf16[24,8192]{1,0:T(8,128)(2,1)S(1)}, u32[]{:S(2)}, u32[]{:S(2)}) collective-permute-start(bf16[24,8192]{1,0:T(8,128)(2,1)} %add_convert_fusion), channel_id=1, source_target_pairs={{0,4},{4,0},{8,12},{12,8},{16,20},{20,16},{1,5},{5,1},{9,13},{13,9... | collective-permute-start | bytes 1179656 | tf_op jit(solution)/shard_map/ppermute | solution.py:18
  38.9 3.2 %collective-permute-start.9 = (bf16[192,256]{1,0:T(8,128)(2,1)S(1)}, bf16[192,256]{1,0:T(8,128)(2,1)S(1)}, u32[]{:S(2)}, u32[]{:S(2)}) collective-permute-start(bf16[192,256]{1,0:T(8,128)(2,1)S(1)} %get-tuple-element.45), channel_id=1, source_target_pairs={{0,24},{24,0},{1,25},{25,1},{2,26},{26,2},{3,27},{27,3},{4,28},{28... | collective-permute-start | bytes 294920 | tf_op jit(solution)/shard_map/ppermute | solution.py:18
  42.1 13.3 %collective-permute-start.10 = (bf16[24,16,256]{2,1,0:T(8,128)(2,1)S(1)}, bf16[24,16,256]{2,1,0:T(8,128)(2,1)}, u32[]{:S(2)}, u32[]{:S(2)}) collective-permute-start(bf16[24,16,256]{2,1,0:T(8,128)(2,1)S(1)} %pad_maximum_fusion.2), channel_id=1, source_target_pairs={{0,48},{48,0},{96,144},{144,96},{192,240},{240,192},{288,336},{336... | collective-permute-start | bytes 589832 | tf_op jit(solution)/shard_map/ppermute | solution.py:18
  46.1 13.1 %collective-permute-start.7 = (bf16[8,8192]{1,0:T(8,128)(2,1)S(1)}, bf16[8,8192]{1,0:T(8,128)(2,1)S(1)}, u32[]{:S(2)}, u32[]{:S(2)}) collective-permute-start(bf16[8,8192]{1,0:T(8,128)(2,1)S(1)} %get-tuple-element.43), channel_id=1, source_target_pairs={{0,16},{4,20},{8,0},{12,4},{16,8},{20,12},{1,17},{5,21},{9,1},{13,... | collective-permute-start | bytes 393224 | tf_op jit(solution)/shard_map/ppermute | solution.py:18
  48.0 13.9 %collective-permute-start.8 = (bf16[8,8192]{1,0:T(8,128)(2,1)S(1)}, bf16[8,8192]{1,0:T(8,128)(2,1)S(1)}, u32[]{:S(2)}, u32[]{:S(2)}) collective-permute-start(bf16[8,8192]{1,0:T(8,128)(2,1)S(1)} %get-tuple-element.44), channel_id=1, source_target_pairs={{0,8},{4,12},{8,16},{12,20},{16,0},{20,4},{1,9},{5,13},{9,17},{13,... | collective-permute-start | bytes 393224 | tf_op jit(solution)/shard_map/ppermute | solution.py:18
  63.6 3.1 %collective-permute-start.11 = (bf16[8,4096]{1,0:T(8,128)(2,1)S(1)}, bf16[8,4096]{1,0:T(8,128)(2,1)S(1)}, u32[]{:S(2)}, u32[]{:S(2)}) collective-permute-start(bf16[8,4096]{1,0:T(8,128)(2,1)S(1)} %get-tuple-element.49), channel_id=1, source_target_pairs={{0,24},{24,0},{1,25},{25,1},{2,26},{26,2},{3,27},{27,3},{4,28},{28... | collective-permute-start | bytes 196616 | tf_op jit(solution)/shard_map/ppermute | solution.py:18
  66.8 6.2 %collective-permute-start.12 = (bf16[16,2048]{1,0:T(8,128)(2,1)S(1)}, bf16[16,2048]{1,0:T(8,128)(2,1)S(1)}, u32[]{:S(2)}, u32[]{:S(2)}) collective-permute-start(bf16[16,2048]{1,0:T(8,128)(2,1)S(1)} %get-tuple-element.61), channel_id=1, source_target_pairs={{0,48},{48,0},{96,144},{144,96},{192,240},{240,192},{288,336},{336... | collective-permute-start | bytes 196616 | tf_op jit(solution)/shard_map/ppermute | solution.py:18
  72.9 13.2 %collective-permute-start.14 = (bf16[32,2048]{1,0:T(8,128)(2,1)S(1)}, bf16[32,2048]{1,0:T(8,128)(2,1)S(1)}, u32[]{:S(2)}, u32[]{:S(2)}) collective-permute-start(bf16[32,2048]{1,0:T(8,128)(2,1)S(1)} %pad_maximum_fusion.3), channel_id=1, source_target_pairs={{0,16},{4,20},{8,0},{12,4},{16,8},{20,12},{1,17},{5,21},{9,1},{13,... | collective-permute-start | bytes 393224 | tf_op jit(solution)/shard_map/ppermute | solution.py:18
  81.7 7.9 %collective-permute-start.13 = (bf16[32,2048]{1,0:T(8,128)(2,1)S(1)}, bf16[32,2048]{1,0:T(8,128)(2,1)S(1)}, u32[]{:S(2)}, u32[]{:S(2)}) collective-permute-start(bf16[32,2048]{1,0:T(8,128)(2,1)S(1)} %pad_maximum_fusion.3), channel_id=1, source_target_pairs={{0,8},{4,12},{8,16},{12,20},{16,0},{20,4},{1,9},{5,13},{9,17},{13,... | collective-permute-start | bytes 393224 | tf_op jit(solution)/shard_map/ppermute | solution.py:18
  89.6 15.0 %collective-permute-start.15 = (bf16[96,2048]{1,0:T(8,128)(2,1)S(1)}, bf16[96,2048]{1,0:T(8,128)(2,1)S(1)}, u32[]{:S(2)}, u32[]{:S(2)}) collective-permute-start(bf16[96,2048]{1,0:T(8,128)(2,1)S(1)} %pad_maximum_fusion.1.refs_0_), channel_id=1, source_target_pairs={{0,4},{4,0},{8,12},{12,8},{16,20},{20,16},{1,5},{5,1},{9,13},{13,9... | collective-permute-start | bytes 1179656 | tf_op jit(solution)/shard_map/ppermute | solution.py:18
  96.5 12.1 %collective-permute-start.17 = (bf16[96,2048]{1,0:T(8,128)(2,1)S(1)}, bf16[96,2048]{1,0:T(8,128)(2,1)S(1)}, u32[]{:S(2)}, u32[]{:S(2)}) collective-permute-start(bf16[96,2048]{1,0:T(8,128)(2,1)S(1)} %pad_maximum_fusion.1.refs_0_), channel_id=1, source_target_pairs={{0,3},{1,0},{2,1},{3,2},{4,7},{5,4},{6,5},{7,6},{8,11},{9,8},{10,9... | collective-permute-start | bytes 1179656 | tf_op jit(solution)/shard_map/ppermute | solution.py:18
  99.4 12.4 %collective-permute-start.16 = (bf16[96,2048]{1,0:T(8,128)(2,1)S(1)}, bf16[96,2048]{1,0:T(8,128)(2,1)S(1)}, u32[]{:S(2)}, u32[]{:S(2)}) collective-permute-start(bf16[96,2048]{1,0:T(8,128)(2,1)S(1)} %pad_maximum_fusion.1.refs_0_), channel_id=1, source_target_pairs={{0,1},{1,2},{2,3},{3,0},{4,5},{5,6},{6,7},{7,4},{8,9},{9,10},{10,1... | collective-permute-start | bytes 1179656 | tf_op jit(solution)/shard_map/ppermute | solution.py:18
  104.6 11.8 %collective-permute-start.18 = (bf16[96,2048]{1,0:T(8,128)(2,1)S(1)}, bf16[96,2048]{1,0:T(8,128)(2,1)S(1)}, u32[]{:S(2)}, u32[]{:S(2)}) collective-permute-start(bf16[96,2048]{1,0:T(8,128)(2,1)S(1)} %collective-permute-done.15.refs_1_), channel_id=1, source_target_pairs={{0,3},{1,0},{2,1},{3,2},{4,7},{5,4},{6,5},{7,6},{8,11},{9,8},{10,9... | collective-permute-start | bytes 1179656 | tf_op jit(solution)/shard_map/ppermute | solution.py:18
  111.8 15.2 %collective-permute-start.20 = (bf16[96,2048]{1,0:T(8,128)(2,1)S(1)}, bf16[96,2048]{1,0:T(8,128)(2,1)S(1)}, u32[]{:S(2)}, u32[]{:S(2)}) collective-permute-start(bf16[96,2048]{1,0:T(8,128)(2,1)S(1)} %tie.1.refs_2_), channel_id=1, source_target_pairs={{0,1},{1,2},{2,3},{3,0},{4,5},{5,6},{6,7},{7,4},{8,9},{9,10},{10,1... | collective-permute-start | bytes 1179656 | tf_op jit(solution)/shard_map/ppermute | solution.py:18
  113.7 18.0 %collective-permute-start.19 = (bf16[96,2048]{1,0:T(8,128)(2,1)S(1)}, bf16[96,2048]{1,0:T(8,128)(2,1)S(1)}, u32[]{:S(2)}, u32[]{:S(2)}) collective-permute-start(bf16[96,2048]{1,0:T(8,128)(2,1)S(1)} %collective-permute-done.15.refs_1_), channel_id=1, source_target_pairs={{0,1},{1,2},{2,3},{3,0},{4,5},{5,6},{6,7},{7,4},{8,9},{9,10},{10,1... | collective-permute-start | bytes 1179656 | tf_op jit(solution)/shard_map/ppermute | solution.py:18
  116.4 15.3 %collective-permute-start.21 = (bf16[96,2048]{1,0:T(8,128)(2,1)S(1)}, bf16[96,2048]{1,0:T(8,128)(2,1)}, u32[]{:S(2)}, u32[]{:S(2)}) collective-permute-start(bf16[96,2048]{1,0:T(8,128)(2,1)S(1)} %collective-permute-done.18.refs_4_.refs_7_), channel_id=1, source_target_pairs={{0,3},{1,0},{2,1},{3,2},{4,7},{5,4},{6,5},{7,6},{8,11},{9,8},{10,9... | collective-permute-start | bytes 1179656 | tf_op jit(solution)/shard_map/ppermute | solution.py:18
  133.7 19.5 %collective-permute-start.27 = (bf16[256,256]{1,0:T(8,128)(2,1)S(1)}, bf16[256,256]{1,0:T(8,128)(2,1)S(1)}, u32[]{:S(2)}, u32[]{:S(2)}) collective-permute-start(bf16[256,256]{1,0:T(8,128)(2,1)S(1)} %get-tuple-element.57), channel_id=1, source_target_pairs={{0,288},{48,336},{96,0},{144,48},{192,96},{240,144},{288,192},{336... | collective-permute-start | bytes 393224 | tf_op jit(solution)/shard_map/ppermute | solution.py:18
  135.9 21.0 %collective-permute-start.28 = (bf16[256,256]{1,0:T(8,128)(2,1)S(1)}, bf16[256,256]{1,0:T(8,128)(2,1)S(1)}, u32[]{:S(2)}, u32[]{:S(2)}) collective-permute-start(bf16[256,256]{1,0:T(8,128)(2,1)S(1)} %get-tuple-element.58), channel_id=1, source_target_pairs={{0,192},{48,240},{96,288},{144,336},{192,0},{240,48},{288,96},{336... | collective-permute-start | bytes 393224 | tf_op jit(solution)/shard_map/ppermute | solution.py:18
  142.8 20.2 %collective-permute-start.29 = (bf16[256,256]{1,0:T(8,128)(2,1)S(1)}, bf16[256,256]{1,0:T(8,128)(2,1)S(1)}, u32[]{:S(2)}, u32[]{:S(2)}) collective-permute-start(bf16[256,256]{1,0:T(8,128)(2,1)S(1)} %get-tuple-element.59), channel_id=1, source_target_pairs={{0,96},{48,144},{96,192},{144,240},{192,288},{240,336},{288,0},{33... | collective-permute-start | bytes 393224 | tf_op jit(solution)/shard_map/ppermute | solution.py:18
  148.3 26.1 %collective-permute-start.22 = (f32[384,256]{1,0:T(8,128)S(1)}, f32[384,256]{1,0:T(8,128)S(1)}, u32[]{:S(2)}, u32[]{:S(2)}) collective-permute-start(f32[384,256]{1,0:T(8,128)S(1)} %get-tuple-element.52), channel_id=1, source_target_pairs={{0,24},{24,0},{1,25},{25,1},{2,26},{26,2},{3,27},{27,3},{4,28},{28... | collective-permute-start | bytes 1179656 | tf_op jit(solution)/shard_map/ppermute | solution.py:18
  150.3 26.6 %collective-permute-start.24 = (bf16[256,256]{1,0:T(8,128)(2,1)S(1)}, bf16[256,256]{1,0:T(8,128)(2,1)S(1)}, u32[]{:S(2)}, u32[]{:S(2)}) collective-permute-start(bf16[256,256]{1,0:T(8,128)(2,1)S(1)} %get-tuple-element.53), channel_id=1, source_target_pairs={{0,288},{48,336},{96,0},{144,48},{192,96},{240,144},{288,192},{336... | collective-permute-start | bytes 393224 | tf_op jit(solution)/shard_map/ppermute | solution.py:18
  153.2 23.7 %collective-permute-start.25 = (bf16[256,256]{1,0:T(8,128)(2,1)S(1)}, bf16[256,256]{1,0:T(8,128)(2,1)S(1)}, u32[]{:S(2)}, u32[]{:S(2)}) collective-permute-start(bf16[256,256]{1,0:T(8,128)(2,1)S(1)} %get-tuple-element.54), channel_id=1, source_target_pairs={{0,192},{48,240},{96,288},{144,336},{192,0},{240,48},{288,96},{336... | collective-permute-start | bytes 393224 | tf_op jit(solution)/shard_map/ppermute | solution.py:18
  157.0 20.0 %collective-permute-start.26 = (bf16[256,256]{1,0:T(8,128)(2,1)S(1)}, bf16[256,256]{1,0:T(8,128)(2,1)S(1)}, u32[]{:S(2)}, u32[]{:S(2)}) collective-permute-start(bf16[256,256]{1,0:T(8,128)(2,1)S(1)} %get-tuple-element.55), channel_id=1, source_target_pairs={{0,96},{48,144},{96,192},{144,240},{192,288},{240,336},{288,0},{33... | collective-permute-start | bytes 393224 | tf_op jit(solution)/shard_map/ppermute | solution.py:18
  163.1 15.7 %collective-permute-start.30 = (bf16[256,256]{1,0:T(8,128)(2,1)S(1)}, bf16[256,256]{1,0:T(8,128)(2,1)S(1)}, u32[]{:S(2)}, u32[]{:S(2)}) collective-permute-start(bf16[256,256]{1,0:T(8,128)(2,1)S(1)} %add_convert_fusion.2), channel_id=1, source_target_pairs={{0,384},{384,0},{1,385},{385,1},{2,386},{386,2},{3,387},{387,3},{4... | collective-permute-start | bytes 393224 | tf_op jit(solution)/shard_map/ppermute | solution.py:18
  174.6 8.1 %collective-permute-start.23 = (f32[192,256]{1,0:T(8,128)S(1)}, f32[192,256]{1,0:T(8,128)S(1)}, u32[]{:S(2)}, u32[]{:S(2)}) collective-permute-start(f32[192,256]{1,0:T(8,128)S(1)} %slice.29), channel_id=1, source_target_pairs={{0,48},{48,0},{96,144},{144,96},{192,240},{240,192},{288,336},{336... | collective-permute-start | bytes 589832 | tf_op jit(solution)/shard_map/ppermute | solution.py:18
  (7 other events, 199.9 us)

commit v5 on v4

--- a/solution.py
+++ b/solution.py
@@ -46,7 +46,8 @@
     return shift(value, "zh", ZH, lambda i: i ^ 1)
 
 
-def product_kernel(near, weight, *outs):
+def product_kernel(order, attention, weight, near, *outs):
+    near[...] = jnp.dot(order[...], attention[...], preferred_element_type=F32).astype(BF)
     for c in range(8):
         at = slice(c * 1024, (c + 1) * 1024)
         total = jnp.dot(near[...], weight[:, at], preferred_element_type=F32)
@@ -54,19 +55,19 @@
             outs[r][:, at] = total[r * 24 : (r + 1) * 24].astype(BF)
 
 
-def products(near, weight):
+def products(order, attention, weight):
     whole = pl.BlockSpec(memory_space=pltpu.VMEM)
     return pl.pallas_call(
         product_kernel,
-        out_shape=(jax.ShapeDtypeStruct((24, D), BF),) * 8,
-        in_specs=[whole] * 2,
-        out_specs=(whole,) * 8,
+        out_shape=(jax.ShapeDtypeStruct((192, 256), BF),) + (jax.ShapeDtypeStruct((24, D), BF),) * 8,
+        in_specs=[whole] * 3,
+        out_specs=(whole,) * 9,
         compiler_params=pltpu.CompilerParams(vmem_limit_bytes=VMEM),
         cost_estimate=pl.CostEstimate(
             flops=2 * 192 * 256 * D, bytes_accessed=(256 + 192) * 2 * D, transcendentals=0
         ),
         name="products",
-    )(near, weight)
+    )(order, attention, weight)
 
 
 def forward_kernel(value, arrived, held, near, out, held_out, near_out):
@@ -266,9 +267,10 @@
     owner = (owner_p * 2 + owner_q) * X + owner_x
     token = jnp.repeat(owner * 8, 8) + jnp.tile(jnp.arange(8, dtype=jnp.int32), 24)
     order = (token[:, None] == jnp.arange(192, dtype=jnp.int32)[None, :]).astype(BF)
-    near = jnp.dot(order, attention, preferred_element_type=F32).astype(BF)
-
-    keep, send, one_keep, one_send, left, right, three_keep, three_send = products(near, out_proj)
+
+    near, keep, send, one_keep, one_send, left, right, three_keep, three_send = products(
+        order, attention, out_proj
+    )
     left, right = to_x(left, 1), to_x(right, 3)
     right = to_x((three_send.astype(F32) + right.astype(F32)).astype(BF), 3)
     from_right = to_x(one_send, 1)

time: 185 us -> 184 us (level)
  no operation moved by 1% of the time
where the time goes in v5:
time: 184 us; the launch traced here: 183 us
  starting transfers between devices  119 us (65%)
  waiting for transfers between devices  45.7 us (25%)
  Pallas kernels  7.45 us (4%)
  local copies, waits for them, and re-layouts  5.62 us (3%)
  other arithmetic  3.25 us (2%)
    ppermute x31, starting transfers between devices, shift(): return lax.ppermute(value, axis, [(i, move(i)) for i in range(size)])  119 us
    ppermute x31, waiting for transfers between devices, shift(): return lax.ppermute(value, axis, [(i, move(i)) for i in range(size)])  45.7 us
    unnamed x17, local copies, waits for them, and re-layouts  5.3 us
  transfers between devices with their start and end apart: 31, of which 19 were waited for; matrix products, arithmetic and copies ran while one was open for 2% of the time, Pallas kernels for 2%

profile of v5, /device:TPU:144, one launch (start us, length us, event | category | flops | bytes accessed | tf_op | source)
XLA Modules:
  0.0 182.9 jit_solution(1091576778917670243)
XLA Ops:
  5.2 3.5 %collective-permute-start.4 = (bf16[24,8192]{1,0:T(8,128)(2,1)S(1)}, bf16[24,8192]{1,0:T(8,128)(2,1)S(1)}, u32[]{:S(2)}, u32[]{:S(2)}) collective-permute-start(bf16[24,8192]{1,0:T(8,128)(2,1)S(1)} %get-tuple-element.43), channel_id=1, source_target_pairs={{0,1},{1,2},{2,3},{3,0},{4,5},{5,6},{6,7},{7,4},{8,9},{9,10},{10,1... | collective-permute-start | bytes 1179656 | tf_op jit(solution)/shard_map/ppermute | solution.py:18
  8.8 3.6 %collective-permute-start = (bf16[24,8192]{1,0:T(8,128)(2,1)S(1)}, bf16[24,8192]{1,0:T(8,128)(2,1)S(1)}, u32[]{:S(2)}, u32[]{:S(2)}) collective-permute-start(bf16[24,8192]{1,0:T(8,128)(2,1)S(1)} %get-tuple-element.35), channel_id=1, source_target_pairs={{0,3},{1,0},{2,1},{3,2},{4,7},{5,4},{6,5},{7,6},{8,11},{9,8},{10,9... | collective-permute-start | bytes 1179656 | tf_op jit(solution)/shard_map/ppermute | solution.py:18
  12.4 3.5 %collective-permute-start.3 = (bf16[24,8192]{1,0:T(8,128)(2,1)S(1)}, bf16[24,8192]{1,0:T(8,128)(2,1)S(1)}, u32[]{:S(2)}, u32[]{:S(2)}) collective-permute-start(bf16[24,8192]{1,0:T(8,128)(2,1)S(1)} %get-tuple-element.41), channel_id=1, source_target_pairs={{0,3},{1,0},{2,1},{3,2},{4,7},{5,4},{6,5},{7,6},{8,11},{9,8},{10,9... | collective-permute-start | bytes 1179656 | tf_op jit(solution)/shard_map/ppermute | solution.py:18
  15.9 3.4 %collective-permute-done.4 = bf16[24,8192]{1,0:T(8,128)(2,1)S(1)} collective-permute-done((bf16[24,8192]{1,0:T(8,128)(2,1)S(1)}, bf16[24,8192]{1,0:T(8,128)(2,1)S(1)}, u32[]{:S(2)}, u32[]{:S(2)}) %collective-permute-start.4) | collective-permute-done | bytes 393248 | tf_op jit(solution)/shard_map/ppermute | solution.py:18
  23.0 4.9 %collective-permute-start.1 = (bf16[24,8192]{1,0:T(8,128)(2,1)S(1)}, bf16[24,8192]{1,0:T(8,128)(2,1)S(1)}, u32[]{:S(2)}, u32[]{:S(2)}) collective-permute-start(bf16[24,8192]{1,0:T(8,128)(2,1)S(1)} %get-tuple-element.38), channel_id=1, source_target_pairs={{0,3},{1,0},{2,1},{3,2},{4,7},{5,4},{6,5},{7,6},{8,11},{9,8},{10,9... | collective-permute-start | bytes 1179656 | tf_op jit(solution)/shard_map/ppermute | solution.py:18
  31.1 2.9 %collective-permute-done.5 = bf16[24,8192]{1,0:T(8,128)(2,1)S(1)} collective-permute-done((bf16[24,8192]{1,0:T(8,128)(2,1)S(1)}, bf16[24,8192]{1,0:T(8,128)(2,1)S(1)}, u32[]{:S(2)}, u32[]{:S(2)}) %collective-permute-start.5) | collective-permute-done | bytes 393248 | tf_op jit(solution)/shard_map/ppermute | solution.py:18
  34.9 4.3 %collective-permute-start.6 = (bf16[24,8192]{1,0:T(8,128)(2,1)}, bf16[24,8192]{1,0:T(8,128)(2,1)S(1)}, u32[]{:S(2)}, u32[]{:S(2)}) collective-permute-start(bf16[24,8192]{1,0:T(8,128)(2,1)} %add_convert_fusion), channel_id=1, source_target_pairs={{0,4},{4,0},{8,12},{12,8},{16,20},{20,16},{1,5},{5,1},{9,13},{13,9... | collective-permute-start | bytes 1179656 | tf_op jit(solution)/shard_map/ppermute | solution.py:18
  42.3 3.5 %collective-permute-start.10 = (bf16[24,16,256]{2,1,0:T(8,128)(2,1)S(1)}, bf16[24,16,256]{2,1,0:T(8,128)(2,1)}, u32[]{:S(2)}, u32[]{:S(2)}) collective-permute-start(bf16[24,16,256]{2,1,0:T(8,128)(2,1)S(1)} %pad_maximum_fusion.2), channel_id=1, source_target_pairs={{0,48},{48,0},{96,144},{144,96},{192,240},{240,192},{288,336},{336... | collective-permute-start | bytes 589832 | tf_op jit(solution)/shard_map/ppermute | solution.py:18
  48.3 7.3 %collective-permute-start.8 = (bf16[8,8192]{1,0:T(8,128)(2,1)S(1)}, bf16[8,8192]{1,0:T(8,128)(2,1)S(1)}, u32[]{:S(2)}, u32[]{:S(2)}) collective-permute-start(bf16[8,8192]{1,0:T(8,128)(2,1)S(1)} %get-tuple-element.46), channel_id=1, source_target_pairs={{0,8},{4,12},{8,16},{12,20},{16,0},{20,4},{1,9},{5,13},{9,17},{13,... | collective-permute-start | bytes 393224 | tf_op jit(solution)/shard_map/ppermute | solution.py:18
  56.8 2.6 %collective-permute-done.7.second = bf16[8,8192]{1,0:T(8,128)(2,1)S(1)} collective-permute-done((bf16[8,8192]{1,0:T(8,128)(2,1)S(1)}, bf16[8,8192]{1,0:T(8,128)(2,1)S(1)}, u32[]{:S(2)}, u32[]{:S(2)}) %collective-permute-start.7) | collective-permute-done | bytes 131104 | tf_op jit(solution)/shard_map/ppermute | solution.py:18
  59.4 2.8 %collective-permute-done.8.third = bf16[8,8192]{1,0:T(8,128)(2,1)S(1)} collective-permute-done((bf16[8,8192]{1,0:T(8,128)(2,1)S(1)}, bf16[8,8192]{1,0:T(8,128)(2,1)S(1)}, u32[]{:S(2)}, u32[]{:S(2)}) %collective-permute-start.8) | collective-permute-done | bytes 131104 | tf_op jit(solution)/shard_map/ppermute | solution.py:18
  67.0 2.3 %collective-permute-start.12 = (bf16[16,2048]{1,0:T(8,128)(2,1)S(1)}, bf16[16,2048]{1,0:T(8,128)(2,1)S(1)}, u32[]{:S(2)}, u32[]{:S(2)}) collective-permute-start(bf16[16,2048]{1,0:T(8,128)(2,1)S(1)} %get-tuple-element.63), channel_id=1, source_target_pairs={{0,48},{48,0},{96,144},{144,96},{192,240},{240,192},{288,336},{336... | collective-permute-start | bytes 196616 | tf_op jit(solution)/shard_map/ppermute | solution.py:18
  69.3 3.8 %collective-permute-done.12 = bf16[16,2048]{1,0:T(8,128)(2,1)S(1)} collective-permute-done((bf16[16,2048]{1,0:T(8,128)(2,1)S(1)}, bf16[16,2048]{1,0:T(8,128)(2,1)S(1)}, u32[]{:S(2)}, u32[]{:S(2)}) %collective-permute-start.12) | collective-permute-done | bytes 65568 | tf_op jit(solution)/shard_map/ppermute | solution.py:18
  73.2 8.8 %collective-permute-start.14 = (bf16[32,2048]{1,0:T(8,128)(2,1)S(1)}, bf16[32,2048]{1,0:T(8,128)(2,1)S(1)}, u32[]{:S(2)}, u32[]{:S(2)}) collective-permute-start(bf16[32,2048]{1,0:T(8,128)(2,1)S(1)} %pad_maximum_fusion.3), channel_id=1, source_target_pairs={{0,16},{4,20},{8,0},{12,4},{16,8},{20,12},{1,17},{5,21},{9,1},{13,... | collective-permute-start | bytes 393224 | tf_op jit(solution)/shard_map/ppermute | solution.py:18
  83.9 2.5 %collective-permute-done.14 = bf16[32,2048]{1,0:T(8,128)(2,1)S(1)} collective-permute-done((bf16[32,2048]{1,0:T(8,128)(2,1)S(1)}, bf16[32,2048]{1,0:T(8,128)(2,1)S(1)}, u32[]{:S(2)}, u32[]{:S(2)}) %collective-permute-start.14) | collective-permute-done | bytes 131104 | tf_op jit(solution)/shard_map/ppermute | solution.py:18
  86.4 3.4 %collective-permute-done.13 = bf16[32,2048]{1,0:T(8,128)(2,1)S(1)} collective-permute-done((bf16[32,2048]{1,0:T(8,128)(2,1)S(1)}, bf16[32,2048]{1,0:T(8,128)(2,1)S(1)}, u32[]{:S(2)}, u32[]{:S(2)}) %collective-permute-start.13) | collective-permute-done | bytes 131104 | tf_op jit(solution)/shard_map/ppermute | solution.py:18
  89.8 6.9 %collective-permute-start.15 = (bf16[96,2048]{1,0:T(8,128)(2,1)S(1)}, bf16[96,2048]{1,0:T(8,128)(2,1)S(1)}, u32[]{:S(2)}, u32[]{:S(2)}) collective-permute-start(bf16[96,2048]{1,0:T(8,128)(2,1)S(1)} %pad_maximum_fusion.1.refs_0_), channel_id=1, source_target_pairs={{0,4},{4,0},{8,12},{12,8},{16,20},{20,16},{1,5},{5,1},{9,13},{13,9... | collective-permute-start | bytes 1179656 | tf_op jit(solution)/shard_map/ppermute | solution.py:18
  96.8 2.8 %collective-permute-start.17 = (bf16[96,2048]{1,0:T(8,128)(2,1)S(1)}, bf16[96,2048]{1,0:T(8,128)(2,1)S(1)}, u32[]{:S(2)}, u32[]{:S(2)}) collective-permute-start(bf16[96,2048]{1,0:T(8,128)(2,1)S(1)} %pad_maximum_fusion.1.refs_0_), channel_id=1, source_target_pairs={{0,3},{1,0},{2,1},{3,2},{4,7},{5,4},{6,5},{7,6},{8,11},{9,8},{10,9... | collective-permute-start | bytes 1179656 | tf_op jit(solution)/shard_map/ppermute | solution.py:18
  99.6 3.0 %collective-permute-start.16 = (bf16[96,2048]{1,0:T(8,128)(2,1)S(1)}, bf16[96,2048]{1,0:T(8,128)(2,1)S(1)}, u32[]{:S(2)}, u32[]{:S(2)}) collective-permute-start(bf16[96,2048]{1,0:T(8,128)(2,1)S(1)} %pad_maximum_fusion.1.refs_0_), channel_id=1, source_target_pairs={{0,1},{1,2},{2,3},{3,0},{4,5},{5,6},{6,7},{7,4},{8,9},{9,10},{10,1... | collective-permute-start | bytes 1179656 | tf_op jit(solution)/shard_map/ppermute | solution.py:18
  104.8 2.8 %collective-permute-start.18 = (bf16[96,2048]{1,0:T(8,128)(2,1)S(1)}, bf16[96,2048]{1,0:T(8,128)(2,1)S(1)}, u32[]{:S(2)}, u32[]{:S(2)}) collective-permute-start(bf16[96,2048]{1,0:T(8,128)(2,1)S(1)} %collective-permute-done.15.refs_1_), channel_id=1, source_target_pairs={{0,3},{1,0},{2,1},{3,2},{4,7},{5,4},{6,5},{7,6},{8,11},{9,8},{10,9... | collective-permute-start | bytes 1179656 | tf_op jit(solution)/shard_map/ppermute | solution.py:18
  108.9 3.1 %collective-permute-done.16.value = bf16[96,2048]{1,0:T(8,128)(2,1)S(1)} collective-permute-done((bf16[96,2048]{1,0:T(8,128)(2,1)S(1)}, bf16[96,2048]{1,0:T(8,128)(2,1)S(1)}, u32[]{:S(2)}, u32[]{:S(2)}) %collective-permute-start.16) | collective-permute-done | bytes 393248 | tf_op jit(solution)/shard_map/ppermute | solution.py:18
  116.6 4.4 %collective-permute-start.21 = (bf16[96,2048]{1,0:T(8,128)(2,1)S(1)}, bf16[96,2048]{1,0:T(8,128)(2,1)S(1)}, u32[]{:S(2)}, u32[]{:S(2)}) collective-permute-start(bf16[96,2048]{1,0:T(8,128)(2,1)S(1)} %collective-permute-done.18.refs_4_.refs_7_), channel_id=1, source_target_pairs={{0,3},{1,0},{2,1},{3,2},{4,7},{5,4},{6,5},{7,6},{8,11},{9,8},{10,9... | collective-permute-start | bytes 1179656 | tf_op jit(solution)/shard_map/ppermute | solution.py:18
  124.6 2.6 %collective-permute-done.20.refs_4_.refs_1_ = bf16[96,2048]{1,0:T(8,128)(2,1)S(1)} collective-permute-done((bf16[96,2048]{1,0:T(8,128)(2,1)S(1)}, bf16[96,2048]{1,0:T(8,128)(2,1)S(1)}, u32[]{:S(2)}, u32[]{:S(2)}) %collective-permute-start.20) | collective-permute-done | bytes 393248 | tf_op jit(solution)/shard_map/ppermute | solution.py:18
  127.2 4.7 %collective-permute-done.19.refs_3_.refs_0_ = bf16[96,2048]{1,0:T(8,128)(2,1)S(1)} collective-permute-done((bf16[96,2048]{1,0:T(8,128)(2,1)S(1)}, bf16[96,2048]{1,0:T(8,128)(2,1)S(1)}, u32[]{:S(2)}, u32[]{:S(2)}) %collective-permute-start.19) | collective-permute-done | bytes 393248 | tf_op jit(solution)/shard_map/ppermute | solution.py:18
  135.7 6.8 %collective-permute-start.28 = (bf16[256,256]{1,0:T(8,128)(2,1)S(1)}, bf16[256,256]{1,0:T(8,128)(2,1)S(1)}, u32[]{:S(2)}, u32[]{:S(2)}) collective-permute-start(bf16[256,256]{1,0:T(8,128)(2,1)S(1)} %get-tuple-element.60), channel_id=1, source_target_pairs={{0,192},{48,240},{96,288},{144,336},{192,0},{240,48},{288,96},{336... | collective-permute-start | bytes 393224 | tf_op jit(solution)/shard_map/ppermute | solution.py:18
  142.6 3.9 %collective-permute-start.29 = (bf16[256,256]{1,0:T(8,128)(2,1)S(1)}, bf16[256,256]{1,0:T(8,128)(2,1)S(1)}, u32[]{:S(2)}, u32[]{:S(2)}) collective-permute-start(bf16[256,256]{1,0:T(8,128)(2,1)S(1)} %get-tuple-element.61), channel_id=1, source_target_pairs={{0,96},{48,144},{96,192},{144,240},{192,288},{240,336},{288,0},{33... | collective-permute-start | bytes 393224 | tf_op jit(solution)/shard_map/ppermute | solution.py:18
  149.6 2.8 %collective-permute-start.24 = (bf16[256,256]{1,0:T(8,128)(2,1)S(1)}, bf16[256,256]{1,0:T(8,128)(2,1)S(1)}, u32[]{:S(2)}, u32[]{:S(2)}) collective-permute-start(bf16[256,256]{1,0:T(8,128)(2,1)S(1)} %get-tuple-element.55), channel_id=1, source_target_pairs={{0,288},{48,336},{96,0},{144,48},{192,96},{240,144},{288,192},{336... | collective-permute-start | bytes 393224 | tf_op jit(solution)/shard_map/ppermute | solution.py:18
  152.4 3.8 %collective-permute-start.25 = (bf16[256,256]{1,0:T(8,128)(2,1)S(1)}, bf16[256,256]{1,0:T(8,128)(2,1)S(1)}, u32[]{:S(2)}, u32[]{:S(2)}) collective-permute-start(bf16[256,256]{1,0:T(8,128)(2,1)S(1)} %get-tuple-element.56), channel_id=1, source_target_pairs={{0,192},{48,240},{96,288},{144,336},{192,0},{240,48},{288,96},{336... | collective-permute-start | bytes 393224 | tf_op jit(solution)/shard_map/ppermute | solution.py:18
  156.2 6.0 %collective-permute-start.26 = (bf16[256,256]{1,0:T(8,128)(2,1)S(1)}, bf16[256,256]{1,0:T(8,128)(2,1)S(1)}, u32[]{:S(2)}, u32[]{:S(2)}) collective-permute-start(bf16[256,256]{1,0:T(8,128)(2,1)S(1)} %get-tuple-element.57), channel_id=1, source_target_pairs={{0,96},{48,144},{96,192},{144,240},{192,288},{240,336},{288,0},{33... | collective-permute-start | bytes 393224 | tf_op jit(solution)/shard_map/ppermute | solution.py:18
  162.4 11.4 %collective-permute-start.30 = (bf16[256,256]{1,0:T(8,128)(2,1)S(1)}, bf16[256,256]{1,0:T(8,128)(2,1)S(1)}, u32[]{:S(2)}, u32[]{:S(2)}) collective-permute-start(bf16[256,256]{1,0:T(8,128)(2,1)S(1)} %add_convert_fusion.2), channel_id=1, source_target_pairs={{0,384},{384,0},{1,385},{385,1},{2,386},{386,2},{3,387},{387,3},{4... | collective-permute-start | bytes 393224 | tf_op jit(solution)/shard_map/ppermute | solution.py:18
  173.9 2.3 %collective-permute-start.23 = (f32[192,256]{1,0:T(8,128)S(1)}, f32[192,256]{1,0:T(8,128)S(1)}, u32[]{:S(2)}, u32[]{:S(2)}) collective-permute-start(f32[192,256]{1,0:T(8,128)S(1)} %slice.29), channel_id=1, source_target_pairs={{0,48},{48,0},{96,144},{144,96},{192,240},{240,192},{288,336},{336... | collective-permute-start | bytes 589832 | tf_op jit(solution)/shard_map/ppermute | solution.py:18
  178.9 3.1 %collective-permute-done.23 = f32[192,256]{1,0:T(8,128)S(1)} collective-permute-done((f32[192,256]{1,0:T(8,128)S(1)}, f32[192,256]{1,0:T(8,128)S(1)}, u32[]{:S(2)}, u32[]{:S(2)}) %collective-permute-start.23) | collective-permute-done | bytes 196640 | tf_op jit(solution)/shard_map/ppermute | solution.py:18
  (79 shorter events, 48.0 us)
Async XLA Ops:
  5.2 57.0 %copy-start.3 = (bf16[8,8192]{1,0:T(8,128)(2,1)S(1)}, bf16[8,8192]{1,0:T(8,128)(2,1)}, u32[]{:S(2)}) copy-start(bf16[8,8192]{1,0:T(8,128)(2,1)} %refs_0_.1) | copy-start | bytes 393220
  5.2 14.1 %collective-permute-start.4 = (bf16[24,8192]{1,0:T(8,128)(2,1)S(1)}, bf16[24,8192]{1,0:T(8,128)(2,1)S(1)}, u32[]{:S(2)}, u32[]{:S(2)}) collective-permute-start(bf16[24,8192]{1,0:T(8,128)(2,1)S(1)} %get-tuple-element.43), channel_id=1, source_target_pairs={{0,1},{1,2},{2,3},{3,0},{4,5},{5,6},{6,7},{7,4},{8,9},{9,10},{10,1... | collective-permute-start | bytes 1179656 | tf_op jit(solution)/shard_map/ppermute | solution.py:18
  8.8 13.9 %collective-permute-start = (bf16[24,8192]{1,0:T(8,128)(2,1)S(1)}, bf16[24,8192]{1,0:T(8,128)(2,1)S(1)}, u32[]{:S(2)}, u32[]{:S(2)}) collective-permute-start(bf16[24,8192]{1,0:T(8,128)(2,1)S(1)} %get-tuple-element.35), channel_id=1, source_target_pairs={{0,3},{1,0},{2,1},{3,2},{4,7},{5,4},{6,5},{7,6},{8,11},{9,8},{10,9... | collective-permute-start | bytes 1179656 | tf_op jit(solution)/shard_map/ppermute | solution.py:18
  12.4 18.7 %collective-permute-start.3 = (bf16[24,8192]{1,0:T(8,128)(2,1)S(1)}, bf16[24,8192]{1,0:T(8,128)(2,1)S(1)}, u32[]{:S(2)}, u32[]{:S(2)}) collective-permute-start(bf16[24,8192]{1,0:T(8,128)(2,1)S(1)} %get-tuple-element.41), channel_id=1, source_target_pairs={{0,3},{1,0},{2,1},{3,2},{4,7},{5,4},{6,5},{7,6},{8,11},{9,8},{10,9... | collective-permute-start | bytes 1179656 | tf_op jit(solution)/shard_map/ppermute | solution.py:18
  19.4 14.6 %collective-permute-start.5 = (bf16[24,8192]{1,0:T(8,128)(2,1)S(1)}, bf16[24,8192]{1,0:T(8,128)(2,1)S(1)}, u32[]{:S(2)}, u32[]{:S(2)}) collective-permute-start(bf16[24,8192]{1,0:T(8,128)(2,1)S(1)} %add_convert_fusion.1), channel_id=1, source_target_pairs={{0,1},{1,2},{2,3},{3,0},{4,5},{5,6},{6,7},{7,4},{8,9},{9,10},{10,1... | collective-permute-start | bytes 1179656 | tf_op jit(solution)/shard_map/ppermute | solution.py:18
  23.0 22.8 %collective-permute-start.1 = (bf16[24,8192]{1,0:T(8,128)(2,1)S(1)}, bf16[24,8192]{1,0:T(8,128)(2,1)S(1)}, u32[]{:S(2)}, u32[]{:S(2)}) collective-permute-start(bf16[24,8192]{1,0:T(8,128)(2,1)S(1)} %get-tuple-element.38), channel_id=1, source_target_pairs={{0,3},{1,0},{2,1},{3,2},{4,7},{5,4},{6,5},{7,6},{8,11},{9,8},{10,9... | collective-permute-start | bytes 1179656 | tf_op jit(solution)/shard_map/ppermute | solution.py:18
  27.9 18.0 %collective-permute-start.2 = (bf16[24,8192]{1,0:T(8,128)(2,1)S(1)}, bf16[24,8192]{1,0:T(8,128)(2,1)S(1)}, u32[]{:S(2)}, u32[]{:S(2)}) collective-permute-start(bf16[24,8192]{1,0:T(8,128)(2,1)S(1)} %get-tuple-element.39), channel_id=1, source_target_pairs={{0,1},{1,2},{2,3},{3,0},{4,5},{5,6},{6,7},{7,4},{8,9},{9,10},{10,1... | collective-permute-start | bytes 1179656 | tf_op jit(solution)/shard_map/ppermute | solution.py:18
  34.9 11.0 %collective-permute-start.6 = (bf16[24,8192]{1,0:T(8,128)(2,1)}, bf16[24,8192]{1,0:T(8,128)(2,1)S(1)}, u32[]{:S(2)}, u32[]{:S(2)}) collective-permute-start(bf16[24,8192]{1,0:T(8,128)(2,1)} %add_convert_fusion), channel_id=1, source_target_pairs={{0,4},{4,0},{8,12},{12,8},{16,20},{20,16},{1,5},{5,1},{9,13},{13,9... | collective-permute-start | bytes 1179656 | tf_op jit(solution)/shard_map/ppermute | solution.py:18
  39.1 3.2 %collective-permute-start.9 = (bf16[192,256]{1,0:T(8,128)(2,1)S(1)}, bf16[192,256]{1,0:T(8,128)(2,1)S(1)}, u32[]{:S(2)}, u32[]{:S(2)}) collective-permute-start(bf16[192,256]{1,0:T(8,128)(2,1)S(1)} %get-tuple-element.47), channel_id=1, source_target_pairs={{0,24},{24,0},{1,25},{25,1},{2,26},{26,2},{3,27},{27,3},{4,28},{28... | collective-permute-start | bytes 294920 | tf_op jit(solution)/shard_map/ppermute | solution.py:18
  42.3 13.3 %collective-permute-start.10 = (bf16[24,16,256]{2,1,0:T(8,128)(2,1)S(1)}, bf16[24,16,256]{2,1,0:T(8,128)(2,1)}, u32[]{:S(2)}, u32[]{:S(2)}) collective-permute-start(bf16[24,16,256]{2,1,0:T(8,128)(2,1)S(1)} %pad_maximum_fusion.2), channel_id=1, source_target_pairs={{0,48},{48,0},{96,144},{144,96},{192,240},{240,192},{288,336},{336... | collective-permute-start | bytes 589832 | tf_op jit(solution)/shard_map/ppermute | solution.py:18
  46.3 13.1 %collective-permute-start.7 = (bf16[8,8192]{1,0:T(8,128)(2,1)S(1)}, bf16[8,8192]{1,0:T(8,128)(2,1)S(1)}, u32[]{:S(2)}, u32[]{:S(2)}) collective-permute-start(bf16[8,8192]{1,0:T(8,128)(2,1)S(1)} %get-tuple-element.45), channel_id=1, source_target_pairs={{0,16},{4,20},{8,0},{12,4},{16,8},{20,12},{1,17},{5,21},{9,1},{13,... | collective-permute-start | bytes 393224 | tf_op jit(solution)/shard_map/ppermute | solution.py:18
  48.3 13.9 %collective-permute-start.8 = (bf16[8,8192]{1,0:T(8,128)(2,1)S(1)}, bf16[8,8192]{1,0:T(8,128)(2,1)S(1)}, u32[]{:S(2)}, u32[]{:S(2)}) collective-permute-start(bf16[8,8192]{1,0:T(8,128)(2,1)S(1)} %get-tuple-element.46), channel_id=1, source_target_pairs={{0,8},{4,12},{8,16},{12,20},{16,0},{20,4},{1,9},{5,13},{9,17},{13,... | collective-permute-start | bytes 393224 | tf_op jit(solution)/shard_map/ppermute | solution.py:18
  63.8 3.1 %collective-permute-start.11 = (bf16[8,4096]{1,0:T(8,128)(2,1)S(1)}, bf16[8,4096]{1,0:T(8,128)(2,1)S(1)}, u32[]{:S(2)}, u32[]{:S(2)}) collective-permute-start(bf16[8,4096]{1,0:T(8,128)(2,1)S(1)} %get-tuple-element.51), channel_id=1, source_target_pairs={{0,24},{24,0},{1,25},{25,1},{2,26},{26,2},{3,27},{27,3},{4,28},{28... | collective-permute-start | bytes 196616 | tf_op jit(solution)/shard_map/ppermute | solution.py:18
  67.0 6.2 %collective-permute-start.12 = (bf16[16,2048]{1,0:T(8,128)(2,1)S(1)}, bf16[16,2048]{1,0:T(8,128)(2,1)S(1)}, u32[]{:S(2)}, u32[]{:S(2)}) collective-permute-start(bf16[16,2048]{1,0:T(8,128)(2,1)S(1)} %get-tuple-element.63), channel_id=1, source_target_pairs={{0,48},{48,0},{96,144},{144,96},{192,240},{240,192},{288,336},{336... | collective-permute-start | bytes 196616 | tf_op jit(solution)/shard_map/ppermute | solution.py:18
  73.2 13.2 %collective-permute-start.14 = (bf16[32,2048]{1,0:T(8,128)(2,1)S(1)}, bf16[32,2048]{1,0:T(8,128)(2,1)S(1)}, u32[]{:S(2)}, u32[]{:S(2)}) collective-permute-start(bf16[32,2048]{1,0:T(8,128)(2,1)S(1)} %pad_maximum_fusion.3), channel_id=1, source_target_pairs={{0,16},{4,20},{8,0},{12,4},{16,8},{20,12},{1,17},{5,21},{9,1},{13,... | collective-permute-start | bytes 393224 | tf_op jit(solution)/shard_map/ppermute | solution.py:18
  82.0 7.9 %collective-permute-start.13 = (bf16[32,2048]{1,0:T(8,128)(2,1)S(1)}, bf16[32,2048]{1,0:T(8,128)(2,1)S(1)}, u32[]{:S(2)}, u32[]{:S(2)}) collective-permute-start(bf16[32,2048]{1,0:T(8,128)(2,1)S(1)} %pad_maximum_fusion.3), channel_id=1, source_target_pairs={{0,8},{4,12},{8,16},{12,20},{16,0},{20,4},{1,9},{5,13},{9,17},{13,... | collective-permute-start | bytes 393224 | tf_op jit(solution)/shard_map/ppermute | solution.py:18
  89.8 15.0 %collective-permute-start.15 = (bf16[96,2048]{1,0:T(8,128)(2,1)S(1)}, bf16[96,2048]{1,0:T(8,128)(2,1)S(1)}, u32[]{:S(2)}, u32[]{:S(2)}) collective-permute-start(bf16[96,2048]{1,0:T(8,128)(2,1)S(1)} %pad_maximum_fusion.1.refs_0_), channel_id=1, source_target_pairs={{0,4},{4,0},{8,12},{12,8},{16,20},{20,16},{1,5},{5,1},{9,13},{13,9... | collective-permute-start | bytes 1179656 | tf_op jit(solution)/shard_map/ppermute | solution.py:18
  96.8 12.1 %collective-permute-start.17 = (bf16[96,2048]{1,0:T(8,128)(2,1)S(1)}, bf16[96,2048]{1,0:T(8,128)(2,1)S(1)}, u32[]{:S(2)}, u32[]{:S(2)}) collective-permute-start(bf16[96,2048]{1,0:T(8,128)(2,1)S(1)} %pad_maximum_fusion.1.refs_0_), channel_id=1, source_target_pairs={{0,3},{1,0},{2,1},{3,2},{4,7},{5,4},{6,5},{7,6},{8,11},{9,8},{10,9... | collective-permute-start | bytes 1179656 | tf_op jit(solution)/shard_map/ppermute | solution.py:18
  99.6 12.4 %collective-permute-start.16 = (bf16[96,2048]{1,0:T(8,128)(2,1)S(1)}, bf16[96,2048]{1,0:T(8,128)(2,1)S(1)}, u32[]{:S(2)}, u32[]{:S(2)}) collective-permute-start(bf16[96,2048]{1,0:T(8,128)(2,1)S(1)} %pad_maximum_fusion.1.refs_0_), channel_id=1, source_target_pairs={{0,1},{1,2},{2,3},{3,0},{4,5},{5,6},{6,7},{7,4},{8,9},{9,10},{10,1... | collective-permute-start | bytes 1179656 | tf_op jit(solution)/shard_map/ppermute | solution.py:18
  104.8 11.8 %collective-permute-start.18 = (bf16[96,2048]{1,0:T(8,128)(2,1)S(1)}, bf16[96,2048]{1,0:T(8,128)(2,1)S(1)}, u32[]{:S(2)}, u32[]{:S(2)}) collective-permute-start(bf16[96,2048]{1,0:T(8,128)(2,1)S(1)} %collective-permute-done.15.refs_1_), channel_id=1, source_target_pairs={{0,3},{1,0},{2,1},{3,2},{4,7},{5,4},{6,5},{7,6},{8,11},{9,8},{10,9... | collective-permute-start | bytes 1179656 | tf_op jit(solution)/shard_map/ppermute | solution.py:18
  112.0 15.2 %collective-permute-start.20 = (bf16[96,2048]{1,0:T(8,128)(2,1)S(1)}, bf16[96,2048]{1,0:T(8,128)(2,1)S(1)}, u32[]{:S(2)}, u32[]{:S(2)}) collective-permute-start(bf16[96,2048]{1,0:T(8,128)(2,1)S(1)} %tie.1.refs_2_), channel_id=1, source_target_pairs={{0,1},{1,2},{2,3},{3,0},{4,5},{5,6},{6,7},{7,4},{8,9},{9,10},{10,1... | collective-permute-start | bytes 1179656 | tf_op jit(solution)/shard_map/ppermute | solution.py:18
  113.9 18.0 %collective-permute-start.19 = (bf16[96,2048]{1,0:T(8,128)(2,1)S(1)}, bf16[96,2048]{1,0:T(8,128)(2,1)S(1)}, u32[]{:S(2)}, u32[]{:S(2)}) collective-permute-start(bf16[96,2048]{1,0:T(8,128)(2,1)S(1)} %collective-permute-done.15.refs_1_), channel_id=1, source_target_pairs={{0,1},{1,2},{2,3},{3,0},{4,5},{5,6},{6,7},{7,4},{8,9},{9,10},{10,1... | collective-permute-start | bytes 1179656 | tf_op jit(solution)/shard_map/ppermute | solution.py:18
  116.6 15.2 %collective-permute-start.21 = (bf16[96,2048]{1,0:T(8,128)(2,1)S(1)}, bf16[96,2048]{1,0:T(8,128)(2,1)S(1)}, u32[]{:S(2)}, u32[]{:S(2)}) collective-permute-start(bf16[96,2048]{1,0:T(8,128)(2,1)S(1)} %collective-permute-done.18.refs_4_.refs_7_), channel_id=1, source_target_pairs={{0,3},{1,0},{2,1},{3,2},{4,7},{5,4},{6,5},{7,6},{8,11},{9,8},{10,9... | collective-permute-start | bytes 1179656 | tf_op jit(solution)/shard_map/ppermute | solution.py:18
  133.4 19.0 %collective-permute-start.27 = (bf16[256,256]{1,0:T(8,128)(2,1)S(1)}, bf16[256,256]{1,0:T(8,128)(2,1)S(1)}, u32[]{:S(2)}, u32[]{:S(2)}) collective-permute-start(bf16[256,256]{1,0:T(8,128)(2,1)S(1)} %get-tuple-element.59), channel_id=1, source_target_pairs={{0,288},{48,336},{96,0},{144,48},{192,96},{240,144},{288,192},{336... | collective-permute-start | bytes 393224 | tf_op jit(solution)/shard_map/ppermute | solution.py:18
  135.7 20.5 %collective-permute-start.28 = (bf16[256,256]{1,0:T(8,128)(2,1)S(1)}, bf16[256,256]{1,0:T(8,128)(2,1)S(1)}, u32[]{:S(2)}, u32[]{:S(2)}) collective-permute-start(bf16[256,256]{1,0:T(8,128)(2,1)S(1)} %get-tuple-element.60), channel_id=1, source_target_pairs={{0,192},{48,240},{96,288},{144,336},{192,0},{240,48},{288,96},{336... | collective-permute-start | bytes 393224 | tf_op jit(solution)/shard_map/ppermute | solution.py:18
  142.6 19.7 %collective-permute-start.29 = (bf16[256,256]{1,0:T(8,128)(2,1)S(1)}, bf16[256,256]{1,0:T(8,128)(2,1)S(1)}, u32[]{:S(2)}, u32[]{:S(2)}) collective-permute-start(bf16[256,256]{1,0:T(8,128)(2,1)S(1)} %get-tuple-element.61), channel_id=1, source_target_pairs={{0,96},{48,144},{96,192},{144,240},{192,288},{240,336},{288,0},{33... | collective-permute-start | bytes 393224 | tf_op jit(solution)/shard_map/ppermute | solution.py:18
  147.7 26.1 %collective-permute-start.22 = (f32[384,256]{1,0:T(8,128)S(1)}, f32[384,256]{1,0:T(8,128)S(1)}, u32[]{:S(2)}, u32[]{:S(2)}) collective-permute-start(f32[384,256]{1,0:T(8,128)S(1)} %get-tuple-element.54), channel_id=1, source_target_pairs={{0,24},{24,0},{1,25},{25,1},{2,26},{26,2},{3,27},{27,3},{4,28},{28... | collective-permute-start | bytes 1179656 | tf_op jit(solution)/shard_map/ppermute | solution.py:18
  149.6 26.6 %collective-permute-start.24 = (bf16[256,256]{1,0:T(8,128)(2,1)S(1)}, bf16[256,256]{1,0:T(8,128)(2,1)S(1)}, u32[]{:S(2)}, u32[]{:S(2)}) collective-permute-start(bf16[256,256]{1,0:T(8,128)(2,1)S(1)} %get-tuple-element.55), channel_id=1, source_target_pairs={{0,288},{48,336},{96,0},{144,48},{192,96},{240,144},{288,192},{336... | collective-permute-start | bytes 393224 | tf_op jit(solution)/shard_map/ppermute | solution.py:18
  152.4 23.8 %collective-permute-start.25 = (bf16[256,256]{1,0:T(8,128)(2,1)S(1)}, bf16[256,256]{1,0:T(8,128)(2,1)S(1)}, u32[]{:S(2)}, u32[]{:S(2)}) collective-permute-start(bf16[256,256]{1,0:T(8,128)(2,1)S(1)} %get-tuple-element.56), channel_id=1, source_target_pairs={{0,192},{48,240},{96,288},{144,336},{192,0},{240,48},{288,96},{336... | collective-permute-start | bytes 393224 | tf_op jit(solution)/shard_map/ppermute | solution.py:18
  156.2 20.0 %collective-permute-start.26 = (bf16[256,256]{1,0:T(8,128)(2,1)S(1)}, bf16[256,256]{1,0:T(8,128)(2,1)S(1)}, u32[]{:S(2)}, u32[]{:S(2)}) collective-permute-start(bf16[256,256]{1,0:T(8,128)(2,1)S(1)} %get-tuple-element.57), channel_id=1, source_target_pairs={{0,96},{48,144},{96,192},{144,240},{192,288},{240,336},{288,0},{33... | collective-permute-start | bytes 393224 | tf_op jit(solution)/shard_map/ppermute | solution.py:18
  162.4 15.7 %collective-permute-start.30 = (bf16[256,256]{1,0:T(8,128)(2,1)S(1)}, bf16[256,256]{1,0:T(8,128)(2,1)S(1)}, u32[]{:S(2)}, u32[]{:S(2)}) collective-permute-start(bf16[256,256]{1,0:T(8,128)(2,1)S(1)} %add_convert_fusion.2), channel_id=1, source_target_pairs={{0,384},{384,0},{1,385},{385,1},{2,386},{386,2},{3,387},{387,3},{4... | collective-permute-start | bytes 393224 | tf_op jit(solution)/shard_map/ppermute | solution.py:18
  173.9 8.1 %collective-permute-start.23 = (f32[192,256]{1,0:T(8,128)S(1)}, f32[192,256]{1,0:T(8,128)S(1)}, u32[]{:S(2)}, u32[]{:S(2)}) collective-permute-start(f32[192,256]{1,0:T(8,128)S(1)} %slice.29), channel_id=1, source_target_pairs={{0,48},{48,0},{96,144},{144,96},{192,240},{240,192},{288,336},{336... | collective-permute-start | bytes 589832 | tf_op jit(solution)/shard_map/ppermute | solution.py:18
  (7 other events, 199.5 us)
